TPU v7x, 256 devices: a whole 4x4x8 slice. The times are simulated.
256 devices in a mesh: mem: 32 (over z, x), fsdp: 8 (over y, core).
Axes of the slice: x: 4, y: 4, z: 8, core: 2. Of those that a mesh axis runs over, the one named last changes fastest.
Arguments:
- layer_input: bfloat16 [32768, 4096], P(('mem', 'fsdp')), may hold values from -6 to 6
- w_query: bfloat16 [4096, 2048], P('mem', 'fsdp'), may hold values from -0.09375 to 0.09375
- local_kv: bfloat16 [2, 32768, 2048], P(None, 'mem', 'fsdp'), may hold values from -200 to 200, as said below
- memory_kv: bfloat16 [512, 2, 128, 2048], P('mem', None, None, 'fsdp'), may hold values from -200 to 200
- memory_ids: int32 [256, 4], P('mem'), may hold values from 0 to 511, as said below
- grad_out: bfloat16 [32768, 2048], P('mem', 'fsdp'), may hold values from -6 to 6
Outputs:
- attended: bfloat16 [32768, 2048], P('mem', 'fsdp')
- grad_input: bfloat16 [32768, 4096], P(('mem', 'fsdp'))
Inputs may be any that keep to these rules, and one draw needn't show every extreme that they name: `memory_ids`: within the tiles of one local context (8 tiles), all named blocks of one owner (same id // 16) are one and the same block, and every owner is named by some tile of every local context; each tile names 4 blocks of different owners. `local_kv`: keys and values of the document's tokens.
All inputs are finite; a program needn't handle non-finite values.
Results may differ from a plain program's by a relative error of at most 0.025.
The roundings to bfloat16 on the way count: a program that leaves them out, or rounds other values in their place, can miss the bound.
Values may be sent and summed in bfloat16 or wider, within the bound.
No kernel may reach another device: no remote copies, remote signals or barrier semaphores. Data moves between devices by JAX's collectives and lax.ppermute only.
A program may use at most 128 MiB of HBM per device.

v0:
```python
import functools
import functools
import math

import jax
import jax.numpy as jnp
from jax import lax
from jax.experimental import pallas as pl
from jax.experimental.pallas import tpu as pltpu
from jax.sharding import Mesh
from jax.sharding import PartitionSpec as P

HD = 128
BLK = 128
TOPK = 4
MB_DEV = 16
CTX = 1024
TILES = CTX // BLK
ZN, XN, YN, CN = 8, 4, 4, 2
OWNERS = ZN * XN
HEADS = 2
WIDTH = HEADS * HD
DM = 4096
PAIR = 2 * BLK
MEM = ("z", "x")
MIB = 1024 * 1024
REST = (XN - 1) * ZN
NEG_FILL = -1e30
SCALE = 1.0 / math.sqrt(HD)
FAR = (2, 1, 3)


def dot(a, b, dims):
    return lax.dot_general(a, b, (dims, ((), ())), preferred_element_type=jnp.float32)


def pick_kernel(asked_ref, block_ref, out_ref):
    out_ref[...] = block_ref[...]


def pick_blocks(asked, memory_kv):
    block = (1, 2, BLK, WIDTH)
    return pl.pallas_call(
        pick_kernel,
        grid_spec=pltpu.PrefetchScalarGridSpec(
            num_scalar_prefetch=1,
            grid=(OWNERS,),
            in_specs=[pl.BlockSpec(block, lambda i, asked_ref: (asked_ref[i], 0, 0, 0))],
            out_specs=pl.BlockSpec(block, lambda i, asked_ref: (i, 0, 0, 0)),
        ),
        out_shape=jax.ShapeDtypeStruct((OWNERS, 2, BLK, WIDTH), jnp.bfloat16),
        compiler_params=pltpu.CompilerParams(vmem_limit_bytes=56 * MIB),
        cost_estimate=pl.CostEstimate(
            flops=0, bytes_accessed=2 * OWNERS * 2 * BLK * WIDTH * 2, transcendentals=0
        ),
        name="pick_blocks",
    )(asked, memory_kv)


def column_of(z_index, x_index, shift):
    return pl.multiple_of((lax.rem(z_index + ZN - shift, ZN) * XN + x_index) * BLK, BLK)


def project_kernel(pos_ref, x_ref, *refs):
    own_ref, rest_ref, out_ref = refs
    total = jnp.zeros((PAIR, WIDTH), jnp.float32)
    for x_shift in range(XN):
        x_index = lax.rem(pos_ref[1] + XN - x_shift, XN)
        rows = jnp.concatenate(
            [x_ref[:, pl.ds(column_of(pos_ref[0], x_index, shift), BLK)] for shift in range(ZN)],
            axis=1,
        )
        piece = rest_ref[(x_shift - 1) * ZN : x_shift * ZN] if x_shift else own_ref[...]
        total += dot(rows, piece.reshape(ZN * BLK, WIDTH), ((1,), (0,)))
    out_ref[...] = total.astype(jnp.bfloat16)


def project(position, rows, own, rest):
    pieces = [
        pl.BlockSpec((count, BLK, WIDTH), lambda i, pos_ref: (0, 0, 0)) for count in (ZN, REST)
    ]
    return pl.pallas_call(
        project_kernel,
        grid_spec=pltpu.PrefetchScalarGridSpec(
            num_scalar_prefetch=1,
            grid=(CTX // PAIR,),
            in_specs=[pl.BlockSpec((PAIR, DM), lambda i, pos_ref: (i, 0)), *pieces],
            out_specs=pl.BlockSpec((PAIR, WIDTH), lambda i, pos_ref: (i, 0)),
        ),
        out_shape=jax.ShapeDtypeStruct((CTX, WIDTH), jnp.bfloat16),
        compiler_params=pltpu.CompilerParams(vmem_limit_bytes=16 * MIB),
        cost_estimate=pl.CostEstimate(
            flops=2 * CTX * DM * WIDTH,
            bytes_accessed=2 * (CTX * DM + DM * WIDTH + CTX * WIDTH),
            transcendentals=0,
        ),
        name="project",
    )(position, rows, own, rest)


def attend_local_kernel(query_ref, local_ref, grad_ref, *out_refs):
    sum_ref, slope_ref, base_ref, stat_ref = out_refs
    row = lax.broadcasted_iota(jnp.int32, (BLK, BLK), 0)
    col = lax.broadcasted_iota(jnp.int32, (BLK, BLK), 1)
    causal = row >= col
    heads = range(HEADS)
    feats = [slice(head * HD, (head + 1) * HD) for head in heads]
    for tile in range(TILES):
        rows = slice(tile * BLK, (tile + 1) * BLK)
        seen = slice(0, (tile + 1) * BLK)
        scores = [dot(query_ref[rows, f], local_ref[0, seen, f], ((1,), (1,))) for f in feats]
        dprobs = [dot(grad_ref[rows, f], local_ref[1, seen, f], ((1,), (1,))) for f in feats]
        last = [jnp.where(causal, s[:, -BLK:] * SCALE, NEG_FILL) for s in scores]
        if tile:
            scores = [
                jnp.concatenate([scores[h][:, :-BLK] * SCALE, last[h]], axis=1) for h in heads
            ]
        else:
            scores = last
        row_max = [jnp.max(s, axis=1, keepdims=True) for s in scores]
        exps = [jnp.exp(scores[h] - row_max[h]) for h in heads]
        total = [jnp.sum(e, axis=1, keepdims=True) for e in exps]
        weights = [e.astype(jnp.bfloat16) for e in exps]
        for h in heads:
            part = dot(weights[h], local_ref[1, seen, feats[h]], ((1,), (0,)))
            sum_ref[rows, feats[h]] = part.astype(jnp.bfloat16)
            part = dot(weights[h], local_ref[0, seen, feats[h]], ((1,), (0,)))
            base_ref[rows, feats[h]] = part.astype(jnp.bfloat16)
        delta = [
            jnp.sum(exps[h] * dprobs[h], axis=1, keepdims=True) / total[h] for h in heads
        ]
        slopes = [(exps[h] * (dprobs[h] - delta[h])).astype(jnp.bfloat16) for h in heads]
        for h in heads:
            part = dot(slopes[h], local_ref[0, seen, feats[h]], ((1,), (0,)))
            slope_ref[rows, feats[h]] = part.astype(jnp.bfloat16)
            for i, stat in enumerate((row_max[h], total[h], delta[h])):
                stat_ref[rows, 3 * h + i : 3 * h + i + 1] = stat


def attend_local(queries, local_kv, grad_out):
    in_vmem = pl.BlockSpec(memory_space=pltpu.VMEM)
    keys_count = BLK * TILES * (TILES + 1) // 2
    return pl.pallas_call(
        attend_local_kernel,
        in_specs=[in_vmem] * 3,
        out_specs=[in_vmem] * 4,
        out_shape=[jax.ShapeDtypeStruct((CTX, WIDTH), jnp.bfloat16)] * 3
        + [jax.ShapeDtypeStruct((CTX, BLK), jnp.float32)],
        compiler_params=pltpu.CompilerParams(vmem_limit_bytes=10 * MIB),
        cost_estimate=pl.CostEstimate(
            flops=10 * BLK * keys_count * WIDTH,
            bytes_accessed=2 * 12 * CTX * WIDTH,
            transcendentals=BLK * keys_count * HEADS,
        ),
        name="attend_local",
    )(queries, local_kv, grad_out)


def attend_memory_kernel(shifts, owner_ref, pos_ref, *refs):
    count, parts = len(shifts), PAIR // BLK
    row_refs, memory_ref, refs = refs[:6], refs[6], refs[7:]
    row_scrs, (held, sems, row_sems), refs = refs[-9:-3], refs[-3:], refs[:-9]
    other_refs, back_refs = refs[:-count], refs[-count:]
    query_scr, grad_scr, sum_scr, slope_scr, base_scr, stat_scr = row_scrs
    groups = [lax.rem(pos_ref[2] + shift, YN) for shift in shifts]
    row_copies = [
        pltpu.make_async_copy(
            ref.at[pl.ds(pl.multiple_of(group * PAIR, PAIR), PAIR)], scr.at[i], row_sems.at[i, j]
        )
        for i, group in enumerate(groups)
        for j, (ref, scr) in enumerate(zip(row_refs, row_scrs))
    ]
    copies = [
        pltpu.make_async_copy(
            memory_ref.at[owner_ref[group * parts + part, slot]],
            held.at[i * parts + part, slot],
            sems.at[i * parts + part, slot],
        )
        for i, group in enumerate(groups)
        for part in range(parts)
        for slot in range(TOPK)
    ]
    for i in range(count):
        for copy in copies[i * parts * TOPK : (i + 1) * parts * TOPK]:
            copy.start()
        for copy in row_copies[i * 6 : i * 6 + 6]:
            copy.start()
    if shifts == (0,):
        *done_refs, whole_ref = other_refs
        for shift, done_ref in zip(FAR, done_refs):
            group = lax.rem(pos_ref[2] + shift, YN)
            whole_ref[pl.ds(pl.multiple_of(group * PAIR, PAIR), PAIR), :] = done_ref[...]
    for i, group in enumerate(groups):
        for copy in copies[i * parts * TOPK : (i + 1) * parts * TOPK]:
            copy.wait()
        for copy in row_copies[i * 6 : i * 6 + 6]:
            copy.wait()
        units = [(part, head) for part in range(parts) for head in range(HEADS)]
        every = range(len(units))
        rows = [slice(part * BLK, (part + 1) * BLK) for part, head in units]
        feats = [slice(head * HD, (head + 1) * HD) for part, head in units]
        keys, values = [
            [
                held[i * parts + part, :, kind, :, feats[u]].reshape(TOPK * BLK, HD)
                for u, (part, head) in enumerate(units)
            ]
            for kind in range(2)
        ]
        scores = [dot(query_scr[i, rows[u], feats[u]], keys[u], ((1,), (1,))) * SCALE for u in every]
        dprobs = [dot(grad_scr[i, rows[u], feats[u]], values[u], ((1,), (1,))) for u in every]
        stats = [
            [stat_scr[i, rows[u], 3 * head + j : 3 * head + j + 1] for j in range(3)]
            for u, (part, head) in enumerate(units)
        ]
        row_max = [
            jnp.maximum(jnp.max(scores[u], axis=1, keepdims=True), stats[u][0]) for u in every
        ]
        exps = [jnp.exp(scores[u] - row_max[u]) for u in every]
        factor = [jnp.exp(stats[u][0] - row_max[u]) for u in every]
        inverse = [
            1.0 / (jnp.sum(exps[u], axis=1, keepdims=True) + factor[u] * stats[u][1])
            for u in every
        ]
        delta = [
            inverse[u]
            * (
                jnp.sum(exps[u] * dprobs[u], axis=1, keepdims=True)
                + factor[u] * stats[u][1] * stats[u][2]
            )
            for u in every
        ]
        dscores = [(exps[u] * (dprobs[u] - delta[u])).astype(jnp.bfloat16) for u in every]
        for u, (part, head) in enumerate(units):
            back = dot(dscores[u], keys[u], ((1,), (0,))) + factor[u] * (
                slope_scr[i, rows[u], feats[u]].astype(jnp.float32)
                + (stats[u][2] - delta[u]) * base_scr[i, rows[u], feats[u]].astype(jnp.float32)
            )
            back_refs[i][rows[u], feats[u]] = (back * (inverse[u] * SCALE)).astype(jnp.bfloat16)
        for u, (part, head) in enumerate(units):
            attended = factor[u] * sum_scr[i, rows[u], feats[u]].astype(jnp.float32) + dot(
                exps[u].astype(jnp.bfloat16), values[u], ((1,), (0,))
            )
            attended = (attended * inverse[u]).astype(jnp.bfloat16)
            if shifts == (0,):
                whole_ref[pl.ds(pl.multiple_of(group * PAIR + part * BLK, BLK), BLK), feats[u]] = (
                    attended
                )
            else:
                other_refs[i][rows[u], feats[u]] = attended


def attend_memory(shifts, owner_of, position, queries, received, grad_out, prepared, done):
    in_smem, in_vmem = (pl.BlockSpec(memory_space=space) for space in (pltpu.SMEM, pltpu.VMEM))
    count, tiles = len(shifts), len(shifts) * (PAIR // BLK)
    part = jax.ShapeDtypeStruct((PAIR, WIDTH), jnp.bfloat16)
    whole = [jax.ShapeDtypeStruct((CTX, WIDTH), jnp.bfloat16)]
    operands = [queries, grad_out, *prepared, received, *done]
    out_shape = (whole if done else [part] * count) + [part] * count
    keys_count = tiles * TOPK * BLK
    outs = pl.pallas_call(
        functools.partial(attend_memory_kernel, shifts),
        in_specs=[in_smem] * 2
        + [pl.BlockSpec(memory_space=pl.ANY)] * 7
        + [in_vmem] * len(done),
        out_specs=[in_vmem] * len(out_shape),
        out_shape=out_shape,
        scratch_shapes=[pltpu.VMEM((count, PAIR, WIDTH), jnp.bfloat16)] * 5
        + [
            pltpu.VMEM((count, PAIR, BLK), jnp.float32),
            pltpu.VMEM((tiles, TOPK, 2, BLK, WIDTH), jnp.bfloat16),
            pltpu.SemaphoreType.DMA((tiles, TOPK)),
            pltpu.SemaphoreType.DMA((count, 6)),
        ],
        compiler_params=pltpu.CompilerParams(vmem_limit_bytes=58 * MIB),
        cost_estimate=pl.CostEstimate(
            flops=8 * BLK * keys_count * WIDTH,
            bytes_accessed=2 * 12 * CTX * WIDTH,
            transcendentals=BLK * keys_count * HEADS,
        ),
        name="attend_memory",
    )(owner_of, position, *operands)
    return outs[:-count], outs[-count:]


PLACES = (
    (0, 0, ZN),
    (1, 0, ZN),
    (2, 0, ZN),
    (3, 0, ZN),
    (0, ZN, REST),
    (1, ZN, REST),
    (2, ZN, REST // 2),
    (2, ZN + REST // 2, REST // 2),
    (3, ZN, REST),
)


def back_kernel(pos_ref, *refs):
    grad_refs, piece_refs = refs[:YN], refs[YN : YN + len(PLACES)]
    own_ref, send_ref, held, total_scr, sems = refs[YN + len(PLACES) :]
    copies = [
        pltpu.make_async_copy(piece, held.at[shift, pl.ds(first, count)], sems.at[i])
        for i, (piece, (shift, first, count)) in enumerate(zip(piece_refs, PLACES))
    ]
    for copy in copies:
        copy.start()
    core = pos_ref[3]
    own_rows = pl.ds(pl.multiple_of(core * BLK, BLK), BLK)
    send_rows = pl.ds(pl.multiple_of((1 - core) * BLK, BLK), BLK)
    for x_shift in range(XN):
        x_index = lax.rem(pos_ref[1] + XN - x_shift, XN)
        if x_shift < 2:
            for copy in copies[YN:] if x_shift else copies[:YN]:
                copy.wait()
        blocks = slice(x_shift * ZN, (x_shift + 1) * ZN)
        total = jnp.zeros((PAIR, ZN * BLK), jnp.float32)
        for shift in range(YN):
            weight = held[shift, blocks].reshape(ZN * BLK, WIDTH)
            total += dot(grad_refs[shift][...], weight, ((1,), (1,)))
        total_scr[...] = total
        for out_ref, rows in ((send_ref, send_rows), (own_ref, own_rows)):
            for shift in range(ZN):
                columns = pl.ds(column_of(pos_ref[0], x_index, shift), BLK)
                part = total_scr[rows, shift * BLK : (shift + 1) * BLK]
                out_ref[:, columns] = part.astype(out_ref.dtype)


def back_project(position, grads, pieces):
    in_vmem = pl.BlockSpec(memory_space=pltpu.VMEM)
    return pl.pallas_call(
        back_kernel,
        in_specs=[pl.BlockSpec(memory_space=pltpu.SMEM)]
        + [in_vmem] * YN
        + [pl.BlockSpec(memory_space=pl.ANY)] * len(pieces),
        out_specs=[in_vmem] * 2,
        out_shape=[
            jax.ShapeDtypeStruct((BLK, DM), jnp.float32),
            jax.ShapeDtypeStruct((BLK, DM), jnp.bfloat16),
        ],
        scratch_shapes=[
            pltpu.VMEM((YN, XN * ZN, BLK, WIDTH), jnp.bfloat16),
            pltpu.VMEM((PAIR, ZN * BLK), jnp.float32),
            pltpu.SemaphoreType.DMA((len(pieces),)),
        ],
        compiler_params=pltpu.CompilerParams(vmem_limit_bytes=20 * MIB),
        cost_estimate=pl.CostEstimate(
            flops=2 * PAIR * DM * YN * WIDTH,
            bytes_accessed=2 * (2 * PAIR * DM + DM * YN * WIDTH),
            transcendentals=0,
        ),
        name="back_project",
    )(position, *grads, *pieces)


def move(array, axis, count, shift):
    if shift % count == 0:
        return array
    return lax.ppermute(array, axis, [(i, (i + shift) % count) for i in range(count)])


def local(layer_input, w_query, local_kv, memory_kv, memory_ids, grad_out):
    position = jnp.stack([lax.axis_index(axis) for axis in ("z", "x", "y", "c")]).astype(jnp.int32)
    owner_of = memory_ids // MB_DEV
    owners = jnp.arange(OWNERS, dtype=jnp.int32)
    wanted = jnp.max(
        jnp.where(owner_of[:, :, None] == owners, (memory_ids % MB_DEV)[:, :, None], 0),
        axis=(0, 1),
    )
    weights = [move(w_query, "z", ZN, shift) for shift in range(ZN)]
    asked = lax.all_to_all(wanted.reshape(OWNERS, 1), MEM, 0, 0, tiled=True)
    asked, weights = lax.optimization_barrier((asked, weights))
    received = lax.all_to_all(pick_blocks(asked[:, 0], memory_kv), MEM, 0, 0, tiled=True)
    own = jnp.stack(weights)
    rows = lax.all_gather(layer_input, ("y", "c"), axis=0, tiled=True)
    rest = jnp.concatenate([move(own, "x", XN, shift) for shift in range(1, XN)])
    near_parts = [own, *[move(own, "y", YN, shift) for shift in range(1, YN)]]
    rest, near_parts = lax.optimization_barrier((rest, near_parts))
    below, above = move(rest, "y", YN, 1), move(rest, "y", YN, -1)
    queries = project(position, rows, own, rest)
    *sums, stats = attend_local(queries, local_kv, grad_out)
    below, above, stats = lax.optimization_barrier((below, above, stats))
    prepared = [*sums, stats]
    far_first = move(below[: REST // 2], "y", YN, 1)
    far_last = move(above[REST // 2 :], "y", YN, -1)
    pieces = [*near_parts, rest, below, far_first, far_last, above]
    done, far = attend_memory(FAR, owner_of, position, queries, received, grad_out, prepared, [])
    far = {shift: move(part, "y", YN, shift) for shift, part in zip(FAR, far)}
    (attended,), (near,) = attend_memory(
        (0,), owner_of, position, queries, received, grad_out, prepared, done
    )
    grads = [near, far[1], far[2], far[3]]
    own_part, send = back_project(position, grads, pieces)
    other = move(send, "c", CN, 1)
    return (attended, (own_part + other.astype(jnp.float32)).astype(jnp.bfloat16))


def solution(mesh):
    torus = Mesh(mesh.devices.reshape(ZN, XN, YN, CN), ("z", "x", "y", "c"))
    in_specs = (
        P(("z", "x", "y", "c"), None),
        P(MEM, ("y", "c")),
        P(None, MEM, ("y", "c")),
        P(MEM, None, None, ("y", "c")),
        P(MEM, None),
        P(MEM, ("y", "c")),
    )
    out_specs = (P(MEM, ("y", "c")), P(("z", "x", "y", "c"), None))
    return jax.shard_map(local, mesh=torus, in_specs=in_specs, out_specs=out_specs, check_vma=False)
```

profile of v0, /device:TPU:129, one launch (start us, length us, event | category | flops | bytes accessed | tf_op | source)
XLA Modules:
  0.0 204.5 jit_solution(15755204086411395786)
XLA Ops:
  7.2 0.0 all-gather.2.cloned.1.call-start
  7.2 0.7 all-gather.2.cloned.1.call-update
  7.9 0.8 collective-permute-start
  8.7 1.2 collective-permute-start.1
  9.9 4.9 %collective-permute-start.3 = (bf16[128,256]{1,0:T(8,128)(2,1)}, bf16[128,256]{1,0:T(8,128)(2,1)S(1)}, u32[]{:S(2)}, u32[]{:S(2)}) collective-permute-start(bf16[128,256]{1,0:T(8,128)(2,1)} %param.7), channel_id=1, source_target_pairs={{0,128},{32,160},{64,192},{96,224},{128,0},{160,32},{192,64},{224,... | collective-permute-start | bytes 196616 | tf_op jit(solution)/shard_map/ppermute | solution.py:358
  14.8 0.7 collective-permute-start.4
  15.5 0.8 copy.22
  16.3 0.1 copy.26
  16.4 0.1 copy.27
  16.5 0.0 collective-permute-done
  16.5 2.1 %collective-permute-start.5 = (bf16[128,256]{1,0:T(8,128)(2,1)}, bf16[128,256]{1,0:T(8,128)(2,1)S(1)}, u32[]{:S(2)}, u32[]{:S(2)}) collective-permute-start(bf16[128,256]{1,0:T(8,128)(2,1)} %param.7), channel_id=1, source_target_pairs={{0,192},{32,224},{64,0},{96,32},{128,64},{160,96},{192,128},{224,1... | collective-permute-start | bytes 196616 | tf_op jit(solution)/shard_map/ppermute | solution.py:358
  18.6 1.3 collective-permute-start.6
  19.9 0.1 select_reduce_fusion
  20.0 0.1 copy.28
  20.1 12.9 %all_to_all.17 = s32[32,1,1]{2,1,0:T(1,128)S(1)} all-to-all(s32[32,1,1]{2,1,0:T(1,128)S(1)} %copy.28), channel_id=1, replica_groups=mesh['z'=8,'x'=4,'y'=4,'c'=2] {'z','x'}, dimensions={0} | all-to-all | bytes 256 | tf_op jit(solution)/shard_map/all_to_all | solution.py:370
  33.0 1.2 reduce
  34.2 0.0 collective-permute-done.2
  34.2 0.0 collective-permute-done.3
  34.2 0.0 collective-permute-done.5
  34.2 18.6 %pick_blocks.1 = bf16[32,2,128,256]{3,2,1,0:T(8,128)(2,1)} custom-call(s32[32]{0:T(128)} %reduce, bf16[16,2,128,256]{3,2,1,0:T(8,128)(2,1)} %block_ref.1), custom_call_target="tpu_custom_call" | custom-call | bytes 8388608 | tf_op jit(solution)/shard_map/pick_blocks/pallas_call | solution.py:43
  52.9 9.6 %all-to-all-start.1 = ((bf16[32,2,128,256]{3,2,1,0:T(8,128)(2,1)}), bf16[32,2,128,256]{3,2,1,0:T(8,128)(2,1)}, u32[]{:S(2)}, u32[]{:S(2)}) async-start(bf16[32,2,128,256]{3,2,1,0:T(8,128)(2,1)} %pick_blocks.1), calls=%async_computation.1 | async-start | bytes 8388608 | tf_op jit(solution)/shard_map/all_to_all | solution.py:372
  62.6 1.3 collective-permute-start.7
  63.9 2.4 %collective-permute-start.8 = (bf16[8,128,256]{2,1,0:T(8,128)(2,1)S(1)}, bf16[8,128,256]{2,1,0:T(8,128)(2,1)S(1)}, u32[]{:S(2)}, u32[]{:S(2)}) collective-permute-start(bf16[8,128,256]{2,1,0:T(8,128)(2,1)S(1)} %bitcast_dynamic-update-slice_fusion.refs_0_.refs_4_), channel_id=1, source_target_pairs={{0,16},{8,24},{16,0},{24,8},{1,17},{9,25},{17,1},{25,9},{2,18},{10... | collective-permute-start | bytes 1572872 | tf_op jit(solution)/shard_map/ppermute | solution.py:358
  66.3 1.2 collective-permute-start.9
  67.5 1.2 collective-permute-start.10
  68.7 2.6 %collective-permute-start.11 = (bf16[8,128,256]{2,1,0:T(8,128)(2,1)S(1)}, bf16[8,128,256]{2,1,0:T(8,128)(2,1)S(1)}, u32[]{:S(2)}, u32[]{:S(2)}) collective-permute-start(bf16[8,128,256]{2,1,0:T(8,128)(2,1)S(1)} %bitcast_dynamic-update-slice_fusion.refs_0_.refs_4_), channel_id=1, source_target_pairs={{0,4},{2,6},{4,0},{6,2},{1,5},{3,7},{5,1},{7,3},{8,12},{10,14},{12... | collective-permute-start | bytes 1572872 | tf_op jit(solution)/shard_map/ppermute | solution.py:358
  71.3 23.9 %collective-permute-done.7 = bf16[8,128,256]{2,1,0:T(8,128)(2,1)S(1)} collective-permute-done((bf16[8,128,256]{2,1,0:T(8,128)(2,1)S(1)}, bf16[8,128,256]{2,1,0:T(8,128)(2,1)S(1)}, u32[]{:S(2)}, u32[]{:S(2)}) %collective-permute-start.7) | collective-permute-done | bytes 524320 | tf_op jit(solution)/shard_map/ppermute | solution.py:358
  95.2 2.7 %collective-permute-start.12 = (bf16[8,128,256]{2,1,0:T(8,128)(2,1)S(1)}, bf16[8,128,256]{2,1,0:T(8,128)(2,1)S(1)}, u32[]{:S(2)}, u32[]{:S(2)}) collective-permute-start(bf16[8,128,256]{2,1,0:T(8,128)(2,1)S(1)} %bitcast_dynamic-update-slice_fusion.refs_0_.refs_4_), channel_id=1, source_target_pairs={{0,6},{2,0},{4,2},{6,4},{1,7},{3,1},{5,3},{7,5},{8,14},{10,8},{12,... | collective-permute-start | bytes 1572872 | tf_op jit(solution)/shard_map/ppermute | solution.py:358
  97.9 15.0 %collective-permute-done.8 = bf16[8,128,256]{2,1,0:T(8,128)(2,1)S(1)} collective-permute-done((bf16[8,128,256]{2,1,0:T(8,128)(2,1)S(1)}, bf16[8,128,256]{2,1,0:T(8,128)(2,1)S(1)}, u32[]{:S(2)}, u32[]{:S(2)}) %collective-permute-start.8) | collective-permute-done | bytes 524320 | tf_op jit(solution)/shard_map/ppermute | solution.py:358
  112.9 3.9 %collective-permute-done.9 = bf16[8,128,256]{2,1,0:T(8,128)(2,1)S(1)} collective-permute-done((bf16[8,128,256]{2,1,0:T(8,128)(2,1)S(1)}, bf16[8,128,256]{2,1,0:T(8,128)(2,1)S(1)}, u32[]{:S(2)}, u32[]{:S(2)}) %collective-permute-start.9) | collective-permute-done | bytes 524320 | tf_op jit(solution)/shard_map/ppermute | solution.py:358
  116.8 0.2 pad_maximum_fusion.refs_1_.refs_8_
  117.0 0.0 collective-permute-done.10.refs_5_
  117.0 0.8 copy-done.7
  117.8 0.8 copy-done.9
  118.6 0.0 collective-permute-done.12.refs_7_
  118.6 0.8 copy-done.11
  119.4 1.3 collective-permute-start.13
  120.7 1.4 collective-permute-start.14
  122.1 0.1 pad_add_fusion.pos_ref
  122.2 3.4 %copy-done = bf16[1024,4096]{1,0:T(8,128)(2,1)S(1)} copy-done((bf16[1024,4096]{1,0:T(8,128)(2,1)S(1)}, bf16[1024,4096]{1,0:T(8,128)(2,1)}, u32[]{:S(2)}) %copy-start) | copy-done | bytes 8388632
  125.6 3.8 %project.1.query_ref.refs_0_ = bf16[1024,256]{1,0:T(8,128)(2,1)S(1)} custom-call(s32[4]{0:T(128)S(1)} %pad_add_fusion.pos_ref, bf16[1024,4096]{1,0:T(8,128)(2,1)S(1)} %copy-done, bf16[8,128,256]{2,1,0:T(8,128)(2,1)S(1)} %bitcast_dynamic-update-slice_fusion.refs_0_.refs_4_, bf16[24,128,256]{2,1,0:T(8,128)(2,1)S(1)} %pad_maximum_fusion.refs_1_.refs_8_), custom_call_target="tpu_custom_call" | custom-call | flops 2147483648 | bytes 11010048 | tf_op jit(solution)/shard_map/project/pallas_call | solution.py:82
  129.4 5.0 %attend_local.1 = (bf16[1024,256]{1,0:T(8,128)(2,1)S(1)}, bf16[1024,256]{1,0:T(8,128)(2,1)S(1)}, bf16[1024,256]{1,0:T(8,128)(2,1)S(1)}, f32[1024,128]{1,0:T(8,128)S(1)}) custom-call(bf16[1024,256]{1,0:T(8,128)(2,1)S(1)} %project.1.query_ref.refs_0_, bf16[2,1024,256]{2,1,0:T(8,128)(2,1)S(1)} %copy-done.16, bf16[1024,256]{1,0:T(8,128)(2,1)S(1)} %copy-done.2), custom_call_target="tpu_custom_call" | custom-call | flops 1509949440 | bytes 6291456 | tf_op jit(solution)/shard_map/attend_local/pallas_call | solution.py:143
  134.4 0.8 copy-done.3
  135.2 0.8 copy-done.4
  136.1 0.8 copy-done.5
  136.8 0.8 copy-done.6
  137.6 9.6 %collective-permute-done.13.refs_9_ = bf16[24,128,256]{2,1,0:T(8,128)(2,1)} collective-permute-done((bf16[24,128,256]{2,1,0:T(8,128)(2,1)S(1)}, bf16[24,128,256]{2,1,0:T(8,128)(2,1)}, u32[]{:S(2)}, u32[]{:S(2)}) %collective-permute-start.13) | collective-permute-done | bytes 1572896 | tf_op jit(solution)/shard_map/ppermute | solution.py:358
  147.2 0.0 collective-permute-done.14.refs_12_
  147.2 2.1 %slice.6 = bf16[12,128,256]{2,1,0:T(8,128)(2,1)} slice(bf16[24,128,256]{2,1,0:T(8,128)(2,1)} %collective-permute-done.13.refs_9_), slice={[0:12], [0:128], [0:256]} | slice | bytes 1572864 | tf_op jit(solution)/shard_map/slice | solution.py:383
  149.3 1.1 collective-permute-start.18
  150.4 2.1 %slice.7 = bf16[12,128,256]{2,1,0:T(8,128)(2,1)} slice(bf16[24,128,256]{2,1,0:T(8,128)(2,1)} %collective-permute-done.14.refs_12_), slice={[12:24], [0:128], [0:256]} | slice | bytes 1572864 | tf_op jit(solution)/shard_map/slice | solution.py:384
  152.5 1.6 collective-permute-start.19
  154.1 9.7 %attend_memory.2 = (bf16[256,256]{1,0:T(8,128)(2,1)}, bf16[256,256]{1,0:T(8,128)(2,1)}, bf16[256,256]{1,0:T(8,128)(2,1)}, bf16[256,256]{1,0:T(8,128)(2,1)}, bf16...) custom-call(s32[8,4]{1,0:T(8,128)} %copy-done.17, s32[4]{0:T(128)} %copy-done.14, bf16[1024,256]{1,0:T(8,128)(2,1)} %copy-done.1, ...), custom_call_target="tpu_custom_call" | custom-call | flops 805306368 | bytes 6291456 | tf_op jit(solution)/shard_map/attend_memory/pallas_call | solution.py:260
  163.8 0.1 collective-permute-start.15
  163.9 2.3 %collective-permute-start.16 = (bf16[256,256]{1,0:T(8,128)(2,1)}, bf16[256,256]{1,0:T(8,128)(2,1)S(1)}, u32[]{:S(2)}, u32[]{:S(2)}) collective-permute-start(bf16[256,256]{1,0:T(8,128)(2,1)} %get-tuple-element.54), channel_id=1, source_target_pairs={{0,4},{2,6},{4,0},{6,2},{1,5},{3,7},{5,1},{7,3},{8,12},{10,14},{12... | collective-permute-start | bytes 393224 | tf_op jit(solution)/shard_map/ppermute | solution.py:358
  166.2 0.8 collective-permute-start.17
  167.1 5.7 %attend_memory.3 = (bf16[1024,256]{1,0:T(8,128)(2,1)}, bf16[256,256]{1,0:T(8,128)(2,1)}) custom-call(s32[8,4]{1,0:T(8,128)} %copy-done.17, s32[4]{0:T(128)} %copy-done.14, bf16[1024,256]{1,0:T(8,128)(2,1)} %copy-done.1, bf16[1024,256]{1,0:T(8,128)(2,1)} %refs_1_.3, bf16[1024,256]{1,0:T(8,128)(2,1)} %copy-done.3, bf16[1024,256]{1,0:T(8,128)(2,1)} %copy-done.4, ...), custom_call_target="tpu_custom_call" | custom-call | flops 268435456 | bytes 6291456 | tf_op jit(solution)/shard_map/attend_memory/pallas_call | solution.py:260
  172.8 0.0 collective-permute-done.15.refs_1_
  172.8 0.9 collective-permute-done.17.refs_3_
  173.8 0.9 copy-done.13
  174.7 5.2 %back_project.1 = (f32[128,4096]{1,0:T(8,128)S(1)}, bf16[128,4096]{1,0:T(8,128)(2,1)S(1)}) custom-call(s32[4]{0:T(128)S(1)} %copy-done.15, bf16[256,256]{1,0:T(8,128)(2,1)S(1)} %copy-done.13, bf16[256,256]{1,0:T(8,128)(2,1)S(1)} %collective-permute-done.15.refs_1_, bf16[256,256]{1,0:T(8,128)(2,1)S(1)} %collective-permute-done.16.refs_2_, ...), custom_call_target="tpu_custom_call" | custom-call | flops 2147483648 | bytes 12582912 | tf_op jit(solution)/shard_map/back_project/pallas_call | solution.py:330
  179.8 14.4 %collective-permute-start.20 = (bf16[128,4096]{1,0:T(8,128)(2,1)S(1)}, bf16[128,4096]{1,0:T(8,128)(2,1)S(1)}, u32[]{:S(2)}, u32[]{:S(2)}) collective-permute-start(bf16[128,4096]{1,0:T(8,128)(2,1)S(1)} %get-tuple-element.63), channel_id=1, source_target_pairs={{0,1},{1,0},{2,3},{3,2},{4,5},{5,4},{6,7},{7,6},{8,9},{9,8},{10,11... | collective-permute-start | bytes 3145736 | tf_op jit(solution)/shard_map/ppermute | solution.py:358
  194.2 2.3 %collective-permute-done.20 = bf16[128,4096]{1,0:T(8,128)(2,1)S(1)} collective-permute-done((bf16[128,4096]{1,0:T(8,128)(2,1)S(1)}, bf16[128,4096]{1,0:T(8,128)(2,1)S(1)}, u32[]{:S(2)}, u32[]{:S(2)}) %collective-permute-start.20) | collective-permute-done | bytes 1048608 | tf_op jit(solution)/shard_map/ppermute | solution.py:358
  196.5 1.2 add_convert_fusion
  (48 shorter events, 0.1 us)
Async XLA Ops:
  7.2 115.0 %all-gather.2.cloned.1.call-start = ((), (), s32[]{:S(2)}) async-start(), calls=%async_computation.2 | async-start | bytes 9437184 | tf_op jit(solution)/shard_map/all_gather | solution.py:374
  7.9 8.6 %collective-permute-start = (bf16[128,256]{1,0:T(8,128)(2,1)}, bf16[128,256]{1,0:T(8,128)(2,1)S(1)}, u32[]{:S(2)}, u32[]{:S(2)}) collective-permute-start(bf16[128,256]{1,0:T(8,128)(2,1)} %param.7), channel_id=1, source_target_pairs={{0,32},{32,64},{64,96},{96,128},{128,160},{160,192},{192,224},{224... | collective-permute-start | bytes 196616 | tf_op jit(solution)/shard_map/ppermute | solution.py:358
  8.7 9.9 %collective-permute-start.1 = (bf16[128,256]{1,0:T(8,128)(2,1)}, bf16[128,256]{1,0:T(8,128)(2,1)S(1)}, u32[]{:S(2)}, u32[]{:S(2)}) collective-permute-start(bf16[128,256]{1,0:T(8,128)(2,1)} %param.7), channel_id=1, source_target_pairs={{0,64},{32,96},{64,128},{96,160},{128,192},{160,224},{192,0},{224,... | collective-permute-start | bytes 196616 | tf_op jit(solution)/shard_map/ppermute | solution.py:358
  9.9 24.3 %collective-permute-start.2 = (bf16[128,256]{1,0:T(8,128)(2,1)}, bf16[128,256]{1,0:T(8,128)(2,1)S(1)}, u32[]{:S(2)}, u32[]{:S(2)}) collective-permute-start(bf16[128,256]{1,0:T(8,128)(2,1)} %param.7), channel_id=1, source_target_pairs={{0,96},{32,128},{64,160},{96,192},{128,224},{160,0},{192,32},{224,... | collective-permute-start | bytes 196616 | tf_op jit(solution)/shard_map/ppermute | solution.py:358
  9.9 24.3 %collective-permute-start.3 = (bf16[128,256]{1,0:T(8,128)(2,1)}, bf16[128,256]{1,0:T(8,128)(2,1)S(1)}, u32[]{:S(2)}, u32[]{:S(2)}) collective-permute-start(bf16[128,256]{1,0:T(8,128)(2,1)} %param.7), channel_id=1, source_target_pairs={{0,128},{32,160},{64,192},{96,224},{128,0},{160,32},{192,64},{224,... | collective-permute-start | bytes 196616 | tf_op jit(solution)/shard_map/ppermute | solution.py:358
  14.8 19.4 %collective-permute-start.4 = (bf16[128,256]{1,0:T(8,128)(2,1)}, bf16[128,256]{1,0:T(8,128)(2,1)S(1)}, u32[]{:S(2)}, u32[]{:S(2)}) collective-permute-start(bf16[128,256]{1,0:T(8,128)(2,1)} %param.7), channel_id=1, source_target_pairs={{0,160},{32,192},{64,224},{96,0},{128,32},{160,64},{192,96},{224,1... | collective-permute-start | bytes 196616 | tf_op jit(solution)/shard_map/ppermute | solution.py:358
  16.3 36.6 %copy-start.17 = (s32[8,4]{1,0:T(8,128)}, s32[8,4]{1,0:T(8,128)S(1)}, u32[]{:S(2)}) copy-start(s32[8,4]{1,0:T(8,128)S(1)} %get-tuple-element.65.owner_ref) | copy-start | bytes 388
  16.5 17.7 %collective-permute-start.5 = (bf16[128,256]{1,0:T(8,128)(2,1)}, bf16[128,256]{1,0:T(8,128)(2,1)S(1)}, u32[]{:S(2)}, u32[]{:S(2)}) collective-permute-start(bf16[128,256]{1,0:T(8,128)(2,1)} %param.7), channel_id=1, source_target_pairs={{0,192},{32,224},{64,0},{96,32},{128,64},{160,96},{192,128},{224,1... | collective-permute-start | bytes 196616 | tf_op jit(solution)/shard_map/ppermute | solution.py:358
  18.6 15.6 %collective-permute-start.6 = (bf16[128,256]{1,0:T(8,128)(2,1)}, bf16[128,256]{1,0:T(8,128)(2,1)S(1)}, u32[]{:S(2)}, u32[]{:S(2)}) collective-permute-start(bf16[128,256]{1,0:T(8,128)(2,1)} %param.7), channel_id=1, source_target_pairs={{0,224},{32,0},{64,32},{96,64},{128,96},{160,128},{192,160},{224,1... | collective-permute-start | bytes 196616 | tf_op jit(solution)/shard_map/ppermute | solution.py:358
  52.9 9.6 %copy-start.18 = (bf16[128,256]{1,0:T(8,128)(2,1)S(1)}, bf16[128,256]{1,0:T(8,128)(2,1)}, u32[]{:S(2)}) copy-start(bf16[128,256]{1,0:T(8,128)(2,1)} %param.7) | copy-start | bytes 196612
  52.9 101.2 %all-to-all-start.1 = ((bf16[32,2,128,256]{3,2,1,0:T(8,128)(2,1)}), bf16[32,2,128,256]{3,2,1,0:T(8,128)(2,1)}, u32[]{:S(2)}, u32[]{:S(2)}) async-start(bf16[32,2,128,256]{3,2,1,0:T(8,128)(2,1)} %pick_blocks.1), calls=%async_computation.1 | async-start | bytes 8388608 | tf_op jit(solution)/shard_map/all_to_all | solution.py:372
  62.6 32.6 %collective-permute-start.7 = (bf16[8,128,256]{2,1,0:T(8,128)(2,1)S(1)}, bf16[8,128,256]{2,1,0:T(8,128)(2,1)S(1)}, u32[]{:S(2)}, u32[]{:S(2)}) collective-permute-start(bf16[8,128,256]{2,1,0:T(8,128)(2,1)S(1)} %bitcast_dynamic-update-slice_fusion.refs_0_.refs_4_), channel_id=1, source_target_pairs={{0,8},{8,16},{16,24},{24,0},{1,9},{9,17},{17,25},{25,1},{2,10},{10... | collective-permute-start | bytes 1572872 | tf_op jit(solution)/shard_map/ppermute | solution.py:358
  63.9 49.0 %collective-permute-start.8 = (bf16[8,128,256]{2,1,0:T(8,128)(2,1)S(1)}, bf16[8,128,256]{2,1,0:T(8,128)(2,1)S(1)}, u32[]{:S(2)}, u32[]{:S(2)}) collective-permute-start(bf16[8,128,256]{2,1,0:T(8,128)(2,1)S(1)} %bitcast_dynamic-update-slice_fusion.refs_0_.refs_4_), channel_id=1, source_target_pairs={{0,16},{8,24},{16,0},{24,8},{1,17},{9,25},{17,1},{25,9},{2,18},{10... | collective-permute-start | bytes 1572872 | tf_op jit(solution)/shard_map/ppermute | solution.py:358
  66.3 50.5 %collective-permute-start.9 = (bf16[8,128,256]{2,1,0:T(8,128)(2,1)S(1)}, bf16[8,128,256]{2,1,0:T(8,128)(2,1)S(1)}, u32[]{:S(2)}, u32[]{:S(2)}) collective-permute-start(bf16[8,128,256]{2,1,0:T(8,128)(2,1)S(1)} %bitcast_dynamic-update-slice_fusion.refs_0_.refs_4_), channel_id=1, source_target_pairs={{0,24},{8,0},{16,8},{24,16},{1,25},{9,1},{17,9},{25,17},{2,26},{10... | collective-permute-start | bytes 1572872 | tf_op jit(solution)/shard_map/ppermute | solution.py:358
  67.5 49.5 %collective-permute-start.10 = (bf16[8,128,256]{2,1,0:T(8,128)(2,1)S(1)}, bf16[8,128,256]{2,1,0:T(8,128)(2,1)S(1)}, u32[]{:S(2)}, u32[]{:S(2)}) collective-permute-start(bf16[8,128,256]{2,1,0:T(8,128)(2,1)S(1)} %bitcast_dynamic-update-slice_fusion.refs_0_.refs_4_), channel_id=1, source_target_pairs={{0,2},{2,4},{4,6},{6,0},{1,3},{3,5},{5,7},{7,1},{8,10},{10,12},{12... | collective-permute-start | bytes 1572872 | tf_op jit(solution)/shard_map/ppermute | solution.py:358
  68.7 49.1 %collective-permute-start.11 = (bf16[8,128,256]{2,1,0:T(8,128)(2,1)S(1)}, bf16[8,128,256]{2,1,0:T(8,128)(2,1)S(1)}, u32[]{:S(2)}, u32[]{:S(2)}) collective-permute-start(bf16[8,128,256]{2,1,0:T(8,128)(2,1)S(1)} %bitcast_dynamic-update-slice_fusion.refs_0_.refs_4_), channel_id=1, source_target_pairs={{0,4},{2,6},{4,0},{6,2},{1,5},{3,7},{5,1},{7,3},{8,12},{10,14},{12... | collective-permute-start | bytes 1572872 | tf_op jit(solution)/shard_map/ppermute | solution.py:358
  95.2 23.4 %collective-permute-start.12 = (bf16[8,128,256]{2,1,0:T(8,128)(2,1)S(1)}, bf16[8,128,256]{2,1,0:T(8,128)(2,1)S(1)}, u32[]{:S(2)}, u32[]{:S(2)}) collective-permute-start(bf16[8,128,256]{2,1,0:T(8,128)(2,1)S(1)} %bitcast_dynamic-update-slice_fusion.refs_0_.refs_4_), channel_id=1, source_target_pairs={{0,6},{2,0},{4,2},{6,4},{1,7},{3,1},{5,3},{7,5},{8,14},{10,8},{12,... | collective-permute-start | bytes 1572872 | tf_op jit(solution)/shard_map/ppermute | solution.py:358
  117.0 0.8 copy-start.7
  117.8 0.8 copy-start.9
  118.6 0.8 copy-start.11
  119.4 27.8 %collective-permute-start.13 = (bf16[24,128,256]{2,1,0:T(8,128)(2,1)S(1)}, bf16[24,128,256]{2,1,0:T(8,128)(2,1)}, u32[]{:S(2)}, u32[]{:S(2)}) collective-permute-start(bf16[24,128,256]{2,1,0:T(8,128)(2,1)S(1)} %pad_maximum_fusion.refs_1_.refs_8_), channel_id=1, source_target_pairs={{0,2},{2,4},{4,6},{6,0},{1,3},{3,5},{5,7},{7,1},{8,10},{10,12},{12... | collective-permute-start | bytes 4718600 | tf_op jit(solution)/shard_map/ppermute | solution.py:358
  120.7 26.5 %collective-permute-start.14 = (bf16[24,128,256]{2,1,0:T(8,128)(2,1)S(1)}, bf16[24,128,256]{2,1,0:T(8,128)(2,1)}, u32[]{:S(2)}, u32[]{:S(2)}) collective-permute-start(bf16[24,128,256]{2,1,0:T(8,128)(2,1)S(1)} %pad_maximum_fusion.refs_1_.refs_8_), channel_id=1, source_target_pairs={{0,6},{2,0},{4,2},{6,4},{1,7},{3,1},{5,3},{7,5},{8,14},{10,8},{12,... | collective-permute-start | bytes 4718600 | tf_op jit(solution)/shard_map/ppermute | solution.py:358
  122.2 7.2 %copy-start.14 = (s32[4]{0:T(128)}, s32[4]{0:T(128)S(1)}, u32[]{:S(2)}) copy-start(s32[4]{0:T(128)S(1)} %pad_add_fusion.pos_ref) | copy-start | bytes 52
  122.2 3.4 %copy-start = (bf16[1024,4096]{1,0:T(8,128)(2,1)S(1)}, bf16[1024,4096]{1,0:T(8,128)(2,1)}, u32[]{:S(2)}) copy-start(bf16[1024,4096]{1,0:T(8,128)(2,1)} %all-gather.2.cloned.1.call-done.x_ref) | copy-start | bytes 25165828
  125.6 3.8 %copy-start.2 = (bf16[1024,256]{1,0:T(8,128)(2,1)S(1)}, bf16[1024,256]{1,0:T(8,128)(2,1)}, u32[]{:S(2)}) copy-start(bf16[1024,256]{1,0:T(8,128)(2,1)} %refs_1_.3) | copy-start | bytes 1572868
  125.6 3.8 %copy-start.16 = (bf16[2,1024,256]{2,1,0:T(8,128)(2,1)S(1)}, bf16[2,1024,256]{2,1,0:T(8,128)(2,1)}, u32[]{:S(2)}) copy-start(bf16[2,1024,256]{2,1,0:T(8,128)(2,1)} %local_ref.1) | copy-start | bytes 3145732
  129.4 5.0 %copy-start.1 = (bf16[1024,256]{1,0:T(8,128)(2,1)}, bf16[1024,256]{1,0:T(8,128)(2,1)S(1)}, u32[]{:S(2)}) copy-start(bf16[1024,256]{1,0:T(8,128)(2,1)S(1)} %project.1.query_ref.refs_0_) | copy-start | bytes 1572868
  134.4 0.8 copy-start.3
  135.2 0.8 copy-start.4
  136.1 0.8 copy-start.5
  136.8 0.8 copy-start.6
  149.3 24.4 %collective-permute-start.18 = (bf16[12,128,256]{2,1,0:T(8,128)(2,1)}, bf16[12,128,256]{2,1,0:T(8,128)(2,1)S(1)}, u32[]{:S(2)}, u32[]{:S(2)}) collective-permute-start(bf16[12,128,256]{2,1,0:T(8,128)(2,1)} %slice.6), channel_id=1, source_target_pairs={{0,2},{2,4},{4,6},{6,0},{1,3},{3,5},{5,7},{7,1},{8,10},{10,12},{12... | collective-permute-start | bytes 2359304 | tf_op jit(solution)/shard_map/ppermute | solution.py:358
  152.5 21.2 %collective-permute-start.19 = (bf16[12,128,256]{2,1,0:T(8,128)(2,1)}, bf16[12,128,256]{2,1,0:T(8,128)(2,1)}, u32[]{:S(2)}, u32[]{:S(2)}) collective-permute-start(bf16[12,128,256]{2,1,0:T(8,128)(2,1)} %slice.7), channel_id=1, source_target_pairs={{0,6},{2,0},{4,2},{6,4},{1,7},{3,1},{5,3},{7,5},{8,14},{10,8},{12,... | collective-permute-start | bytes 2359304 | tf_op jit(solution)/shard_map/ppermute | solution.py:358
  163.8 9.0 %collective-permute-start.15 = (bf16[256,256]{1,0:T(8,128)(2,1)}, bf16[256,256]{1,0:T(8,128)(2,1)S(1)}, u32[]{:S(2)}, u32[]{:S(2)}) collective-permute-start(bf16[256,256]{1,0:T(8,128)(2,1)} %get-tuple-element.53), channel_id=1, source_target_pairs={{0,2},{2,4},{4,6},{6,0},{1,3},{3,5},{5,7},{7,1},{8,10},{10,12},{12... | collective-permute-start | bytes 393224 | tf_op jit(solution)/shard_map/ppermute | solution.py:358
  163.9 9.0 %collective-permute-start.16 = (bf16[256,256]{1,0:T(8,128)(2,1)}, bf16[256,256]{1,0:T(8,128)(2,1)S(1)}, u32[]{:S(2)}, u32[]{:S(2)}) collective-permute-start(bf16[256,256]{1,0:T(8,128)(2,1)} %get-tuple-element.54), channel_id=1, source_target_pairs={{0,4},{2,6},{4,0},{6,2},{1,5},{3,7},{5,1},{7,3},{8,12},{10,14},{12... | collective-permute-start | bytes 393224 | tf_op jit(solution)/shard_map/ppermute | solution.py:358
  166.2 7.5 %collective-permute-start.17 = (bf16[256,256]{1,0:T(8,128)(2,1)}, bf16[256,256]{1,0:T(8,128)(2,1)S(1)}, u32[]{:S(2)}, u32[]{:S(2)}) collective-permute-start(bf16[256,256]{1,0:T(8,128)(2,1)} %get-tuple-element.55), channel_id=1, source_target_pairs={{0,6},{2,0},{4,2},{6,4},{1,7},{3,1},{5,3},{7,5},{8,14},{10,8},{12,... | collective-permute-start | bytes 393224 | tf_op jit(solution)/shard_map/ppermute | solution.py:358
  167.1 6.7 %copy-start.8 = (bf16[8,128,256]{2,1,0:T(8,128)(2,1)S(1)}, bf16[8,128,256]{2,1,0:T(8,128)(2,1)}, u32[]{:S(2)}) copy-start(bf16[8,128,256]{2,1,0:T(8,128)(2,1)} %copy-done.7) | copy-start | bytes 1572868
  167.1 6.7 %copy-start.10 = (bf16[8,128,256]{2,1,0:T(8,128)(2,1)S(1)}, bf16[8,128,256]{2,1,0:T(8,128)(2,1)}, u32[]{:S(2)}) copy-start(bf16[8,128,256]{2,1,0:T(8,128)(2,1)} %copy-done.9) | copy-start | bytes 1572868
  167.1 6.7 %copy-start.12 = (bf16[8,128,256]{2,1,0:T(8,128)(2,1)S(1)}, bf16[8,128,256]{2,1,0:T(8,128)(2,1)}, u32[]{:S(2)}) copy-start(bf16[8,128,256]{2,1,0:T(8,128)(2,1)} %copy-done.11) | copy-start | bytes 1572868
  167.1 6.7 %copy-start.15 = (s32[4]{0:T(128)S(1)}, s32[4]{0:T(128)}, u32[]{:S(2)}) copy-start(s32[4]{0:T(128)} %copy-done.14) | copy-start | bytes 52
  173.8 0.9 copy-start.13
  179.8 16.6 %collective-permute-start.20 = (bf16[128,4096]{1,0:T(8,128)(2,1)S(1)}, bf16[128,4096]{1,0:T(8,128)(2,1)S(1)}, u32[]{:S(2)}, u32[]{:S(2)}) collective-permute-start(bf16[128,4096]{1,0:T(8,128)(2,1)S(1)} %get-tuple-element.63), channel_id=1, source_target_pairs={{0,1},{1,0},{2,3},{3,2},{4,5},{5,4},{6,7},{7,6},{8,9},{9,8},{10,11... | collective-permute-start | bytes 3145736 | tf_op jit(solution)/shard_map/ppermute | solution.py:358
Sparse Core Ops, SparseCore 0:
  9.9 54.2 all-gather.1
where the time goes:
time: 205 us
  waiting for transfers between devices  56.3 us (27%)
  starting transfers between devices  55.1 us (27%)
  Pallas kernels  48 us (23%)
  local copies, waits for them, and re-layouts  15.1 us (7%)
  between operations  14.3 us (7%)
  blocking collectives  12.9 us (6%)
  other arithmetic  2.71 us (1%)
    ppermute x21, waiting for transfers between devices, move(): lax.ppermute(array, axis, [(i, (i + shift) % count) for i in range(count)])  55.6 us
    ppermute x21, starting transfers between devices, move(): lax.ppermute(array, axis, [(i, (i + shift) % count) for i in range(count)])  45.4 us
    pallas_call x1, Pallas kernels, pick_blocks(): pl.pallas_call(pick_kernel, grid_spec=pltpu.PrefetchScalarGridSpec(num_sc...  18.6 us
    pallas_call x2, Pallas kernels, attend_memory(): pl.pallas_call(functools.partial(attend_memory_kernel, shifts), in_specs=...  15.4 us
    all_to_all x1, blocking collectives, local(): asked = lax.all_to_all(wanted.reshape(OWNERS, 1), MEM, 0, 0, tiled=True)  12.9 us
    unnamed x46, local copies, waits for them, and re-layouts  10.7 us
    all_to_all x1, starting transfers between devices, local(): lax.all_to_all(pick_blocks(asked[:, 0], memory_kv), MEM, 0, 0, tiled=True)  9.61 us
    pallas_call x1, Pallas kernels, back_project(): pl.pallas_call(back_kernel, in_specs=[pl.BlockSpec(memory_space=pltpu.SME...  5.15 us
  transfers between devices with their start and end apart: 23, of which 6 were waited for; matrix products, arithmetic and copies ran while one was open for 3% of the time, Pallas kernels for 21%

commit v1 on v0

--- a/solution.py
+++ b/solution.py
@@ -49,7 +49,7 @@
             out_specs=pl.BlockSpec(block, lambda i, asked_ref: (i, 0, 0, 0)),
         ),
         out_shape=jax.ShapeDtypeStruct((OWNERS, 2, BLK, WIDTH), jnp.bfloat16),
-        compiler_params=pltpu.CompilerParams(vmem_limit_bytes=56 * MIB),
+        compiler_params=pltpu.CompilerParams(vmem_limit_bytes=4 * MIB),
         cost_estimate=pl.CostEstimate(
             flops=0, bytes_accessed=2 * OWNERS * 2 * BLK * WIDTH * 2, transcendentals=0
         ),

time: 205 us -> 191 us (0.932)
  Pallas kernels: 48 us -> 30.6 us
  local copies, waits for them, and re-layouts: 15.1 us -> 18.7 us
    pallas_call x1, Pallas kernels: 18.6 us -> 1.27 us  [pick_blocks(): pl.pallas_call(pick_kernel, grid_spec=pltpu.PrefetchScalarGridSpec(num_sc...]
    unnamed x46 -> x50, local copies, waits for them, and re-layouts: 10.7 us -> 14.3 us
  transfers between devices with their start and end apart: 23 -> 23, of which waited for: 6 -> 7; matrix products, arithmetic and copies ran while one was open for 3% -> 3% of each run, Pallas kernels for 21% -> 13%
where the time goes in v1:
time: 191 us; the launch traced here: 190 us
  waiting for transfers between devices  56.5 us (30%)
  starting transfers between devices  54.8 us (29%)
  Pallas kernels  30.6 us (16%)
  local copies, waits for them, and re-layouts  18.7 us (10%)
  between operations  14.4 us (8%)
  blocking collectives  12.9 us (7%)
  other arithmetic  2.19 us (1%)
    ppermute x21, waiting for transfers between devices, move(): lax.ppermute(array, axis, [(i, (i + shift) % count) for i in range(count)])  55.9 us
    ppermute x21, starting transfers between devices, move(): lax.ppermute(array, axis, [(i, (i + shift) % count) for i in range(count)])  45.2 us
    pallas_call x2, Pallas kernels, attend_memory(): pl.pallas_call(functools.partial(attend_memory_kernel, shifts), in_specs=...  15.4 us
    unnamed x50, local copies, waits for them, and re-layouts  14.3 us
    all_to_all x1, blocking collectives, local(): asked = lax.all_to_all(wanted.reshape(OWNERS, 1), MEM, 0, 0, tiled=True)  12.9 us
    all_to_all x1, starting transfers between devices, local(): lax.all_to_all(pick_blocks(asked[:, 0], memory_kv), MEM, 0, 0, tiled=True)  9.52 us
    pallas_call x1, Pallas kernels, back_project(): pl.pallas_call(back_kernel, in_specs=[pl.BlockSpec(memory_space=pltpu.SME...  5.14 us
    pallas_call x1, Pallas kernels, attend_local(): pl.pallas_call(attend_local_kernel, in_specs=[in_vmem] * 3, out_specs=[in...  5 us
  transfers between devices with their start and end apart: 23, of which 7 were waited for; matrix products, arithmetic and copies ran while one was open for 3% of the time, Pallas kernels for 13%

profile of v1, /device:TPU:129, one launch (start us, length us, event | category | flops | bytes accessed | tf_op | source)
XLA Modules:
  0.0 190.1 jit_solution(5866855112083135422)
XLA Ops:
  7.2 0.0 all-gather.2.cloned.1.call-start
  7.2 0.7 all-gather.2.cloned.1.call-update
  7.9 0.8 collective-permute-start
  8.7 1.2 collective-permute-start.1
  9.9 4.9 %collective-permute-start.3 = (bf16[128,256]{1,0:T(8,128)(2,1)}, bf16[128,256]{1,0:T(8,128)(2,1)S(1)}, u32[]{:S(2)}, u32[]{:S(2)}) collective-permute-start(bf16[128,256]{1,0:T(8,128)(2,1)} %param.7), channel_id=1, source_target_pairs={{0,128},{32,160},{64,192},{96,224},{128,0},{160,32},{192,64},{224,... | collective-permute-start | bytes 196616 | tf_op jit(solution)/shard_map/ppermute | solution.py:358
  14.8 0.7 collective-permute-start.4
  15.5 0.8 copy.22
  16.3 0.1 copy.26
  16.4 0.1 copy.27
  16.5 0.0 collective-permute-done
  16.5 2.1 %collective-permute-start.5 = (bf16[128,256]{1,0:T(8,128)(2,1)}, bf16[128,256]{1,0:T(8,128)(2,1)S(1)}, u32[]{:S(2)}, u32[]{:S(2)}) collective-permute-start(bf16[128,256]{1,0:T(8,128)(2,1)} %param.7), channel_id=1, source_target_pairs={{0,192},{32,224},{64,0},{96,32},{128,64},{160,96},{192,128},{224,1... | collective-permute-start | bytes 196616 | tf_op jit(solution)/shard_map/ppermute | solution.py:358
  18.6 1.3 collective-permute-start.6
  19.9 0.1 select_reduce_fusion
  20.0 0.1 copy.28
  20.1 12.9 %all_to_all.17 = s32[32,1,1]{2,1,0:T(1,128)S(1)} all-to-all(s32[32,1,1]{2,1,0:T(1,128)S(1)} %copy.28), channel_id=1, replica_groups=mesh['z'=8,'x'=4,'y'=4,'c'=2] {'z','x'}, dimensions={0} | all-to-all | bytes 256 | tf_op jit(solution)/shard_map/all_to_all | solution.py:370
  33.0 0.7 reduce
  33.7 0.0 collective-permute-done.2
  33.7 0.0 collective-permute-done.4
  33.7 0.0 copy-start.3
  33.7 1.7 copy-done.3
  35.4 1.3 pick_blocks.1
  36.7 1.9 %copy-done = bf16[32,2,128,256]{3,2,1,0:T(8,128)(2,1)} copy-done((bf16[32,2,128,256]{3,2,1,0:T(8,128)(2,1)}, bf16[32,2,128,256]{3,2,1,0:T(8,128)(2,1)S(1)}, u32[]{:S(2)}) %copy-start) | copy-done | bytes 4194328
  38.7 9.5 %all-to-all-start.1 = ((bf16[32,2,128,256]{3,2,1,0:T(8,128)(2,1)}), bf16[32,2,128,256]{3,2,1,0:T(8,128)(2,1)}, u32[]{:S(2)}, u32[]{:S(2)}) async-start(bf16[32,2,128,256]{3,2,1,0:T(8,128)(2,1)} %copy-done), calls=%async_computation.1 | async-start | bytes 8388608 | tf_op jit(solution)/shard_map/all_to_all | solution.py:372
  48.3 1.3 collective-permute-start.7
  49.6 2.4 %collective-permute-start.8 = (bf16[8,128,256]{2,1,0:T(8,128)(2,1)S(1)}, bf16[8,128,256]{2,1,0:T(8,128)(2,1)S(1)}, u32[]{:S(2)}, u32[]{:S(2)}) collective-permute-start(bf16[8,128,256]{2,1,0:T(8,128)(2,1)S(1)} %bitcast_dynamic-update-slice_fusion.refs_0_.refs_4_), channel_id=1, source_target_pairs={{0,16},{8,24},{16,0},{24,8},{1,17},{9,25},{17,1},{25,9},{2,18},{10... | collective-permute-start | bytes 1572872 | tf_op jit(solution)/shard_map/ppermute | solution.py:358
  52.0 1.2 collective-permute-start.9
  53.2 1.3 collective-permute-start.10
  54.5 2.6 %collective-permute-start.11 = (bf16[8,128,256]{2,1,0:T(8,128)(2,1)S(1)}, bf16[8,128,256]{2,1,0:T(8,128)(2,1)S(1)}, u32[]{:S(2)}, u32[]{:S(2)}) collective-permute-start(bf16[8,128,256]{2,1,0:T(8,128)(2,1)S(1)} %bitcast_dynamic-update-slice_fusion.refs_0_.refs_4_), channel_id=1, source_target_pairs={{0,4},{2,6},{4,0},{6,2},{1,5},{3,7},{5,1},{7,3},{8,12},{10,14},{12... | collective-permute-start | bytes 1572872 | tf_op jit(solution)/shard_map/ppermute | solution.py:358
  57.1 23.8 %collective-permute-done.7 = bf16[8,128,256]{2,1,0:T(8,128)(2,1)S(1)} collective-permute-done((bf16[8,128,256]{2,1,0:T(8,128)(2,1)S(1)}, bf16[8,128,256]{2,1,0:T(8,128)(2,1)S(1)}, u32[]{:S(2)}, u32[]{:S(2)}) %collective-permute-start.7) | collective-permute-done | bytes 524320 | tf_op jit(solution)/shard_map/ppermute | solution.py:358
  80.9 2.7 %collective-permute-start.12 = (bf16[8,128,256]{2,1,0:T(8,128)(2,1)S(1)}, bf16[8,128,256]{2,1,0:T(8,128)(2,1)S(1)}, u32[]{:S(2)}, u32[]{:S(2)}) collective-permute-start(bf16[8,128,256]{2,1,0:T(8,128)(2,1)S(1)} %bitcast_dynamic-update-slice_fusion.refs_0_.refs_4_), channel_id=1, source_target_pairs={{0,6},{2,0},{4,2},{6,4},{1,7},{3,1},{5,3},{7,5},{8,14},{10,8},{12,... | collective-permute-start | bytes 1572872 | tf_op jit(solution)/shard_map/ppermute | solution.py:358
  83.6 14.9 %collective-permute-done.8 = bf16[8,128,256]{2,1,0:T(8,128)(2,1)S(1)} collective-permute-done((bf16[8,128,256]{2,1,0:T(8,128)(2,1)S(1)}, bf16[8,128,256]{2,1,0:T(8,128)(2,1)S(1)}, u32[]{:S(2)}, u32[]{:S(2)}) %collective-permute-start.8) | collective-permute-done | bytes 524320 | tf_op jit(solution)/shard_map/ppermute | solution.py:358
  98.4 4.1 %collective-permute-done.9 = bf16[8,128,256]{2,1,0:T(8,128)(2,1)S(1)} collective-permute-done((bf16[8,128,256]{2,1,0:T(8,128)(2,1)S(1)}, bf16[8,128,256]{2,1,0:T(8,128)(2,1)S(1)}, u32[]{:S(2)}, u32[]{:S(2)}) %collective-permute-start.9) | collective-permute-done | bytes 524320 | tf_op jit(solution)/shard_map/ppermute | solution.py:358
  102.5 0.2 pad_maximum_fusion.refs_1_.refs_8_
  102.7 0.8 copy-done.9
  103.5 0.0 collective-permute-done.11.refs_6_
  103.5 0.8 copy-done.11
  104.3 0.8 copy-done.13
  105.1 1.4 collective-permute-start.13
  106.5 1.4 collective-permute-start.14
  107.9 0.1 pad_add_fusion.pos_ref
  108.0 3.4 %copy-done.1 = bf16[1024,4096]{1,0:T(8,128)(2,1)S(1)} copy-done((bf16[1024,4096]{1,0:T(8,128)(2,1)S(1)}, bf16[1024,4096]{1,0:T(8,128)(2,1)}, u32[]{:S(2)}) %copy-start.1) | copy-done | bytes 8388632
  111.4 3.8 %project.1.query_ref.refs_0_ = bf16[1024,256]{1,0:T(8,128)(2,1)S(1)} custom-call(s32[4]{0:T(128)S(1)} %pad_add_fusion.pos_ref, bf16[1024,4096]{1,0:T(8,128)(2,1)S(1)} %copy-done.1, bf16[8,128,256]{2,1,0:T(8,128)(2,1)S(1)} %bitcast_dynamic-update-slice_fusion.refs_0_.refs_4_, bf16[24,128,256]{2,1,0:T(8,128)(2,1)S(1)} %pad_maximum_fusion.refs_1_.refs_8_), custom_call_target="tpu_custom_call" | custom-call | flops 2147483648 | bytes 11010048 | tf_op jit(solution)/shard_map/project/pallas_call | solution.py:82
  115.2 5.0 %attend_local.1 = (bf16[1024,256]{1,0:T(8,128)(2,1)S(1)}, bf16[1024,256]{1,0:T(8,128)(2,1)S(1)}, bf16[1024,256]{1,0:T(8,128)(2,1)S(1)}, f32[1024,128]{1,0:T(8,128)S(1)}) custom-call(bf16[1024,256]{1,0:T(8,128)(2,1)S(1)} %project.1.query_ref.refs_0_, bf16[2,1024,256]{2,1,0:T(8,128)(2,1)S(1)} %copy-done.18, bf16[1024,256]{1,0:T(8,128)(2,1)S(1)} %copy-done.4), custom_call_target="tpu_custom_call" | custom-call | flops 1509949440 | bytes 6291456 | tf_op jit(solution)/shard_map/attend_local/pallas_call | solution.py:143
  120.3 0.8 copy-done.5
  121.0 0.8 copy-done.6
  121.9 0.8 copy-done.7
  122.6 0.8 copy-done.8
  123.4 9.7 %collective-permute-done.13.refs_9_ = bf16[24,128,256]{2,1,0:T(8,128)(2,1)} collective-permute-done((bf16[24,128,256]{2,1,0:T(8,128)(2,1)S(1)}, bf16[24,128,256]{2,1,0:T(8,128)(2,1)}, u32[]{:S(2)}, u32[]{:S(2)}) %collective-permute-start.13) | collective-permute-done | bytes 1572896 | tf_op jit(solution)/shard_map/ppermute | solution.py:358
  133.2 2.1 %slice.6 = bf16[12,128,256]{2,1,0:T(8,128)(2,1)} slice(bf16[24,128,256]{2,1,0:T(8,128)(2,1)} %collective-permute-done.13.refs_9_), slice={[0:12], [0:128], [0:256]} | slice | bytes 1572864 | tf_op jit(solution)/shard_map/slice | solution.py:383
  135.2 0.9 collective-permute-start.18
  136.1 2.1 %slice.7 = bf16[12,128,256]{2,1,0:T(8,128)(2,1)} slice(bf16[24,128,256]{2,1,0:T(8,128)(2,1)} %collective-permute-done.14.refs_12_), slice={[12:24], [0:128], [0:256]} | slice | bytes 1572864 | tf_op jit(solution)/shard_map/slice | solution.py:384
  138.2 1.8 collective-permute-start.19
  140.0 9.7 %attend_memory.2 = (bf16[256,256]{1,0:T(8,128)(2,1)}, bf16[256,256]{1,0:T(8,128)(2,1)}, bf16[256,256]{1,0:T(8,128)(2,1)}, bf16[256,256]{1,0:T(8,128)(2,1)}, bf16...) custom-call(s32[8,4]{1,0:T(8,128)} %copy-done.19, s32[4]{0:T(128)} %copy-done.16, bf16[1024,256]{1,0:T(8,128)(2,1)} %copy-done.2, ...), custom_call_target="tpu_custom_call" | custom-call | flops 805306368 | bytes 6291456 | tf_op jit(solution)/shard_map/attend_memory/pallas_call | solution.py:260
  149.7 0.1 collective-permute-start.15
  149.8 2.4 %collective-permute-start.16 = (bf16[256,256]{1,0:T(8,128)(2,1)}, bf16[256,256]{1,0:T(8,128)(2,1)S(1)}, u32[]{:S(2)}, u32[]{:S(2)}) collective-permute-start(bf16[256,256]{1,0:T(8,128)(2,1)} %get-tuple-element.54), channel_id=1, source_target_pairs={{0,4},{2,6},{4,0},{6,2},{1,5},{3,7},{5,1},{7,3},{8,12},{10,14},{12... | collective-permute-start | bytes 393224 | tf_op jit(solution)/shard_map/ppermute | solution.py:358
  152.1 0.8 collective-permute-start.17
  152.9 5.7 %attend_memory.3 = (bf16[1024,256]{1,0:T(8,128)(2,1)}, bf16[256,256]{1,0:T(8,128)(2,1)}) custom-call(s32[8,4]{1,0:T(8,128)} %copy-done.19, s32[4]{0:T(128)} %copy-done.16, bf16[1024,256]{1,0:T(8,128)(2,1)} %copy-done.2, bf16[1024,256]{1,0:T(8,128)(2,1)} %refs_1_.3, bf16[1024,256]{1,0:T(8,128)(2,1)} %copy-done.5, bf16[1024,256]{1,0:T(8,128)(2,1)} %copy-done.6, ...), custom_call_target="tpu_custom_call" | custom-call | flops 268435456 | bytes 6291456 | tf_op jit(solution)/shard_map/attend_memory/pallas_call | solution.py:260
  158.6 0.2 collective-permute-done.16.refs_2_
  158.8 0.9 collective-permute-done.17.refs_3_
  159.8 0.9 copy-done.15
  160.7 5.1 %back_project.1 = (f32[128,4096]{1,0:T(8,128)S(1)}, bf16[128,4096]{1,0:T(8,128)(2,1)S(1)}) custom-call(s32[4]{0:T(128)S(1)} %copy-done.17, bf16[256,256]{1,0:T(8,128)(2,1)S(1)} %copy-done.15, bf16[256,256]{1,0:T(8,128)(2,1)S(1)} %collective-permute-done.15.refs_1_, bf16[256,256]{1,0:T(8,128)(2,1)S(1)} %collective-permute-done.16.refs_2_, ...), custom_call_target="tpu_custom_call" | custom-call | flops 2147483648 | bytes 12582912 | tf_op jit(solution)/shard_map/back_project/pallas_call | solution.py:330
  165.8 14.0 %collective-permute-start.20 = (bf16[128,4096]{1,0:T(8,128)(2,1)S(1)}, bf16[128,4096]{1,0:T(8,128)(2,1)S(1)}, u32[]{:S(2)}, u32[]{:S(2)}) collective-permute-start(bf16[128,4096]{1,0:T(8,128)(2,1)S(1)} %get-tuple-element.63), channel_id=1, source_target_pairs={{0,1},{1,0},{2,3},{3,2},{4,5},{5,4},{6,7},{7,6},{8,9},{9,8},{10,11... | collective-permute-start | bytes 3145736 | tf_op jit(solution)/shard_map/ppermute | solution.py:358
  179.8 2.3 %collective-permute-done.20 = bf16[128,4096]{1,0:T(8,128)(2,1)S(1)} collective-permute-done((bf16[128,4096]{1,0:T(8,128)(2,1)S(1)}, bf16[128,4096]{1,0:T(8,128)(2,1)S(1)}, u32[]{:S(2)}, u32[]{:S(2)}) %collective-permute-start.20) | collective-permute-done | bytes 1048608 | tf_op jit(solution)/shard_map/ppermute | solution.py:358
  182.1 1.2 add_convert_fusion
  (52 shorter events, 0.2 us)
Async XLA Ops:
  7.2 100.8 %all-gather.2.cloned.1.call-start = ((), (), s32[]{:S(2)}) async-start(), calls=%async_computation.2 | async-start | bytes 9437184 | tf_op jit(solution)/shard_map/all_gather | solution.py:374
  7.9 8.6 %collective-permute-start = (bf16[128,256]{1,0:T(8,128)(2,1)}, bf16[128,256]{1,0:T(8,128)(2,1)S(1)}, u32[]{:S(2)}, u32[]{:S(2)}) collective-permute-start(bf16[128,256]{1,0:T(8,128)(2,1)} %param.7), channel_id=1, source_target_pairs={{0,32},{32,64},{64,96},{96,128},{128,160},{160,192},{192,224},{224... | collective-permute-start | bytes 196616 | tf_op jit(solution)/shard_map/ppermute | solution.py:358
  8.7 9.9 %collective-permute-start.1 = (bf16[128,256]{1,0:T(8,128)(2,1)}, bf16[128,256]{1,0:T(8,128)(2,1)S(1)}, u32[]{:S(2)}, u32[]{:S(2)}) collective-permute-start(bf16[128,256]{1,0:T(8,128)(2,1)} %param.7), channel_id=1, source_target_pairs={{0,64},{32,96},{64,128},{96,160},{128,192},{160,224},{192,0},{224,... | collective-permute-start | bytes 196616 | tf_op jit(solution)/shard_map/ppermute | solution.py:358
  9.9 23.8 %collective-permute-start.2 = (bf16[128,256]{1,0:T(8,128)(2,1)}, bf16[128,256]{1,0:T(8,128)(2,1)S(1)}, u32[]{:S(2)}, u32[]{:S(2)}) collective-permute-start(bf16[128,256]{1,0:T(8,128)(2,1)} %param.7), channel_id=1, source_target_pairs={{0,96},{32,128},{64,160},{96,192},{128,224},{160,0},{192,32},{224,... | collective-permute-start | bytes 196616 | tf_op jit(solution)/shard_map/ppermute | solution.py:358
  9.9 23.8 %collective-permute-start.3 = (bf16[128,256]{1,0:T(8,128)(2,1)}, bf16[128,256]{1,0:T(8,128)(2,1)S(1)}, u32[]{:S(2)}, u32[]{:S(2)}) collective-permute-start(bf16[128,256]{1,0:T(8,128)(2,1)} %param.7), channel_id=1, source_target_pairs={{0,128},{32,160},{64,192},{96,224},{128,0},{160,32},{192,64},{224,... | collective-permute-start | bytes 196616 | tf_op jit(solution)/shard_map/ppermute | solution.py:358
  14.8 18.9 %collective-permute-start.4 = (bf16[128,256]{1,0:T(8,128)(2,1)}, bf16[128,256]{1,0:T(8,128)(2,1)S(1)}, u32[]{:S(2)}, u32[]{:S(2)}) collective-permute-start(bf16[128,256]{1,0:T(8,128)(2,1)} %param.7), channel_id=1, source_target_pairs={{0,160},{32,192},{64,224},{96,0},{128,32},{160,64},{192,96},{224,1... | collective-permute-start | bytes 196616 | tf_op jit(solution)/shard_map/ppermute | solution.py:358
  16.3 20.4 %copy-start.19 = (s32[8,4]{1,0:T(8,128)}, s32[8,4]{1,0:T(8,128)S(1)}, u32[]{:S(2)}) copy-start(s32[8,4]{1,0:T(8,128)S(1)} %get-tuple-element.65.owner_ref) | copy-start | bytes 388
  16.5 17.2 %collective-permute-start.5 = (bf16[128,256]{1,0:T(8,128)(2,1)}, bf16[128,256]{1,0:T(8,128)(2,1)S(1)}, u32[]{:S(2)}, u32[]{:S(2)}) collective-permute-start(bf16[128,256]{1,0:T(8,128)(2,1)} %param.7), channel_id=1, source_target_pairs={{0,192},{32,224},{64,0},{96,32},{128,64},{160,96},{192,128},{224,1... | collective-permute-start | bytes 196616 | tf_op jit(solution)/shard_map/ppermute | solution.py:358
  18.6 15.1 %collective-permute-start.6 = (bf16[128,256]{1,0:T(8,128)(2,1)}, bf16[128,256]{1,0:T(8,128)(2,1)S(1)}, u32[]{:S(2)}, u32[]{:S(2)}) collective-permute-start(bf16[128,256]{1,0:T(8,128)(2,1)} %param.7), channel_id=1, source_target_pairs={{0,224},{32,0},{64,32},{96,64},{128,96},{160,128},{192,160},{224,1... | collective-permute-start | bytes 196616 | tf_op jit(solution)/shard_map/ppermute | solution.py:358
  33.7 1.7 copy-start.3
  36.7 1.9 %copy-start = (bf16[32,2,128,256]{3,2,1,0:T(8,128)(2,1)}, bf16[32,2,128,256]{3,2,1,0:T(8,128)(2,1)S(1)}, u32[]{:S(2)}) copy-start(bf16[32,2,128,256]{3,2,1,0:T(8,128)(2,1)S(1)} %pick_blocks.1) | copy-start | bytes 12582916
  38.7 9.5 %copy-start.20 = (bf16[128,256]{1,0:T(8,128)(2,1)S(1)}, bf16[128,256]{1,0:T(8,128)(2,1)}, u32[]{:S(2)}) copy-start(bf16[128,256]{1,0:T(8,128)(2,1)} %param.7) | copy-start | bytes 196612
  38.7 101.3 %all-to-all-start.1 = ((bf16[32,2,128,256]{3,2,1,0:T(8,128)(2,1)}), bf16[32,2,128,256]{3,2,1,0:T(8,128)(2,1)}, u32[]{:S(2)}, u32[]{:S(2)}) async-start(bf16[32,2,128,256]{3,2,1,0:T(8,128)(2,1)} %copy-done), calls=%async_computation.1 | async-start | bytes 8388608 | tf_op jit(solution)/shard_map/all_to_all | solution.py:372
  48.3 32.6 %collective-permute-start.7 = (bf16[8,128,256]{2,1,0:T(8,128)(2,1)S(1)}, bf16[8,128,256]{2,1,0:T(8,128)(2,1)S(1)}, u32[]{:S(2)}, u32[]{:S(2)}) collective-permute-start(bf16[8,128,256]{2,1,0:T(8,128)(2,1)S(1)} %bitcast_dynamic-update-slice_fusion.refs_0_.refs_4_), channel_id=1, source_target_pairs={{0,8},{8,16},{16,24},{24,0},{1,9},{9,17},{17,25},{25,1},{2,10},{10... | collective-permute-start | bytes 1572872 | tf_op jit(solution)/shard_map/ppermute | solution.py:358
  49.6 48.9 %collective-permute-start.8 = (bf16[8,128,256]{2,1,0:T(8,128)(2,1)S(1)}, bf16[8,128,256]{2,1,0:T(8,128)(2,1)S(1)}, u32[]{:S(2)}, u32[]{:S(2)}) collective-permute-start(bf16[8,128,256]{2,1,0:T(8,128)(2,1)S(1)} %bitcast_dynamic-update-slice_fusion.refs_0_.refs_4_), channel_id=1, source_target_pairs={{0,16},{8,24},{16,0},{24,8},{1,17},{9,25},{17,1},{25,9},{2,18},{10... | collective-permute-start | bytes 1572872 | tf_op jit(solution)/shard_map/ppermute | solution.py:358
  52.0 50.6 %collective-permute-start.9 = (bf16[8,128,256]{2,1,0:T(8,128)(2,1)S(1)}, bf16[8,128,256]{2,1,0:T(8,128)(2,1)S(1)}, u32[]{:S(2)}, u32[]{:S(2)}) collective-permute-start(bf16[8,128,256]{2,1,0:T(8,128)(2,1)S(1)} %bitcast_dynamic-update-slice_fusion.refs_0_.refs_4_), channel_id=1, source_target_pairs={{0,24},{8,0},{16,8},{24,16},{1,25},{9,1},{17,9},{25,17},{2,26},{10... | collective-permute-start | bytes 1572872 | tf_op jit(solution)/shard_map/ppermute | solution.py:358
  53.2 49.6 %collective-permute-start.10 = (bf16[8,128,256]{2,1,0:T(8,128)(2,1)S(1)}, bf16[8,128,256]{2,1,0:T(8,128)(2,1)S(1)}, u32[]{:S(2)}, u32[]{:S(2)}) collective-permute-start(bf16[8,128,256]{2,1,0:T(8,128)(2,1)S(1)} %bitcast_dynamic-update-slice_fusion.refs_0_.refs_4_), channel_id=1, source_target_pairs={{0,2},{2,4},{4,6},{6,0},{1,3},{3,5},{5,7},{7,1},{8,10},{10,12},{12... | collective-permute-start | bytes 1572872 | tf_op jit(solution)/shard_map/ppermute | solution.py:358
  54.5 49.0 %collective-permute-start.11 = (bf16[8,128,256]{2,1,0:T(8,128)(2,1)S(1)}, bf16[8,128,256]{2,1,0:T(8,128)(2,1)S(1)}, u32[]{:S(2)}, u32[]{:S(2)}) collective-permute-start(bf16[8,128,256]{2,1,0:T(8,128)(2,1)S(1)} %bitcast_dynamic-update-slice_fusion.refs_0_.refs_4_), channel_id=1, source_target_pairs={{0,4},{2,6},{4,0},{6,2},{1,5},{3,7},{5,1},{7,3},{8,12},{10,14},{12... | collective-permute-start | bytes 1572872 | tf_op jit(solution)/shard_map/ppermute | solution.py:358
  80.9 23.5 %collective-permute-start.12 = (bf16[8,128,256]{2,1,0:T(8,128)(2,1)S(1)}, bf16[8,128,256]{2,1,0:T(8,128)(2,1)S(1)}, u32[]{:S(2)}, u32[]{:S(2)}) collective-permute-start(bf16[8,128,256]{2,1,0:T(8,128)(2,1)S(1)} %bitcast_dynamic-update-slice_fusion.refs_0_.refs_4_), channel_id=1, source_target_pairs={{0,6},{2,0},{4,2},{6,4},{1,7},{3,1},{5,3},{7,5},{8,14},{10,8},{12,... | collective-permute-start | bytes 1572872 | tf_op jit(solution)/shard_map/ppermute | solution.py:358
  102.7 0.8 copy-start.9
  103.5 0.8 copy-start.11
  104.3 0.8 copy-start.13
  105.1 28.1 %collective-permute-start.13 = (bf16[24,128,256]{2,1,0:T(8,128)(2,1)S(1)}, bf16[24,128,256]{2,1,0:T(8,128)(2,1)}, u32[]{:S(2)}, u32[]{:S(2)}) collective-permute-start(bf16[24,128,256]{2,1,0:T(8,128)(2,1)S(1)} %pad_maximum_fusion.refs_1_.refs_8_), channel_id=1, source_target_pairs={{0,2},{2,4},{4,6},{6,0},{1,3},{3,5},{5,7},{7,1},{8,10},{10,12},{12... | collective-permute-start | bytes 4718600 | tf_op jit(solution)/shard_map/ppermute | solution.py:358
  106.5 26.7 %collective-permute-start.14 = (bf16[24,128,256]{2,1,0:T(8,128)(2,1)S(1)}, bf16[24,128,256]{2,1,0:T(8,128)(2,1)}, u32[]{:S(2)}, u32[]{:S(2)}) collective-permute-start(bf16[24,128,256]{2,1,0:T(8,128)(2,1)S(1)} %pad_maximum_fusion.refs_1_.refs_8_), channel_id=1, source_target_pairs={{0,6},{2,0},{4,2},{6,4},{1,7},{3,1},{5,3},{7,5},{8,14},{10,8},{12,... | collective-permute-start | bytes 4718600 | tf_op jit(solution)/shard_map/ppermute | solution.py:358
  108.0 7.2 %copy-start.16 = (s32[4]{0:T(128)}, s32[4]{0:T(128)S(1)}, u32[]{:S(2)}) copy-start(s32[4]{0:T(128)S(1)} %pad_add_fusion.pos_ref) | copy-start | bytes 52
  108.0 3.4 %copy-start.1 = (bf16[1024,4096]{1,0:T(8,128)(2,1)S(1)}, bf16[1024,4096]{1,0:T(8,128)(2,1)}, u32[]{:S(2)}) copy-start(bf16[1024,4096]{1,0:T(8,128)(2,1)} %all-gather.2.cloned.1.call-done.x_ref) | copy-start | bytes 25165828
  111.4 3.8 %copy-start.4 = (bf16[1024,256]{1,0:T(8,128)(2,1)S(1)}, bf16[1024,256]{1,0:T(8,128)(2,1)}, u32[]{:S(2)}) copy-start(bf16[1024,256]{1,0:T(8,128)(2,1)} %refs_1_.3) | copy-start | bytes 1572868
  111.4 3.8 %copy-start.18 = (bf16[2,1024,256]{2,1,0:T(8,128)(2,1)S(1)}, bf16[2,1024,256]{2,1,0:T(8,128)(2,1)}, u32[]{:S(2)}) copy-start(bf16[2,1024,256]{2,1,0:T(8,128)(2,1)} %local_ref.1) | copy-start | bytes 3145732
  115.2 5.0 %copy-start.2 = (bf16[1024,256]{1,0:T(8,128)(2,1)}, bf16[1024,256]{1,0:T(8,128)(2,1)S(1)}, u32[]{:S(2)}) copy-start(bf16[1024,256]{1,0:T(8,128)(2,1)S(1)} %project.1.query_ref.refs_0_) | copy-start | bytes 1572868
  120.2 0.8 copy-start.5
  121.0 0.8 copy-start.6
  121.9 0.8 copy-start.7
  122.6 0.8 copy-start.8
  135.2 24.5 %collective-permute-start.18 = (bf16[12,128,256]{2,1,0:T(8,128)(2,1)}, bf16[12,128,256]{2,1,0:T(8,128)(2,1)S(1)}, u32[]{:S(2)}, u32[]{:S(2)}) collective-permute-start(bf16[12,128,256]{2,1,0:T(8,128)(2,1)} %slice.6), channel_id=1, source_target_pairs={{0,2},{2,4},{4,6},{6,0},{1,3},{3,5},{5,7},{7,1},{8,10},{10,12},{12... | collective-permute-start | bytes 2359304 | tf_op jit(solution)/shard_map/ppermute | solution.py:358
  138.2 21.5 %collective-permute-start.19 = (bf16[12,128,256]{2,1,0:T(8,128)(2,1)}, bf16[12,128,256]{2,1,0:T(8,128)(2,1)}, u32[]{:S(2)}, u32[]{:S(2)}) collective-permute-start(bf16[12,128,256]{2,1,0:T(8,128)(2,1)} %slice.7), channel_id=1, source_target_pairs={{0,6},{2,0},{4,2},{6,4},{1,7},{3,1},{5,3},{7,5},{8,14},{10,8},{12,... | collective-permute-start | bytes 2359304 | tf_op jit(solution)/shard_map/ppermute | solution.py:358
  149.7 8.9 %collective-permute-start.15 = (bf16[256,256]{1,0:T(8,128)(2,1)}, bf16[256,256]{1,0:T(8,128)(2,1)S(1)}, u32[]{:S(2)}, u32[]{:S(2)}) collective-permute-start(bf16[256,256]{1,0:T(8,128)(2,1)} %get-tuple-element.53), channel_id=1, source_target_pairs={{0,2},{2,4},{4,6},{6,0},{1,3},{3,5},{5,7},{7,1},{8,10},{10,12},{12... | collective-permute-start | bytes 393224 | tf_op jit(solution)/shard_map/ppermute | solution.py:358
  149.8 9.0 %collective-permute-start.16 = (bf16[256,256]{1,0:T(8,128)(2,1)}, bf16[256,256]{1,0:T(8,128)(2,1)S(1)}, u32[]{:S(2)}, u32[]{:S(2)}) collective-permute-start(bf16[256,256]{1,0:T(8,128)(2,1)} %get-tuple-element.54), channel_id=1, source_target_pairs={{0,4},{2,6},{4,0},{6,2},{1,5},{3,7},{5,1},{7,3},{8,12},{10,14},{12... | collective-permute-start | bytes 393224 | tf_op jit(solution)/shard_map/ppermute | solution.py:358
  152.1 7.6 %collective-permute-start.17 = (bf16[256,256]{1,0:T(8,128)(2,1)}, bf16[256,256]{1,0:T(8,128)(2,1)S(1)}, u32[]{:S(2)}, u32[]{:S(2)}) collective-permute-start(bf16[256,256]{1,0:T(8,128)(2,1)} %get-tuple-element.55), channel_id=1, source_target_pairs={{0,6},{2,0},{4,2},{6,4},{1,7},{3,1},{5,3},{7,5},{8,14},{10,8},{12,... | collective-permute-start | bytes 393224 | tf_op jit(solution)/shard_map/ppermute | solution.py:358
  152.9 6.8 %copy-start.10 = (bf16[8,128,256]{2,1,0:T(8,128)(2,1)S(1)}, bf16[8,128,256]{2,1,0:T(8,128)(2,1)}, u32[]{:S(2)}) copy-start(bf16[8,128,256]{2,1,0:T(8,128)(2,1)} %copy-done.9) | copy-start | bytes 1572868
  152.9 6.8 %copy-start.12 = (bf16[8,128,256]{2,1,0:T(8,128)(2,1)S(1)}, bf16[8,128,256]{2,1,0:T(8,128)(2,1)}, u32[]{:S(2)}) copy-start(bf16[8,128,256]{2,1,0:T(8,128)(2,1)} %copy-done.11) | copy-start | bytes 1572868
  152.9 6.8 %copy-start.14 = (bf16[8,128,256]{2,1,0:T(8,128)(2,1)S(1)}, bf16[8,128,256]{2,1,0:T(8,128)(2,1)}, u32[]{:S(2)}) copy-start(bf16[8,128,256]{2,1,0:T(8,128)(2,1)} %copy-done.13) | copy-start | bytes 1572868
  152.9 6.8 %copy-start.17 = (s32[4]{0:T(128)S(1)}, s32[4]{0:T(128)}, u32[]{:S(2)}) copy-start(s32[4]{0:T(128)} %copy-done.16) | copy-start | bytes 52
  159.8 0.9 copy-start.15
  165.8 16.3 %collective-permute-start.20 = (bf16[128,4096]{1,0:T(8,128)(2,1)S(1)}, bf16[128,4096]{1,0:T(8,128)(2,1)S(1)}, u32[]{:S(2)}, u32[]{:S(2)}) collective-permute-start(bf16[128,4096]{1,0:T(8,128)(2,1)S(1)} %get-tuple-element.63), channel_id=1, source_target_pairs={{0,1},{1,0},{2,3},{3,2},{4,5},{5,4},{6,7},{7,6},{8,9},{9,8},{10,11... | collective-permute-start | bytes 3145736 | tf_op jit(solution)/shard_map/ppermute | solution.py:358
Sparse Core Ops, SparseCore 0:
  9.9 57.6 all-gather.1

commit v2 on v1

--- a/solution.py
+++ b/solution.py
@@ -24,7 +24,7 @@
 PAIR = 2 * BLK
 MEM = ("z", "x")
 MIB = 1024 * 1024
-REST = (XN - 1) * ZN
+HALF = (XN - 1) * ZN // 2
 NEG_FILL = -1e30
 SCALE = 1.0 / math.sqrt(HD)
 FAR = (2, 1, 3)
@@ -62,7 +62,9 @@
 
 
 def project_kernel(pos_ref, x_ref, *refs):
-    own_ref, rest_ref, out_ref = refs
+    own_ref, first_ref, last_ref, out_ref = refs
+    middle = [first_ref[ZN:], last_ref[: ZN // 2]]
+    pieces = [own_ref[...], first_ref[:ZN], jnp.concatenate(middle), last_ref[ZN // 2 :]]
     total = jnp.zeros((PAIR, WIDTH), jnp.float32)
     for x_shift in range(XN):
         x_index = lax.rem(pos_ref[1] + XN - x_shift, XN)
@@ -70,14 +72,13 @@
             [x_ref[:, pl.ds(column_of(pos_ref[0], x_index, shift), BLK)] for shift in range(ZN)],
             axis=1,
         )
-        piece = rest_ref[(x_shift - 1) * ZN : x_shift * ZN] if x_shift else own_ref[...]
-        total += dot(rows, piece.reshape(ZN * BLK, WIDTH), ((1,), (0,)))
+        total += dot(rows, pieces[x_shift].reshape(ZN * BLK, WIDTH), ((1,), (0,)))
     out_ref[...] = total.astype(jnp.bfloat16)
 
 
-def project(position, rows, own, rest):
+def project(position, rows, own, first, last):
     pieces = [
-        pl.BlockSpec((count, BLK, WIDTH), lambda i, pos_ref: (0, 0, 0)) for count in (ZN, REST)
+        pl.BlockSpec((count, BLK, WIDTH), lambda i, pos_ref: (0, 0, 0)) for count in (ZN, HALF, HALF)
     ]
     return pl.pallas_call(
         project_kernel,
@@ -95,7 +96,7 @@
             transcendentals=0,
         ),
         name="project",
-    )(position, rows, own, rest)
+    )(position, rows, own, first, last)
 
 
 def attend_local_kernel(query_ref, local_ref, grad_ref, *out_refs):
@@ -156,7 +157,7 @@
     )(queries, local_kv, grad_out)
 
 
-def attend_memory_kernel(shifts, owner_ref, pos_ref, *refs):
+def attend_memory_kernel(shifts, pos_ref, *refs):
     count, parts = len(shifts), PAIR // BLK
     row_refs, memory_ref, refs = refs[:6], refs[6], refs[7:]
     row_scrs, (held, sems, row_sems), refs = refs[-9:-3], refs[-3:], refs[:-9]
@@ -172,7 +173,7 @@
     ]
     copies = [
         pltpu.make_async_copy(
-            memory_ref.at[owner_ref[group * parts + part, slot]],
+            memory_ref.at[pos_ref[4 + (group * parts + part) * TOPK + slot]],
             held.at[i * parts + part, slot],
             sems.at[i * parts + part, slot],
         )
@@ -249,7 +250,7 @@
                 other_refs[i][rows[u], feats[u]] = attended
 
 
-def attend_memory(shifts, owner_of, position, queries, received, grad_out, prepared, done):
+def attend_memory(shifts, scalars, queries, received, grad_out, prepared, done):
     in_smem, in_vmem = (pl.BlockSpec(memory_space=space) for space in (pltpu.SMEM, pltpu.VMEM))
     count, tiles = len(shifts), len(shifts) * (PAIR // BLK)
     part = jax.ShapeDtypeStruct((PAIR, WIDTH), jnp.bfloat16)
@@ -259,7 +260,7 @@
     keys_count = tiles * TOPK * BLK
     outs = pl.pallas_call(
         functools.partial(attend_memory_kernel, shifts),
-        in_specs=[in_smem] * 2
+        in_specs=[in_smem]
         + [pl.BlockSpec(memory_space=pl.ANY)] * 7
         + [in_vmem] * len(done),
         out_specs=[in_vmem] * len(out_shape),
@@ -278,7 +279,7 @@
             transcendentals=BLK * keys_count * HEADS,
         ),
         name="attend_memory",
-    )(owner_of, position, *operands)
+    )(scalars, *operands)
     return outs[:-count], outs[-count:]
 
 
@@ -287,11 +288,7 @@
     (1, 0, ZN),
     (2, 0, ZN),
     (3, 0, ZN),
-    (0, ZN, REST),
-    (1, ZN, REST),
-    (2, ZN, REST // 2),
-    (2, ZN + REST // 2, REST // 2),
-    (3, ZN, REST),
+    *[(shift, ZN + part * HALF, HALF) for shift in range(YN) for part in range(2)],
 )
 
 
@@ -361,6 +358,7 @@
 def local(layer_input, w_query, local_kv, memory_kv, memory_ids, grad_out):
     position = jnp.stack([lax.axis_index(axis) for axis in ("z", "x", "y", "c")]).astype(jnp.int32)
     owner_of = memory_ids // MB_DEV
+    scalars = jnp.concatenate([position, owner_of.reshape(TILES * TOPK)])
     owners = jnp.arange(OWNERS, dtype=jnp.int32)
     wanted = jnp.max(
         jnp.where(owner_of[:, :, None] == owners, (memory_ids % MB_DEV)[:, :, None], 0),
@@ -372,24 +370,27 @@
     received = lax.all_to_all(pick_blocks(asked[:, 0], memory_kv), MEM, 0, 0, tiled=True)
     own = jnp.stack(weights)
     rows = lax.all_gather(layer_input, ("y", "c"), axis=0, tiled=True)
-    rest = jnp.concatenate([move(own, "x", XN, shift) for shift in range(1, XN)])
+    others = [move(own, "x", XN, shift) for shift in range(1, XN)]
+    first = jnp.concatenate([others[0], others[1][: ZN // 2]])
+    last = jnp.concatenate([others[1][ZN // 2 :], others[2]])
     near_parts = [own, *[move(own, "y", YN, shift) for shift in range(1, YN)]]
-    rest, near_parts = lax.optimization_barrier((rest, near_parts))
-    below, above = move(rest, "y", YN, 1), move(rest, "y", YN, -1)
-    queries = project(position, rows, own, rest)
+    first, last, near_parts = lax.optimization_barrier((first, last, near_parts))
+    below, above = move(first, "y", YN, 1), move(last, "y", YN, -1)
+    below_last, above_first = move(last, "y", YN, 1), move(first, "y", YN, -1)
+    queries = project(scalars, rows, own, first, last)
     *sums, stats = attend_local(queries, local_kv, grad_out)
     below, above, stats = lax.optimization_barrier((below, above, stats))
     prepared = [*sums, stats]
-    far_first = move(below[: REST // 2], "y", YN, 1)
-    far_last = move(above[REST // 2 :], "y", YN, -1)
-    pieces = [*near_parts, rest, below, far_first, far_last, above]
-    done, far = attend_memory(FAR, owner_of, position, queries, received, grad_out, prepared, [])
+    far_first, far_last = move(below, "y", YN, 1), move(above, "y", YN, -1)
+    rest = [first, last, below, below_last, far_first, far_last, above_first, above]
+    pieces = [*near_parts, *rest]
+    done, far = attend_memory(FAR, scalars, queries, received, grad_out, prepared, [])
     far = {shift: move(part, "y", YN, shift) for shift, part in zip(FAR, far)}
     (attended,), (near,) = attend_memory(
-        (0,), owner_of, position, queries, received, grad_out, prepared, done
+        (0,), scalars, queries, received, grad_out, prepared, done
     )
     grads = [near, far[1], far[2], far[3]]
-    own_part, send = back_project(position, grads, pieces)
+    own_part, send = back_project(scalars, grads, pieces)
     other = move(send, "c", CN, 1)
     return (attended, (own_part + other.astype(jnp.float32)).astype(jnp.bfloat16))
 

time: 191 us -> 186 us (0.974)
  local copies, waits for them, and re-layouts: 18.7 us -> 13.9 us
  waiting for transfers between devices: 56.5 us -> 53.2 us
    ppermute x21 -> x23, waiting for transfers between devices: 55.9 us -> 46.7 us  [move(): lax.ppermute(array, axis, [(i, (i + shift) % count) for i in range(count)])]
    all_to_all x1, waiting for transfers between devices: 0.01 us -> 5.8 us  [local(): lax.all_to_all(pick_blocks(asked[:, 0], memory_kv), MEM, 0, 0, tiled=True)]
    slice x2 -> x1, local copies, waits for them, and re-layouts: 4.12 us -> 0.03 us  [local(): last = jnp.concatenate([others[1][ZN // 2:], others[2]])]
    unnamed x50 -> x47, local copies, waits for them, and re-layouts: 14.3 us -> 13.5 us
    ppermute x21 -> x23, starting transfers between devices: 45.2 us -> 45.8 us  [move(): lax.ppermute(array, axis, [(i, (i + shift) % count) for i in range(count)])]
  transfers between devices with their start and end apart: 23 -> 25, of which waited for: 7 -> 5; matrix products, arithmetic and copies ran while one was open for 3% -> 1% of each run, Pallas kernels for 13% -> 14%
where the time goes in v2:
time: 186 us; the launch traced here: 183 us
  starting transfers between devices  55.5 us (30%)
  waiting for transfers between devices  53.2 us (29%)
  Pallas kernels  30.6 us (16%)
  between operations  14.4 us (8%)
  local copies, waits for them, and re-layouts  13.9 us (7%)
  blocking collectives  12.9 us (7%)
  other arithmetic  2.76 us (1%)
    ppermute x23, waiting for transfers between devices, move(): lax.ppermute(array, axis, [(i, (i + shift) % count) for i in range(count)])  46.7 us
    ppermute x23, starting transfers between devices, move(): lax.ppermute(array, axis, [(i, (i + shift) % count) for i in range(count)])  45.8 us
    pallas_call x2, Pallas kernels, attend_memory(): pl.pallas_call(functools.partial(attend_memory_kernel, shifts), in_specs=...  15.4 us
    unnamed x47, local copies, waits for them, and re-layouts  13.5 us
    all_to_all x1, blocking collectives, local(): asked = lax.all_to_all(wanted.reshape(OWNERS, 1), MEM, 0, 0, tiled=True)  12.9 us
    all_to_all x1, starting transfers between devices, local(): lax.all_to_all(pick_blocks(asked[:, 0], memory_kv), MEM, 0, 0, tiled=True)  9.68 us
    all_to_all x1, waiting for transfers between devices, local(): lax.all_to_all(pick_blocks(asked[:, 0], memory_kv), MEM, 0, 0, tiled=True)  5.8 us
    pallas_call x1, Pallas kernels, back_project(): pl.pallas_call(back_kernel, in_specs=[pl.BlockSpec(memory_space=pltpu.SME...  5.15 us
  transfers between devices with their start and end apart: 25, of which 5 were waited for; matrix products, arithmetic and copies ran while one was open for 1% of the time, Pallas kernels for 14%

profile of v2, /device:TPU:129, one launch (start us, length us, event | category | flops | bytes accessed | tf_op | source)
XLA Modules:
  0.0 183.2 jit_solution(2361178086135364495)
XLA Ops:
  7.2 0.0 all-gather.2.cloned.1.call-start
  7.2 0.7 all-gather.2.cloned.1.call-update
  7.9 0.8 collective-permute-start
  8.7 1.2 collective-permute-start.1
  9.9 4.9 %collective-permute-start.3 = (bf16[128,256]{1,0:T(8,128)(2,1)}, bf16[128,256]{1,0:T(8,128)(2,1)S(1)}, u32[]{:S(2)}, u32[]{:S(2)}) collective-permute-start(bf16[128,256]{1,0:T(8,128)(2,1)} %param.7), channel_id=1, source_target_pairs={{0,128},{32,160},{64,192},{96,224},{128,0},{160,32},{192,64},{224,... | collective-permute-start | bytes 196616 | tf_op jit(solution)/shard_map/ppermute | solution.py:355
  14.8 0.7 collective-permute-start.4
  15.5 0.7 add_select_fusion
  16.2 2.2 %collective-permute-start.5 = (bf16[128,256]{1,0:T(8,128)(2,1)}, bf16[128,256]{1,0:T(8,128)(2,1)S(1)}, u32[]{:S(2)}, u32[]{:S(2)}) collective-permute-start(bf16[128,256]{1,0:T(8,128)(2,1)} %param.7), channel_id=1, source_target_pairs={{0,192},{32,224},{64,0},{96,32},{128,64},{160,96},{192,128},{224,1... | collective-permute-start | bytes 196616 | tf_op jit(solution)/shard_map/ppermute | solution.py:355
  18.4 0.0 collective-permute-done.1
  18.5 1.3 collective-permute-start.6
  19.7 0.1 select_reduce_fusion
  19.8 0.1 copy.23
  19.9 12.9 %all_to_all.17 = s32[32,1,1]{2,1,0:T(1,128)S(1)} all-to-all(s32[32,1,1]{2,1,0:T(1,128)S(1)} %copy.23), channel_id=1, replica_groups=mesh['z'=8,'x'=4,'y'=4,'c'=2] {'z','x'}, dimensions={0} | all-to-all | bytes 256 | tf_op jit(solution)/shard_map/all_to_all | solution.py:368
  32.9 0.7 reduce
  33.5 0.0 collective-permute-done.3
  33.5 0.0 collective-permute-done.5
  33.6 0.0 collective-permute-done.6
  33.6 0.0 copy-start.3
  33.6 1.6 copy-done.3
  35.2 1.3 pick_blocks.1
  36.4 1.9 %copy-done = bf16[32,2,128,256]{3,2,1,0:T(8,128)(2,1)} copy-done((bf16[32,2,128,256]{3,2,1,0:T(8,128)(2,1)}, bf16[32,2,128,256]{3,2,1,0:T(8,128)(2,1)S(1)}, u32[]{:S(2)}) %copy-start) | copy-done | bytes 4194328
  38.4 9.7 %all-to-all-start.1 = ((bf16[32,2,128,256]{3,2,1,0:T(8,128)(2,1)}), bf16[32,2,128,256]{3,2,1,0:T(8,128)(2,1)}, u32[]{:S(2)}, u32[]{:S(2)}) async-start(bf16[32,2,128,256]{3,2,1,0:T(8,128)(2,1)} %copy-done), calls=%async_computation.1 | async-start | bytes 8388608 | tf_op jit(solution)/shard_map/all_to_all | solution.py:370
  48.2 2.8 %collective-permute-start.8 = (bf16[8,128,256]{2,1,0:T(8,128)(2,1)S(1)}, bf16[8,128,256]{2,1,0:T(8,128)(2,1)S(1)}, u32[]{:S(2)}, u32[]{:S(2)}) collective-permute-start(bf16[8,128,256]{2,1,0:T(8,128)(2,1)S(1)} %bitcast_dynamic-update-slice_fusion.refs_0_.refs_4_), channel_id=1, source_target_pairs={{0,16},{8,24},{16,0},{24,8},{1,17},{9,25},{17,1},{25,9},{2,18},{10... | collective-permute-start | bytes 1572872 | tf_op jit(solution)/shard_map/ppermute | solution.py:355
  51.0 0.9 collective-permute-start.9
  51.9 0.6 collective-permute-start.7
  52.4 1.3 collective-permute-start.10
  53.7 2.6 %collective-permute-start.11 = (bf16[8,128,256]{2,1,0:T(8,128)(2,1)S(1)}, bf16[8,128,256]{2,1,0:T(8,128)(2,1)S(1)}, u32[]{:S(2)}, u32[]{:S(2)}) collective-permute-start(bf16[8,128,256]{2,1,0:T(8,128)(2,1)S(1)} %bitcast_dynamic-update-slice_fusion.refs_0_.refs_4_), channel_id=1, source_target_pairs={{0,4},{2,6},{4,0},{6,2},{1,5},{3,7},{5,1},{7,3},{8,12},{10,14},{12... | collective-permute-start | bytes 1572872 | tf_op jit(solution)/shard_map/ppermute | solution.py:355
  56.3 29.5 %collective-permute-done.8 = bf16[8,128,256]{2,1,0:T(8,128)(2,1)S(1)} collective-permute-done((bf16[8,128,256]{2,1,0:T(8,128)(2,1)S(1)}, bf16[8,128,256]{2,1,0:T(8,128)(2,1)S(1)}, u32[]{:S(2)}, u32[]{:S(2)}) %collective-permute-start.8) | collective-permute-done | bytes 524320 | tf_op jit(solution)/shard_map/ppermute | solution.py:355
  85.8 2.7 %collective-permute-start.12 = (bf16[8,128,256]{2,1,0:T(8,128)(2,1)S(1)}, bf16[8,128,256]{2,1,0:T(8,128)(2,1)S(1)}, u32[]{:S(2)}, u32[]{:S(2)}) collective-permute-start(bf16[8,128,256]{2,1,0:T(8,128)(2,1)S(1)} %bitcast_dynamic-update-slice_fusion.refs_0_.refs_4_), channel_id=1, source_target_pairs={{0,6},{2,0},{4,2},{6,4},{1,7},{3,1},{5,3},{7,5},{8,14},{10,8},{12,... | collective-permute-start | bytes 1572872 | tf_op jit(solution)/shard_map/ppermute | solution.py:355
  88.5 13.8 %collective-permute-done.9 = bf16[8,128,256]{2,1,0:T(8,128)(2,1)S(1)} collective-permute-done((bf16[8,128,256]{2,1,0:T(8,128)(2,1)S(1)}, bf16[8,128,256]{2,1,0:T(8,128)(2,1)S(1)}, u32[]{:S(2)}, u32[]{:S(2)}) %collective-permute-start.9) | collective-permute-done | bytes 524320 | tf_op jit(solution)/shard_map/ppermute | solution.py:355
  102.4 0.1 pad_maximum_fusion.1.refs_2_.refs_9_
  102.4 0.1 pad_maximum_fusion.refs_1_.refs_8_
  102.5 0.0 collective-permute-done.10.refs_5_
  102.5 0.8 copy-done.9
  103.4 0.8 copy-done.11
  104.2 0.8 copy-done.13
  105.0 1.4 collective-permute-start.13
  106.4 1.4 collective-permute-start.14
  107.7 0.1 copy.22
  107.8 0.1 reshape.13
  107.9 0.1 concatenate.9.pos_ref
  108.0 0.1 collective-permute-start.18
  108.1 2.6 %collective-permute-start.21 = (bf16[12,128,256]{2,1,0:T(8,128)(2,1)S(1)}, bf16[12,128,256]{2,1,0:T(8,128)(2,1)}, u32[]{:S(2)}, u32[]{:S(2)}) collective-permute-start(bf16[12,128,256]{2,1,0:T(8,128)(2,1)S(1)} %pad_maximum_fusion.refs_1_.refs_8_), channel_id=1, source_target_pairs={{0,6},{2,0},{4,2},{6,4},{1,7},{3,1},{5,3},{7,5},{8,14},{10,8},{12,... | collective-permute-start | bytes 2359304 | tf_op jit(solution)/shard_map/ppermute | solution.py:355
  110.7 3.4 %copy-done.1 = bf16[1024,4096]{1,0:T(8,128)(2,1)S(1)} copy-done((bf16[1024,4096]{1,0:T(8,128)(2,1)S(1)}, bf16[1024,4096]{1,0:T(8,128)(2,1)}, u32[]{:S(2)}) %copy-start.1) | copy-done | bytes 8388632
  114.1 3.8 %project.1.query_ref.refs_0_ = bf16[1024,256]{1,0:T(8,128)(2,1)S(1)} custom-call(s32[36]{0:T(128)S(1)} %concatenate.9.pos_ref, bf16[1024,4096]{1,0:T(8,128)(2,1)S(1)} %copy-done.1, bf16[8,128,256]{2,1,0:T(8,128)(2,1)S(1)} %bitcast_dynamic-update-slice_fusion.refs_0_.refs_4_, bf16[12,128,256]{2,1,0:T(8,128)(2,1)S(1)} %pad_maximum_fusion.refs_1_.refs_8_, ...), custom_call_target="tpu_custom_call" | custom-call | flops 2147483648 | bytes 11010048 | tf_op jit(solution)/shard_map/project/pallas_call | solution.py:83
  117.9 0.0 copy-start.2
  117.9 5.0 %attend_local.1 = (bf16[1024,256]{1,0:T(8,128)(2,1)S(1)}, bf16[1024,256]{1,0:T(8,128)(2,1)S(1)}, bf16[1024,256]{1,0:T(8,128)(2,1)S(1)}, f32[1024,128]{1,0:T(8,128)S(1)}) custom-call(bf16[1024,256]{1,0:T(8,128)(2,1)S(1)} %project.1.query_ref.refs_0_, bf16[2,1024,256]{2,1,0:T(8,128)(2,1)S(1)} %copy-done.18, bf16[1024,256]{1,0:T(8,128)(2,1)S(1)} %copy-done.4), custom_call_target="tpu_custom_call" | custom-call | flops 1509949440 | bytes 6291456 | tf_op jit(solution)/shard_map/attend_local/pallas_call | solution.py:144
  122.9 0.8 copy-done.5
  123.7 0.8 copy-done.6
  124.5 0.8 copy-done.7
  125.3 0.8 copy-done.8
  126.1 2.7 %collective-permute-start.20 = (bf16[12,128,256]{2,1,0:T(8,128)(2,1)}, bf16[12,128,256]{2,1,0:T(8,128)(2,1)}, u32[]{:S(2)}, u32[]{:S(2)}) collective-permute-start(bf16[12,128,256]{2,1,0:T(8,128)(2,1)} %collective-permute-done.14.refs_15_), channel_id=1, source_target_pairs={{0,6},{2,0},{4,2},{6,4},{1,7},{3,1},{5,3},{7,5},{8,14},{10,8},{12,... | collective-permute-start | bytes 2359304 | tf_op jit(solution)/shard_map/ppermute | solution.py:355
  128.8 5.8 %all-to-all-done.1.refs_6_ = bf16[32,2,128,256]{3,2,1,0:T(8,128)(2,1)} async-done(((bf16[32,2,128,256]{3,2,1,0:T(8,128)(2,1)}), bf16[32,2,128,256]{3,2,1,0:T(8,128)(2,1)}, u32[]{:S(2)}, u32[]{:S(2)}) %all-to-all-start.1) | async-done | bytes 4194336 | tf_op jit(solution)/shard_map/all_to_all | solution.py:370
  134.6 9.6 %attend_memory.2 = (bf16[256,256]{1,0:T(8,128)(2,1)}, bf16[256,256]{1,0:T(8,128)(2,1)}, bf16[256,256]{1,0:T(8,128)(2,1)}, bf16[256,256]{1,0:T(8,128)(2,1)}, bf16...) custom-call(s32[36]{0:T(128)} %copy-done.16, bf16[1024,256]{1,0:T(8,128)(2,1)} %copy-done.2, bf16[1024,256]{1,0:T(8,128)(2,1)} %refs_1_.3, ...), custom_call_target="tpu_custom_call" | custom-call | flops 805306368 | bytes 6291456 | tf_op jit(solution)/shard_map/attend_memory/pallas_call | solution.py:261
  144.3 1.3 collective-permute-start.15
  145.6 2.6 %collective-permute-start.16 = (bf16[256,256]{1,0:T(8,128)(2,1)}, bf16[256,256]{1,0:T(8,128)(2,1)S(1)}, u32[]{:S(2)}, u32[]{:S(2)}) collective-permute-start(bf16[256,256]{1,0:T(8,128)(2,1)} %get-tuple-element.56), channel_id=1, source_target_pairs={{0,4},{2,6},{4,0},{6,2},{1,5},{3,7},{5,1},{7,3},{8,12},{10,14},{12... | collective-permute-start | bytes 393224 | tf_op jit(solution)/shard_map/ppermute | solution.py:355
  148.2 1.1 collective-permute-start.17
  149.4 5.7 %attend_memory.3 = (bf16[1024,256]{1,0:T(8,128)(2,1)}, bf16[256,256]{1,0:T(8,128)(2,1)}) custom-call(s32[36]{0:T(128)} %copy-done.16, bf16[1024,256]{1,0:T(8,128)(2,1)} %copy-done.2, bf16[1024,256]{1,0:T(8,128)(2,1)} %refs_1_.3, bf16[1024,256]{1,0:T(8,128)(2,1)} %copy-done.5, bf16[1024,256]{1,0:T(8,128)(2,1)} %copy-done.6, bf16[1024,256]{1,0:T(8,128)(2,1)} %copy-done.7, ...), custom_call_target="tpu_custom_call" | custom-call | flops 268435456 | bytes 6291456 | tf_op jit(solution)/shard_map/attend_memory/pallas_call | solution.py:261
  155.1 1.1 collective-permute-done.16.refs_2_
  156.2 0.9 copy-done.15
  157.1 5.1 %back_project.1 = (f32[128,4096]{1,0:T(8,128)S(1)}, bf16[128,4096]{1,0:T(8,128)(2,1)S(1)}) custom-call(s32[36]{0:T(128)S(1)} %copy-done.17, bf16[256,256]{1,0:T(8,128)(2,1)S(1)} %copy-done.15, bf16[256,256]{1,0:T(8,128)(2,1)S(1)} %collective-permute-done.15.refs_1_, bf16[256,256]{1,0:T(8,128)(2,1)S(1)} %collective-permute-done.16.refs_2_, ...), custom_call_target="tpu_custom_call" | custom-call | flops 2147483648 | bytes 12582912 | tf_op jit(solution)/shard_map/back_project/pallas_call | solution.py:327
  162.3 10.7 %collective-permute-start.22 = (bf16[128,4096]{1,0:T(8,128)(2,1)S(1)}, bf16[128,4096]{1,0:T(8,128)(2,1)S(1)}, u32[]{:S(2)}, u32[]{:S(2)}) collective-permute-start(bf16[128,4096]{1,0:T(8,128)(2,1)S(1)} %get-tuple-element.65), channel_id=1, source_target_pairs={{0,1},{1,0},{2,3},{3,2},{4,5},{5,4},{6,7},{7,6},{8,9},{9,8},{10,11... | collective-permute-start | bytes 3145736 | tf_op jit(solution)/shard_map/ppermute | solution.py:355
  172.9 2.3 %collective-permute-done.22 = bf16[128,4096]{1,0:T(8,128)(2,1)S(1)} collective-permute-done((bf16[128,4096]{1,0:T(8,128)(2,1)S(1)}, bf16[128,4096]{1,0:T(8,128)(2,1)S(1)}, u32[]{:S(2)}, u32[]{:S(2)}) %collective-permute-start.22) | collective-permute-done | bytes 1048608 | tf_op jit(solution)/shard_map/ppermute | solution.py:355
  175.2 1.2 add_convert_fusion
  (53 shorter events, 0.2 us)
Async XLA Ops:
  7.2 103.5 %all-gather.2.cloned.1.call-start = ((), (), s32[]{:S(2)}) async-start(), calls=%async_computation.2 | async-start | bytes 9437184 | tf_op jit(solution)/shard_map/all_gather | solution.py:372
  7.9 8.3 %collective-permute-start = (bf16[128,256]{1,0:T(8,128)(2,1)}, bf16[128,256]{1,0:T(8,128)(2,1)S(1)}, u32[]{:S(2)}, u32[]{:S(2)}) collective-permute-start(bf16[128,256]{1,0:T(8,128)(2,1)} %param.7), channel_id=1, source_target_pairs={{0,32},{32,64},{64,96},{96,128},{128,160},{160,192},{192,224},{224... | collective-permute-start | bytes 196616 | tf_op jit(solution)/shard_map/ppermute | solution.py:355
  8.7 9.7 %collective-permute-start.1 = (bf16[128,256]{1,0:T(8,128)(2,1)}, bf16[128,256]{1,0:T(8,128)(2,1)S(1)}, u32[]{:S(2)}, u32[]{:S(2)}) collective-permute-start(bf16[128,256]{1,0:T(8,128)(2,1)} %param.7), channel_id=1, source_target_pairs={{0,64},{32,96},{64,128},{96,160},{128,192},{160,224},{192,0},{224,... | collective-permute-start | bytes 196616 | tf_op jit(solution)/shard_map/ppermute | solution.py:355
  9.9 23.6 %collective-permute-start.2 = (bf16[128,256]{1,0:T(8,128)(2,1)}, bf16[128,256]{1,0:T(8,128)(2,1)S(1)}, u32[]{:S(2)}, u32[]{:S(2)}) collective-permute-start(bf16[128,256]{1,0:T(8,128)(2,1)} %param.7), channel_id=1, source_target_pairs={{0,96},{32,128},{64,160},{96,192},{128,224},{160,0},{192,32},{224,... | collective-permute-start | bytes 196616 | tf_op jit(solution)/shard_map/ppermute | solution.py:355
  9.9 23.6 %collective-permute-start.3 = (bf16[128,256]{1,0:T(8,128)(2,1)}, bf16[128,256]{1,0:T(8,128)(2,1)S(1)}, u32[]{:S(2)}, u32[]{:S(2)}) collective-permute-start(bf16[128,256]{1,0:T(8,128)(2,1)} %param.7), channel_id=1, source_target_pairs={{0,128},{32,160},{64,192},{96,224},{128,0},{160,32},{192,64},{224,... | collective-permute-start | bytes 196616 | tf_op jit(solution)/shard_map/ppermute | solution.py:355
  14.8 18.7 %collective-permute-start.4 = (bf16[128,256]{1,0:T(8,128)(2,1)}, bf16[128,256]{1,0:T(8,128)(2,1)S(1)}, u32[]{:S(2)}, u32[]{:S(2)}) collective-permute-start(bf16[128,256]{1,0:T(8,128)(2,1)} %param.7), channel_id=1, source_target_pairs={{0,160},{32,192},{64,224},{96,0},{128,32},{160,64},{192,96},{224,1... | collective-permute-start | bytes 196616 | tf_op jit(solution)/shard_map/ppermute | solution.py:355
  16.2 17.3 %collective-permute-start.5 = (bf16[128,256]{1,0:T(8,128)(2,1)}, bf16[128,256]{1,0:T(8,128)(2,1)S(1)}, u32[]{:S(2)}, u32[]{:S(2)}) collective-permute-start(bf16[128,256]{1,0:T(8,128)(2,1)} %param.7), channel_id=1, source_target_pairs={{0,192},{32,224},{64,0},{96,32},{128,64},{160,96},{192,128},{224,1... | collective-permute-start | bytes 196616 | tf_op jit(solution)/shard_map/ppermute | solution.py:355
  18.5 15.1 %collective-permute-start.6 = (bf16[128,256]{1,0:T(8,128)(2,1)}, bf16[128,256]{1,0:T(8,128)(2,1)S(1)}, u32[]{:S(2)}, u32[]{:S(2)}) collective-permute-start(bf16[128,256]{1,0:T(8,128)(2,1)} %param.7), channel_id=1, source_target_pairs={{0,224},{32,0},{64,32},{96,64},{128,96},{160,128},{192,160},{224,1... | collective-permute-start | bytes 196616 | tf_op jit(solution)/shard_map/ppermute | solution.py:355
  33.6 1.6 copy-start.3
  36.4 1.9 %copy-start = (bf16[32,2,128,256]{3,2,1,0:T(8,128)(2,1)}, bf16[32,2,128,256]{3,2,1,0:T(8,128)(2,1)S(1)}, u32[]{:S(2)}) copy-start(bf16[32,2,128,256]{3,2,1,0:T(8,128)(2,1)S(1)} %pick_blocks.1) | copy-start | bytes 12582916
  38.4 9.7 %copy-start.19 = (bf16[128,256]{1,0:T(8,128)(2,1)S(1)}, bf16[128,256]{1,0:T(8,128)(2,1)}, u32[]{:S(2)}) copy-start(bf16[128,256]{1,0:T(8,128)(2,1)} %param.7) | copy-start | bytes 196612
  38.4 96.3 %all-to-all-start.1 = ((bf16[32,2,128,256]{3,2,1,0:T(8,128)(2,1)}), bf16[32,2,128,256]{3,2,1,0:T(8,128)(2,1)}, u32[]{:S(2)}, u32[]{:S(2)}) async-start(bf16[32,2,128,256]{3,2,1,0:T(8,128)(2,1)} %copy-done), calls=%async_computation.1 | async-start | bytes 8388608 | tf_op jit(solution)/shard_map/all_to_all | solution.py:370
  48.2 37.6 %collective-permute-start.8 = (bf16[8,128,256]{2,1,0:T(8,128)(2,1)S(1)}, bf16[8,128,256]{2,1,0:T(8,128)(2,1)S(1)}, u32[]{:S(2)}, u32[]{:S(2)}) collective-permute-start(bf16[8,128,256]{2,1,0:T(8,128)(2,1)S(1)} %bitcast_dynamic-update-slice_fusion.refs_0_.refs_4_), channel_id=1, source_target_pairs={{0,16},{8,24},{16,0},{24,8},{1,17},{9,25},{17,1},{25,9},{2,18},{10... | collective-permute-start | bytes 1572872 | tf_op jit(solution)/shard_map/ppermute | solution.py:355
  51.0 51.4 %collective-permute-start.9 = (bf16[8,128,256]{2,1,0:T(8,128)(2,1)S(1)}, bf16[8,128,256]{2,1,0:T(8,128)(2,1)S(1)}, u32[]{:S(2)}, u32[]{:S(2)}) collective-permute-start(bf16[8,128,256]{2,1,0:T(8,128)(2,1)S(1)} %bitcast_dynamic-update-slice_fusion.refs_0_.refs_4_), channel_id=1, source_target_pairs={{0,24},{8,0},{16,8},{24,16},{1,25},{9,1},{17,9},{25,17},{2,26},{10... | collective-permute-start | bytes 1572872 | tf_op jit(solution)/shard_map/ppermute | solution.py:355
  51.9 50.6 %collective-permute-start.7 = (bf16[8,128,256]{2,1,0:T(8,128)(2,1)S(1)}, bf16[8,128,256]{2,1,0:T(8,128)(2,1)S(1)}, u32[]{:S(2)}, u32[]{:S(2)}) collective-permute-start(bf16[8,128,256]{2,1,0:T(8,128)(2,1)S(1)} %bitcast_dynamic-update-slice_fusion.refs_0_.refs_4_), channel_id=1, source_target_pairs={{0,8},{8,16},{16,24},{24,0},{1,9},{9,17},{17,25},{25,1},{2,10},{10... | collective-permute-start | bytes 1572872 | tf_op jit(solution)/shard_map/ppermute | solution.py:355
  52.4 50.1 %collective-permute-start.10 = (bf16[8,128,256]{2,1,0:T(8,128)(2,1)S(1)}, bf16[8,128,256]{2,1,0:T(8,128)(2,1)S(1)}, u32[]{:S(2)}, u32[]{:S(2)}) collective-permute-start(bf16[8,128,256]{2,1,0:T(8,128)(2,1)S(1)} %bitcast_dynamic-update-slice_fusion.refs_0_.refs_4_), channel_id=1, source_target_pairs={{0,2},{2,4},{4,6},{6,0},{1,3},{3,5},{5,7},{7,1},{8,10},{10,12},{12... | collective-permute-start | bytes 1572872 | tf_op jit(solution)/shard_map/ppermute | solution.py:355
  53.7 49.6 %collective-permute-start.11 = (bf16[8,128,256]{2,1,0:T(8,128)(2,1)S(1)}, bf16[8,128,256]{2,1,0:T(8,128)(2,1)S(1)}, u32[]{:S(2)}, u32[]{:S(2)}) collective-permute-start(bf16[8,128,256]{2,1,0:T(8,128)(2,1)S(1)} %bitcast_dynamic-update-slice_fusion.refs_0_.refs_4_), channel_id=1, source_target_pairs={{0,4},{2,6},{4,0},{6,2},{1,5},{3,7},{5,1},{7,3},{8,12},{10,14},{12... | collective-permute-start | bytes 1572872 | tf_op jit(solution)/shard_map/ppermute | solution.py:355
  85.8 18.3 %collective-permute-start.12 = (bf16[8,128,256]{2,1,0:T(8,128)(2,1)S(1)}, bf16[8,128,256]{2,1,0:T(8,128)(2,1)S(1)}, u32[]{:S(2)}, u32[]{:S(2)}) collective-permute-start(bf16[8,128,256]{2,1,0:T(8,128)(2,1)S(1)} %bitcast_dynamic-update-slice_fusion.refs_0_.refs_4_), channel_id=1, source_target_pairs={{0,6},{2,0},{4,2},{6,4},{1,7},{3,1},{5,3},{7,5},{8,14},{10,8},{12,... | collective-permute-start | bytes 1572872 | tf_op jit(solution)/shard_map/ppermute | solution.py:355
  102.5 0.8 copy-start.9
  103.4 0.8 copy-start.11
  104.2 0.8 copy-start.13
  105.0 21.2 %collective-permute-start.13 = (bf16[12,128,256]{2,1,0:T(8,128)(2,1)S(1)}, bf16[12,128,256]{2,1,0:T(8,128)(2,1)}, u32[]{:S(2)}, u32[]{:S(2)}) collective-permute-start(bf16[12,128,256]{2,1,0:T(8,128)(2,1)S(1)} %pad_maximum_fusion.refs_1_.refs_8_), channel_id=1, source_target_pairs={{0,2},{2,4},{4,6},{6,0},{1,3},{3,5},{5,7},{7,1},{8,10},{10,12},{12... | collective-permute-start | bytes 2359304 | tf_op jit(solution)/shard_map/ppermute | solution.py:355
  106.4 19.8 %collective-permute-start.14 = (bf16[12,128,256]{2,1,0:T(8,128)(2,1)S(1)}, bf16[12,128,256]{2,1,0:T(8,128)(2,1)}, u32[]{:S(2)}, u32[]{:S(2)}) collective-permute-start(bf16[12,128,256]{2,1,0:T(8,128)(2,1)S(1)} %pad_maximum_fusion.1.refs_2_.refs_9_), channel_id=1, source_target_pairs={{0,6},{2,0},{4,2},{6,4},{1,7},{3,1},{5,3},{7,5},{8,14},{10,8},{12,... | collective-permute-start | bytes 2359304 | tf_op jit(solution)/shard_map/ppermute | solution.py:355
  108.0 9.9 %copy-start.16 = (s32[36]{0:T(128)}, s32[36]{0:T(128)S(1)}, u32[]{:S(2)}) copy-start(s32[36]{0:T(128)S(1)} %concatenate.9.pos_ref) | copy-start | bytes 436
  108.0 37.6 %collective-permute-start.18 = (bf16[12,128,256]{2,1,0:T(8,128)(2,1)S(1)}, bf16[12,128,256]{2,1,0:T(8,128)(2,1)}, u32[]{:S(2)}, u32[]{:S(2)}) collective-permute-start(bf16[12,128,256]{2,1,0:T(8,128)(2,1)S(1)} %pad_maximum_fusion.1.refs_2_.refs_9_), channel_id=1, source_target_pairs={{0,2},{2,4},{4,6},{6,0},{1,3},{3,5},{5,7},{7,1},{8,10},{10,12},{12... | collective-permute-start | bytes 2359304 | tf_op jit(solution)/shard_map/ppermute | solution.py:355
  108.1 40.1 %collective-permute-start.21 = (bf16[12,128,256]{2,1,0:T(8,128)(2,1)S(1)}, bf16[12,128,256]{2,1,0:T(8,128)(2,1)}, u32[]{:S(2)}, u32[]{:S(2)}) collective-permute-start(bf16[12,128,256]{2,1,0:T(8,128)(2,1)S(1)} %pad_maximum_fusion.refs_1_.refs_8_), channel_id=1, source_target_pairs={{0,6},{2,0},{4,2},{6,4},{1,7},{3,1},{5,3},{7,5},{8,14},{10,8},{12,... | collective-permute-start | bytes 2359304 | tf_op jit(solution)/shard_map/ppermute | solution.py:355
  110.7 3.4 %copy-start.1 = (bf16[1024,4096]{1,0:T(8,128)(2,1)S(1)}, bf16[1024,4096]{1,0:T(8,128)(2,1)}, u32[]{:S(2)}) copy-start(bf16[1024,4096]{1,0:T(8,128)(2,1)} %all-gather.2.cloned.1.call-done.x_ref) | copy-start | bytes 25165828
  114.1 3.8 %copy-start.4 = (bf16[1024,256]{1,0:T(8,128)(2,1)S(1)}, bf16[1024,256]{1,0:T(8,128)(2,1)}, u32[]{:S(2)}) copy-start(bf16[1024,256]{1,0:T(8,128)(2,1)} %refs_1_.3) | copy-start | bytes 1572868
  114.1 3.8 %copy-start.18 = (bf16[2,1024,256]{2,1,0:T(8,128)(2,1)S(1)}, bf16[2,1024,256]{2,1,0:T(8,128)(2,1)}, u32[]{:S(2)}) copy-start(bf16[2,1024,256]{2,1,0:T(8,128)(2,1)} %local_ref.1) | copy-start | bytes 3145732
  117.9 5.0 %copy-start.2 = (bf16[1024,256]{1,0:T(8,128)(2,1)}, bf16[1024,256]{1,0:T(8,128)(2,1)S(1)}, u32[]{:S(2)}) copy-start(bf16[1024,256]{1,0:T(8,128)(2,1)S(1)} %project.1.query_ref.refs_0_) | copy-start | bytes 1572868
  122.9 0.8 copy-start.5
  123.7 0.8 copy-start.6
  124.5 0.8 copy-start.7
  125.3 0.8 copy-start.8
  126.1 30.0 %collective-permute-start.19 = (bf16[12,128,256]{2,1,0:T(8,128)(2,1)}, bf16[12,128,256]{2,1,0:T(8,128)(2,1)S(1)}, u32[]{:S(2)}, u32[]{:S(2)}) collective-permute-start(bf16[12,128,256]{2,1,0:T(8,128)(2,1)} %collective-permute-done.13.refs_10_), channel_id=1, source_target_pairs={{0,2},{2,4},{4,6},{6,0},{1,3},{3,5},{5,7},{7,1},{8,10},{10,12},{12... | collective-permute-start | bytes 2359304 | tf_op jit(solution)/shard_map/ppermute | solution.py:355
  126.1 30.0 %collective-permute-start.20 = (bf16[12,128,256]{2,1,0:T(8,128)(2,1)}, bf16[12,128,256]{2,1,0:T(8,128)(2,1)}, u32[]{:S(2)}, u32[]{:S(2)}) collective-permute-start(bf16[12,128,256]{2,1,0:T(8,128)(2,1)} %collective-permute-done.14.refs_15_), channel_id=1, source_target_pairs={{0,6},{2,0},{4,2},{6,4},{1,7},{3,1},{5,3},{7,5},{8,14},{10,8},{12,... | collective-permute-start | bytes 2359304 | tf_op jit(solution)/shard_map/ppermute | solution.py:355
  144.3 10.8 %collective-permute-start.15 = (bf16[256,256]{1,0:T(8,128)(2,1)}, bf16[256,256]{1,0:T(8,128)(2,1)S(1)}, u32[]{:S(2)}, u32[]{:S(2)}) collective-permute-start(bf16[256,256]{1,0:T(8,128)(2,1)} %get-tuple-element.55), channel_id=1, source_target_pairs={{0,2},{2,4},{4,6},{6,0},{1,3},{3,5},{5,7},{7,1},{8,10},{10,12},{12... | collective-permute-start | bytes 393224 | tf_op jit(solution)/shard_map/ppermute | solution.py:355
  145.6 10.6 %collective-permute-start.16 = (bf16[256,256]{1,0:T(8,128)(2,1)}, bf16[256,256]{1,0:T(8,128)(2,1)S(1)}, u32[]{:S(2)}, u32[]{:S(2)}) collective-permute-start(bf16[256,256]{1,0:T(8,128)(2,1)} %get-tuple-element.56), channel_id=1, source_target_pairs={{0,4},{2,6},{4,0},{6,2},{1,5},{3,7},{5,1},{7,3},{8,12},{10,14},{12... | collective-permute-start | bytes 393224 | tf_op jit(solution)/shard_map/ppermute | solution.py:355
  148.2 7.9 %collective-permute-start.17 = (bf16[256,256]{1,0:T(8,128)(2,1)}, bf16[256,256]{1,0:T(8,128)(2,1)S(1)}, u32[]{:S(2)}, u32[]{:S(2)}) collective-permute-start(bf16[256,256]{1,0:T(8,128)(2,1)} %get-tuple-element.57), channel_id=1, source_target_pairs={{0,6},{2,0},{4,2},{6,4},{1,7},{3,1},{5,3},{7,5},{8,14},{10,8},{12,... | collective-permute-start | bytes 393224 | tf_op jit(solution)/shard_map/ppermute | solution.py:355
  149.3 6.8 %copy-start.10 = (bf16[8,128,256]{2,1,0:T(8,128)(2,1)S(1)}, bf16[8,128,256]{2,1,0:T(8,128)(2,1)}, u32[]{:S(2)}) copy-start(bf16[8,128,256]{2,1,0:T(8,128)(2,1)} %copy-done.9) | copy-start | bytes 1572868
  149.4 6.8 %copy-start.12 = (bf16[8,128,256]{2,1,0:T(8,128)(2,1)S(1)}, bf16[8,128,256]{2,1,0:T(8,128)(2,1)}, u32[]{:S(2)}) copy-start(bf16[8,128,256]{2,1,0:T(8,128)(2,1)} %copy-done.11) | copy-start | bytes 1572868
  149.4 6.8 %copy-start.14 = (bf16[8,128,256]{2,1,0:T(8,128)(2,1)S(1)}, bf16[8,128,256]{2,1,0:T(8,128)(2,1)}, u32[]{:S(2)}) copy-start(bf16[8,128,256]{2,1,0:T(8,128)(2,1)} %copy-done.13) | copy-start | bytes 1572868
  149.4 6.9 %copy-start.17 = (s32[36]{0:T(128)S(1)}, s32[36]{0:T(128)}, u32[]{:S(2)}) copy-start(s32[36]{0:T(128)} %copy-done.16) | copy-start | bytes 436
  156.2 0.9 copy-start.15
  162.3 12.9 %collective-permute-start.22 = (bf16[128,4096]{1,0:T(8,128)(2,1)S(1)}, bf16[128,4096]{1,0:T(8,128)(2,1)S(1)}, u32[]{:S(2)}, u32[]{:S(2)}) collective-permute-start(bf16[128,4096]{1,0:T(8,128)(2,1)S(1)} %get-tuple-element.65), channel_id=1, source_target_pairs={{0,1},{1,0},{2,3},{3,2},{4,5},{5,4},{6,7},{7,6},{8,9},{9,8},{10,11... | collective-permute-start | bytes 3145736 | tf_op jit(solution)/shard_map/ppermute | solution.py:355
Sparse Core Ops, SparseCore 0:
  9.9 58.4 all-gather.1

commit v3 on v2

--- a/solution.py
+++ b/solution.py
@@ -24,6 +24,8 @@
 PAIR = 2 * BLK
 MEM = ("z", "x")
 MIB = 1024 * 1024
+PICK_PARTS = 4
+Z_ORDER = (0, 4, 1, 5, 2, 6, 7, 3)
 HALF = (XN - 1) * ZN // 2
 NEG_FILL = -1e30
 SCALE = 1.0 / math.sqrt(HD)
@@ -34,22 +36,38 @@
     return lax.dot_general(a, b, (dims, ((), ())), preferred_element_type=jnp.float32)
 
 
-def pick_kernel(asked_ref, block_ref, out_ref):
-    out_ref[...] = block_ref[...]
+def pick_kernel(asked_ref, memory_ref, out_ref, held, in_sems, out_sems):
+    count = MB_DEV // PICK_PARTS
+    loads = [
+        pltpu.make_async_copy(
+            memory_ref.at[pl.ds(i * count, count)], held.at[pl.ds(i * count, count)], in_sems.at[i]
+        )
+        for i in range(PICK_PARTS)
+    ]
+    stores = [
+        pltpu.make_async_copy(held.at[asked_ref[i]], out_ref.at[i], out_sems.at[i])
+        for i in range(OWNERS)
+    ]
+    for copies in (loads, stores):
+        for copy in copies:
+            copy.start()
+        for copy in copies:
+            copy.wait()
 
 
 def pick_blocks(asked, memory_kv):
-    block = (1, 2, BLK, WIDTH)
+    anywhere = pl.BlockSpec(memory_space=pl.ANY)
     return pl.pallas_call(
         pick_kernel,
-        grid_spec=pltpu.PrefetchScalarGridSpec(
-            num_scalar_prefetch=1,
-            grid=(OWNERS,),
-            in_specs=[pl.BlockSpec(block, lambda i, asked_ref: (asked_ref[i], 0, 0, 0))],
-            out_specs=pl.BlockSpec(block, lambda i, asked_ref: (i, 0, 0, 0)),
-        ),
+        in_specs=[pl.BlockSpec(memory_space=pltpu.SMEM), anywhere],
+        out_specs=anywhere,
         out_shape=jax.ShapeDtypeStruct((OWNERS, 2, BLK, WIDTH), jnp.bfloat16),
-        compiler_params=pltpu.CompilerParams(vmem_limit_bytes=4 * MIB),
+        scratch_shapes=[
+            pltpu.VMEM((MB_DEV, 2, BLK, WIDTH), jnp.bfloat16),
+            pltpu.SemaphoreType.DMA((PICK_PARTS,)),
+            pltpu.SemaphoreType.DMA((OWNERS,)),
+        ],
+        compiler_params=pltpu.CompilerParams(vmem_limit_bytes=58 * MIB),
         cost_estimate=pl.CostEstimate(
             flops=0, bytes_accessed=2 * OWNERS * 2 * BLK * WIDTH * 2, transcendentals=0
         ),
@@ -69,7 +87,7 @@
     for x_shift in range(XN):
         x_index = lax.rem(pos_ref[1] + XN - x_shift, XN)
         rows = jnp.concatenate(
-            [x_ref[:, pl.ds(column_of(pos_ref[0], x_index, shift), BLK)] for shift in range(ZN)],
+            [x_ref[:, pl.ds(column_of(pos_ref[0], x_index, shift), BLK)] for shift in Z_ORDER],
             axis=1,
         )
         total += dot(rows, pieces[x_shift].reshape(ZN * BLK, WIDTH), ((1,), (0,)))
@@ -181,21 +199,22 @@
         for part in range(parts)
         for slot in range(TOPK)
     ]
-    for i in range(count):
-        for copy in copies[i * parts * TOPK : (i + 1) * parts * TOPK]:
-            copy.start()
-        for copy in row_copies[i * 6 : i * 6 + 6]:
-            copy.start()
+    grouped = [
+        copies[i * parts * TOPK : (i + 1) * parts * TOPK] + row_copies[i * 6 : i * 6 + 6]
+        for i in range(count)
+    ]
+    for copy in grouped[0]:
+        copy.start()
     if shifts == (0,):
         *done_refs, whole_ref = other_refs
         for shift, done_ref in zip(FAR, done_refs):
             group = lax.rem(pos_ref[2] + shift, YN)
             whole_ref[pl.ds(pl.multiple_of(group * PAIR, PAIR), PAIR), :] = done_ref[...]
     for i, group in enumerate(groups):
-        for copy in copies[i * parts * TOPK : (i + 1) * parts * TOPK]:
+        for copy in grouped[i]:
             copy.wait()
-        for copy in row_copies[i * 6 : i * 6 + 6]:
-            copy.wait()
+        for copy in grouped[i + 1] if i + 1 < count else []:
+            copy.start()
         units = [(part, head) for part in range(parts) for head in range(HEADS)]
         every = range(len(units))
         rows = [slice(part * BLK, (part + 1) * BLK) for part, head in units]
@@ -299,16 +318,18 @@
         pltpu.make_async_copy(piece, held.at[shift, pl.ds(first, count)], sems.at[i])
         for i, (piece, (shift, first, count)) in enumerate(zip(piece_refs, PLACES))
     ]
-    for copy in copies:
+    stages = [copies[:YN], copies[YN::2], copies[YN + 1 :: 2]]
+    for copy in stages[0] + stages[1]:
         copy.start()
     core = pos_ref[3]
     own_rows = pl.ds(pl.multiple_of(core * BLK, BLK), BLK)
     send_rows = pl.ds(pl.multiple_of((1 - core) * BLK, BLK), BLK)
     for x_shift in range(XN):
         x_index = lax.rem(pos_ref[1] + XN - x_shift, XN)
-        if x_shift < 2:
-            for copy in copies[YN:] if x_shift else copies[:YN]:
-                copy.wait()
+        for copy in stages[x_shift] if x_shift < len(stages) else []:
+            copy.wait()
+        for copy in stages[2] if x_shift == 0 else []:
+            copy.start()
         blocks = slice(x_shift * ZN, (x_shift + 1) * ZN)
         total = jnp.zeros((PAIR, ZN * BLK), jnp.float32)
         for shift in range(YN):
@@ -316,9 +337,9 @@
             total += dot(grad_refs[shift][...], weight, ((1,), (1,)))
         total_scr[...] = total
         for out_ref, rows in ((send_ref, send_rows), (own_ref, own_rows)):
-            for shift in range(ZN):
+            for i, shift in enumerate(Z_ORDER):
                 columns = pl.ds(column_of(pos_ref[0], x_index, shift), BLK)
-                part = total_scr[rows, shift * BLK : (shift + 1) * BLK]
+                part = total_scr[rows, i * BLK : (i + 1) * BLK]
                 out_ref[:, columns] = part.astype(out_ref.dtype)
 
 
@@ -364,11 +385,12 @@
         jnp.where(owner_of[:, :, None] == owners, (memory_ids % MB_DEV)[:, :, None], 0),
         axis=(0, 1),
     )
-    weights = [move(w_query, "z", ZN, shift) for shift in range(ZN)]
+    pair = jnp.stack([w_query, move(w_query, "z", ZN, 4)])
+    weights = [pair, *[move(pair, "z", ZN, shift) for shift in (1, 2, -1)]]
     asked = lax.all_to_all(wanted.reshape(OWNERS, 1), MEM, 0, 0, tiled=True)
     asked, weights = lax.optimization_barrier((asked, weights))
     received = lax.all_to_all(pick_blocks(asked[:, 0], memory_kv), MEM, 0, 0, tiled=True)
-    own = jnp.stack(weights)
+    own = jnp.concatenate(weights)
     rows = lax.all_gather(layer_input, ("y", "c"), axis=0, tiled=True)
     others = [move(own, "x", XN, shift) for shift in range(1, XN)]
     first = jnp.concatenate([others[0], others[1][: ZN // 2]])

time: 186 us -> 186 us (level); the launches traced: 183 us -> 185 us
  waiting for transfers between devices: 53.2 us -> 64.3 us
  starting transfers between devices: 55.5 us -> 46.2 us
  local copies, waits for them, and re-layouts: 13.9 us -> 10.3 us
  Pallas kernels: 30.6 us -> 33.1 us
    ppermute x23 -> x20, waiting for transfers between devices: 46.7 us -> 61.2 us  [move(): lax.ppermute(array, axis, [(i, (i + shift) % count) for i in range(count)])]
    ppermute x23 -> x20, starting transfers between devices: 45.8 us -> 36.6 us  [move(): lax.ppermute(array, axis, [(i, (i + shift) % count) for i in range(count)])]
    unnamed x47 -> x37, local copies, waits for them, and re-layouts: 13.5 us -> 9.93 us
    all_to_all x1, waiting for transfers between devices: 5.8 us -> 2.42 us  [local(): lax.all_to_all(pick_blocks(asked[:, 0], memory_kv), MEM, 0, 0, tiled=True)]
    pallas_call x1, Pallas kernels: 1.27 us -> 4.48 us  [pick_blocks(): pl.pallas_call(pick_kernel, in_specs=[pl.BlockSpec(memory_space=pltpu.SME...]
  transfers between devices with their start and end apart: 25 -> 22, of which waited for: 5 -> 7; matrix products, arithmetic and copies ran while one was open for 1% -> 2% of each run, Pallas kernels for 14% -> 15%
where the time goes in v3:
time: 186 us; the launch traced here: 185 us
  waiting for transfers between devices  64.3 us (35%)
  starting transfers between devices  46.2 us (25%)
  Pallas kernels  33.1 us (18%)
  between operations  14.3 us (8%)
  blocking collectives  12.9 us (7%)
  local copies, waits for them, and re-layouts  10.3 us (6%)
  other arithmetic  4.13 us (2%)
    ppermute x20, waiting for transfers between devices, move(): lax.ppermute(array, axis, [(i, (i + shift) % count) for i in range(count)])  61.2 us
    ppermute x20, starting transfers between devices, move(): lax.ppermute(array, axis, [(i, (i + shift) % count) for i in range(count)])  36.6 us
    pallas_call x2, Pallas kernels, attend_memory(): pl.pallas_call(functools.partial(attend_memory_kernel, shifts), in_specs=...  15.2 us
    all_to_all x1, blocking collectives, local(): asked = lax.all_to_all(wanted.reshape(OWNERS, 1), MEM, 0, 0, tiled=True)  12.9 us
    unnamed x37, local copies, waits for them, and re-layouts  9.93 us
    all_to_all x1, starting transfers between devices, local(): lax.all_to_all(pick_blocks(asked[:, 0], memory_kv), MEM, 0, 0, tiled=True)  9.53 us
    pallas_call x1, Pallas kernels, attend_local(): pl.pallas_call(attend_local_kernel, in_specs=[in_vmem] * 3, out_specs=[in...  4.99 us
    pallas_call x1, Pallas kernels, back_project(): pl.pallas_call(back_kernel, in_specs=[pl.BlockSpec(memory_space=pltpu.SME...  4.65 us
  transfers between devices with their start and end apart: 22, of which 7 were waited for; matrix products, arithmetic and copies ran while one was open for 2% of the time, Pallas kernels for 15%

profile of v3, /device:TPU:129, one launch (start us, length us, event | category | flops | bytes accessed | tf_op | source)
XLA Modules:
  0.0 185.3 jit_solution(2943225262852795632)
XLA Ops:
  7.2 0.0 all-gather.2.cloned.1.call-start
  7.2 0.7 all-gather.2.cloned.1.call-update
  7.9 0.1 collective-permute-start
  8.0 8.3 %collective-permute-done = bf16[128,256]{1,0:T(8,128)(2,1)S(1)} collective-permute-done((bf16[128,256]{1,0:T(8,128)(2,1)}, bf16[128,256]{1,0:T(8,128)(2,1)S(1)}, u32[]{:S(2)}, u32[]{:S(2)}) %collective-permute-start) | collective-permute-done | bytes 65568 | tf_op jit(solution)/shard_map/ppermute | solution.py:376
  16.3 0.9 pad_maximum_fusion.2
  17.1 0.1 collective-permute-start.1
  17.2 1.3 collective-permute-start.2
  18.6 1.5 collective-permute-start.3
  20.0 0.7 add_select_fusion
  20.7 0.1 select_reduce_fusion
  20.8 0.1 copy.23
  20.9 12.9 %all_to_all.17 = s32[32,1,1]{2,1,0:T(1,128)S(1)} all-to-all(s32[32,1,1]{2,1,0:T(1,128)S(1)} %copy.23), channel_id=1, replica_groups=mesh['z'=8,'x'=4,'y'=4,'c'=2] {'z','x'}, dimensions={0} | all-to-all | bytes 256 | tf_op jit(solution)/shard_map/all_to_all | solution.py:390
  33.8 1.2 reduce
  35.0 0.0 collective-permute-done.1
  35.0 0.0 collective-permute-done.2
  35.0 0.0 collective-permute-done.3
  35.0 4.5 %pick_blocks.1 = bf16[32,2,128,256]{3,2,1,0:T(8,128)(2,1)} custom-call(s32[32]{0:T(128)} %reduce, bf16[16,2,128,256]{3,2,1,0:T(8,128)(2,1)} %memory_ref.1), custom_call_target="tpu_custom_call" | custom-call | bytes 8388608 | tf_op jit(solution)/shard_map/pick_blocks/pallas_call | solution.py:60
  39.5 9.5 %all-to-all-start.1 = ((bf16[32,2,128,256]{3,2,1,0:T(8,128)(2,1)}), bf16[32,2,128,256]{3,2,1,0:T(8,128)(2,1)}, u32[]{:S(2)}, u32[]{:S(2)}) async-start(bf16[32,2,128,256]{3,2,1,0:T(8,128)(2,1)} %pick_blocks.1), calls=%async_computation.1 | async-start | bytes 8388608 | tf_op jit(solution)/shard_map/all_to_all | solution.py:392
  49.1 2.8 %collective-permute-start.5 = (bf16[8,128,256]{2,1,0:T(8,128)(2,1)S(1)}, bf16[8,128,256]{2,1,0:T(8,128)(2,1)S(1)}, u32[]{:S(2)}, u32[]{:S(2)}) collective-permute-start(bf16[8,128,256]{2,1,0:T(8,128)(2,1)S(1)} %constant_dynamic-update-slice_fusion.refs_0_.refs_4_), channel_id=1, source_target_pairs={{0,16},{8,24},{16,0},{24,8},{1,17},{9,25},{17,1},{25,9},{2,18},{10... | collective-permute-start | bytes 1572872 | tf_op jit(solution)/shard_map/ppermute | solution.py:376
  51.9 0.9 collective-permute-start.6
  52.8 0.6 collective-permute-start.4
  53.4 1.3 collective-permute-start.7
  54.6 2.7 %collective-permute-start.8 = (bf16[8,128,256]{2,1,0:T(8,128)(2,1)S(1)}, bf16[8,128,256]{2,1,0:T(8,128)(2,1)S(1)}, u32[]{:S(2)}, u32[]{:S(2)}) collective-permute-start(bf16[8,128,256]{2,1,0:T(8,128)(2,1)S(1)} %constant_dynamic-update-slice_fusion.refs_0_.refs_4_), channel_id=1, source_target_pairs={{0,4},{2,6},{4,0},{6,2},{1,5},{3,7},{5,1},{7,3},{8,12},{10,14},{12... | collective-permute-start | bytes 1572872 | tf_op jit(solution)/shard_map/ppermute | solution.py:376
  57.3 27.1 %collective-permute-done.5 = bf16[8,128,256]{2,1,0:T(8,128)(2,1)S(1)} collective-permute-done((bf16[8,128,256]{2,1,0:T(8,128)(2,1)S(1)}, bf16[8,128,256]{2,1,0:T(8,128)(2,1)S(1)}, u32[]{:S(2)}, u32[]{:S(2)}) %collective-permute-start.5) | collective-permute-done | bytes 524320 | tf_op jit(solution)/shard_map/ppermute | solution.py:376
  84.4 2.7 %collective-permute-start.9 = (bf16[8,128,256]{2,1,0:T(8,128)(2,1)S(1)}, bf16[8,128,256]{2,1,0:T(8,128)(2,1)S(1)}, u32[]{:S(2)}, u32[]{:S(2)}) collective-permute-start(bf16[8,128,256]{2,1,0:T(8,128)(2,1)S(1)} %constant_dynamic-update-slice_fusion.refs_0_.refs_4_), channel_id=1, source_target_pairs={{0,6},{2,0},{4,2},{6,4},{1,7},{3,1},{5,3},{7,5},{8,14},{10,8},{12,... | collective-permute-start | bytes 1572872 | tf_op jit(solution)/shard_map/ppermute | solution.py:376
  87.2 17.9 %collective-permute-done.6 = bf16[8,128,256]{2,1,0:T(8,128)(2,1)S(1)} collective-permute-done((bf16[8,128,256]{2,1,0:T(8,128)(2,1)S(1)}, bf16[8,128,256]{2,1,0:T(8,128)(2,1)S(1)}, u32[]{:S(2)}, u32[]{:S(2)}) %collective-permute-start.6) | collective-permute-done | bytes 524320 | tf_op jit(solution)/shard_map/ppermute | solution.py:376
  105.1 0.1 pad_maximum_fusion.1.refs_2_.refs_9_
  105.2 0.1 pad_maximum_fusion.refs_1_.refs_8_
  105.3 0.0 collective-permute-done.7.refs_5_
  105.3 0.8 copy-done.7
  106.1 0.0 collective-permute-done.8.refs_6_
  106.1 0.8 copy-done.9
  106.9 0.0 collective-permute-done.9.refs_7_
  106.9 0.8 copy-done.11
  107.7 0.8 collective-permute-start.10
  108.5 1.9 %collective-permute-start.11 = (bf16[12,128,256]{2,1,0:T(8,128)(2,1)S(1)}, bf16[12,128,256]{2,1,0:T(8,128)(2,1)}, u32[]{:S(2)}, u32[]{:S(2)}) collective-permute-start(bf16[12,128,256]{2,1,0:T(8,128)(2,1)S(1)} %pad_maximum_fusion.1.refs_2_.refs_9_), channel_id=1, source_target_pairs={{0,6},{2,0},{4,2},{6,4},{1,7},{3,1},{5,3},{7,5},{8,14},{10,8},{12,... | collective-permute-start | bytes 2359304 | tf_op jit(solution)/shard_map/ppermute | solution.py:376
  110.4 0.1 copy.22
  110.5 0.1 reshape.13
  110.5 0.1 concatenate.12.pos_ref
  110.6 0.0 collective-permute-start.15
  110.7 2.7 %collective-permute-start.18 = (bf16[12,128,256]{2,1,0:T(8,128)(2,1)S(1)}, bf16[12,128,256]{2,1,0:T(8,128)(2,1)}, u32[]{:S(2)}, u32[]{:S(2)}) collective-permute-start(bf16[12,128,256]{2,1,0:T(8,128)(2,1)S(1)} %pad_maximum_fusion.refs_1_.refs_8_), channel_id=1, source_target_pairs={{0,6},{2,0},{4,2},{6,4},{1,7},{3,1},{5,3},{7,5},{8,14},{10,8},{12,... | collective-permute-start | bytes 2359304 | tf_op jit(solution)/shard_map/ppermute | solution.py:376
  113.3 3.4 %copy-done = bf16[1024,4096]{1,0:T(8,128)(2,1)S(1)} copy-done((bf16[1024,4096]{1,0:T(8,128)(2,1)S(1)}, bf16[1024,4096]{1,0:T(8,128)(2,1)}, u32[]{:S(2)}) %copy-start) | copy-done | bytes 8388632
  116.7 3.8 %project.1.query_ref.refs_0_ = bf16[1024,256]{1,0:T(8,128)(2,1)S(1)} custom-call(s32[36]{0:T(128)S(1)} %concatenate.12.pos_ref, bf16[1024,4096]{1,0:T(8,128)(2,1)S(1)} %copy-done, bf16[8,128,256]{2,1,0:T(8,128)(2,1)S(1)} %constant_dynamic-update-slice_fusion.refs_0_.refs_4_, bf16[12,128,256]{2,1,0:T(8,128)(2,1)S(1)} %pad_maximum_fusion.refs_1_.refs_8_, ...), custom_call_target="tpu_custom_call" | custom-call | flops 2147483648 | bytes 11010048 | tf_op jit(solution)/shard_map/project/pallas_call | solution.py:101
  120.5 0.0 copy-start.1
  120.5 5.0 %attend_local.1 = (bf16[1024,256]{1,0:T(8,128)(2,1)S(1)}, bf16[1024,256]{1,0:T(8,128)(2,1)S(1)}, bf16[1024,256]{1,0:T(8,128)(2,1)S(1)}, f32[1024,128]{1,0:T(8,128)S(1)}) custom-call(bf16[1024,256]{1,0:T(8,128)(2,1)S(1)} %project.1.query_ref.refs_0_, bf16[2,1024,256]{2,1,0:T(8,128)(2,1)S(1)} %copy-done.16, bf16[1024,256]{1,0:T(8,128)(2,1)S(1)} %copy-done.2), custom_call_target="tpu_custom_call" | custom-call | flops 1509949440 | bytes 6291456 | tf_op jit(solution)/shard_map/attend_local/pallas_call | solution.py:162
  125.5 0.8 copy-done.3
  126.4 0.8 copy-done.4
  127.2 0.8 copy-done.5
  128.0 0.8 copy-done.6
  128.8 0.0 collective-permute-start.16
  128.8 2.7 %collective-permute-start.17 = (bf16[12,128,256]{2,1,0:T(8,128)(2,1)}, bf16[12,128,256]{2,1,0:T(8,128)(2,1)}, u32[]{:S(2)}, u32[]{:S(2)}) collective-permute-start(bf16[12,128,256]{2,1,0:T(8,128)(2,1)} %collective-permute-done.11.refs_15_), channel_id=1, source_target_pairs={{0,6},{2,0},{4,2},{6,4},{1,7},{3,1},{5,3},{7,5},{8,14},{10,8},{12,... | collective-permute-start | bytes 2359304 | tf_op jit(solution)/shard_map/ppermute | solution.py:376
  131.4 2.4 %all-to-all-done.1.refs_6_ = bf16[32,2,128,256]{3,2,1,0:T(8,128)(2,1)} async-done(((bf16[32,2,128,256]{3,2,1,0:T(8,128)(2,1)}), bf16[32,2,128,256]{3,2,1,0:T(8,128)(2,1)}, u32[]{:S(2)}, u32[]{:S(2)}) %all-to-all-start.1) | async-done | bytes 4194336 | tf_op jit(solution)/shard_map/all_to_all | solution.py:392
  133.9 9.5 %attend_memory.2 = (bf16[256,256]{1,0:T(8,128)(2,1)}, bf16[256,256]{1,0:T(8,128)(2,1)}, bf16[256,256]{1,0:T(8,128)(2,1)}, bf16[256,256]{1,0:T(8,128)(2,1)}, bf16...) custom-call(s32[36]{0:T(128)} %copy-done.14, bf16[1024,256]{1,0:T(8,128)(2,1)} %copy-done.1, bf16[1024,256]{1,0:T(8,128)(2,1)} %refs_1_.3, ...), custom_call_target="tpu_custom_call" | custom-call | flops 805306368 | bytes 6291456 | tf_op jit(solution)/shard_map/attend_memory/pallas_call | solution.py:280
  143.3 1.2 collective-permute-start.12
  144.6 2.8 %collective-permute-start.13 = (bf16[256,256]{1,0:T(8,128)(2,1)}, bf16[256,256]{1,0:T(8,128)(2,1)S(1)}, u32[]{:S(2)}, u32[]{:S(2)}) collective-permute-start(bf16[256,256]{1,0:T(8,128)(2,1)} %get-tuple-element.48), channel_id=1, source_target_pairs={{0,4},{2,6},{4,0},{6,2},{1,5},{3,7},{5,1},{7,3},{8,12},{10,14},{12... | collective-permute-start | bytes 393224 | tf_op jit(solution)/shard_map/ppermute | solution.py:376
  147.3 1.0 collective-permute-start.14
  148.4 5.7 %attend_memory.3 = (bf16[1024,256]{1,0:T(8,128)(2,1)}, bf16[256,256]{1,0:T(8,128)(2,1)}) custom-call(s32[36]{0:T(128)} %copy-done.14, bf16[1024,256]{1,0:T(8,128)(2,1)} %copy-done.1, bf16[1024,256]{1,0:T(8,128)(2,1)} %refs_1_.3, bf16[1024,256]{1,0:T(8,128)(2,1)} %copy-done.3, bf16[1024,256]{1,0:T(8,128)(2,1)} %copy-done.4, bf16[1024,256]{1,0:T(8,128)(2,1)} %copy-done.5, ...), custom_call_target="tpu_custom_call" | custom-call | flops 268435456 | bytes 6291456 | tf_op jit(solution)/shard_map/attend_memory/pallas_call | solution.py:280
  154.1 2.1 %collective-permute-done.12.refs_1_ = bf16[256,256]{1,0:T(8,128)(2,1)S(1)} collective-permute-done((bf16[256,256]{1,0:T(8,128)(2,1)}, bf16[256,256]{1,0:T(8,128)(2,1)S(1)}, u32[]{:S(2)}, u32[]{:S(2)}) %collective-permute-start.12) | collective-permute-done | bytes 131104 | tf_op jit(solution)/shard_map/ppermute | solution.py:376
  156.3 3.4 %collective-permute-done.13.refs_2_ = bf16[256,256]{1,0:T(8,128)(2,1)S(1)} collective-permute-done((bf16[256,256]{1,0:T(8,128)(2,1)}, bf16[256,256]{1,0:T(8,128)(2,1)S(1)}, u32[]{:S(2)}, u32[]{:S(2)}) %collective-permute-start.13) | collective-permute-done | bytes 131104 | tf_op jit(solution)/shard_map/ppermute | solution.py:376
  159.8 0.9 copy-done.13
  160.7 4.6 %back_project.1 = (f32[128,4096]{1,0:T(8,128)S(1)}, bf16[128,4096]{1,0:T(8,128)(2,1)S(1)}) custom-call(s32[36]{0:T(128)S(1)} %copy-done.15, bf16[256,256]{1,0:T(8,128)(2,1)S(1)} %copy-done.13, bf16[256,256]{1,0:T(8,128)(2,1)S(1)} %collective-permute-done.12.refs_1_, bf16[256,256]{1,0:T(8,128)(2,1)S(1)} %collective-permute-done.13.refs_2_, ...), custom_call_target="tpu_custom_call" | custom-call | flops 2147483648 | bytes 12582912 | tf_op jit(solution)/shard_map/back_project/pallas_call | solution.py:348
  165.3 9.7 %collective-permute-start.19 = (bf16[128,4096]{1,0:T(8,128)(2,1)S(1)}, bf16[128,4096]{1,0:T(8,128)(2,1)S(1)}, u32[]{:S(2)}, u32[]{:S(2)}) collective-permute-start(bf16[128,4096]{1,0:T(8,128)(2,1)S(1)} %get-tuple-element.57), channel_id=1, source_target_pairs={{0,1},{1,0},{2,3},{3,2},{4,5},{5,4},{6,7},{7,6},{8,9},{9,8},{10,11... | collective-permute-start | bytes 3145736 | tf_op jit(solution)/shard_map/ppermute | solution.py:376
  175.0 2.3 %collective-permute-done.19 = bf16[128,4096]{1,0:T(8,128)(2,1)S(1)} collective-permute-done((bf16[128,4096]{1,0:T(8,128)(2,1)S(1)}, bf16[128,4096]{1,0:T(8,128)(2,1)S(1)}, u32[]{:S(2)}, u32[]{:S(2)}) %collective-permute-start.19) | collective-permute-done | bytes 1048608 | tf_op jit(solution)/shard_map/ppermute | solution.py:376
  177.3 1.2 add_convert_fusion
  (38 shorter events, 0.1 us)
Async XLA Ops:
  7.2 106.2 %all-gather.2.cloned.1.call-start = ((), (), s32[]{:S(2)}) async-start(), calls=%async_computation.2 | async-start | bytes 9437184 | tf_op jit(solution)/shard_map/all_gather | solution.py:394
  7.9 8.4 %collective-permute-start = (bf16[128,256]{1,0:T(8,128)(2,1)}, bf16[128,256]{1,0:T(8,128)(2,1)S(1)}, u32[]{:S(2)}, u32[]{:S(2)}) collective-permute-start(bf16[128,256]{1,0:T(8,128)(2,1)} %param.7), channel_id=1, source_target_pairs={{0,128},{32,160},{64,192},{96,224},{128,0},{160,32},{192,64},{224,... | collective-permute-start | bytes 196616 | tf_op jit(solution)/shard_map/ppermute | solution.py:376
  17.1 17.9 %collective-permute-start.1 = (bf16[2,128,256]{2,1,0:T(8,128)(2,1)S(1)}, bf16[2,128,256]{2,1,0:T(8,128)(2,1)S(1)}, u32[]{:S(2)}, u32[]{:S(2)}) collective-permute-start(bf16[2,128,256]{2,1,0:T(8,128)(2,1)S(1)} %pad_maximum_fusion.2), channel_id=1, source_target_pairs={{0,32},{32,64},{64,96},{96,128},{128,160},{160,192},{192,224},{224... | collective-permute-start | bytes 393224 | tf_op jit(solution)/shard_map/ppermute | solution.py:376
  17.2 17.8 %collective-permute-start.2 = (bf16[2,128,256]{2,1,0:T(8,128)(2,1)S(1)}, bf16[2,128,256]{2,1,0:T(8,128)(2,1)S(1)}, u32[]{:S(2)}, u32[]{:S(2)}) collective-permute-start(bf16[2,128,256]{2,1,0:T(8,128)(2,1)S(1)} %pad_maximum_fusion.2), channel_id=1, source_target_pairs={{0,64},{32,96},{64,128},{96,160},{128,192},{160,224},{192,0},{224,... | collective-permute-start | bytes 393224 | tf_op jit(solution)/shard_map/ppermute | solution.py:376
  18.6 16.5 %collective-permute-start.3 = (bf16[2,128,256]{2,1,0:T(8,128)(2,1)S(1)}, bf16[2,128,256]{2,1,0:T(8,128)(2,1)S(1)}, u32[]{:S(2)}, u32[]{:S(2)}) collective-permute-start(bf16[2,128,256]{2,1,0:T(8,128)(2,1)S(1)} %pad_maximum_fusion.2), channel_id=1, source_target_pairs={{0,224},{32,0},{64,32},{96,64},{128,96},{160,128},{192,160},{224,1... | collective-permute-start | bytes 393224 | tf_op jit(solution)/shard_map/ppermute | solution.py:376
  39.5 94.3 %all-to-all-start.1 = ((bf16[32,2,128,256]{3,2,1,0:T(8,128)(2,1)}), bf16[32,2,128,256]{3,2,1,0:T(8,128)(2,1)}, u32[]{:S(2)}, u32[]{:S(2)}) async-start(bf16[32,2,128,256]{3,2,1,0:T(8,128)(2,1)} %pick_blocks.1), calls=%async_computation.1 | async-start | bytes 8388608 | tf_op jit(solution)/shard_map/all_to_all | solution.py:392
  49.1 35.3 %collective-permute-start.5 = (bf16[8,128,256]{2,1,0:T(8,128)(2,1)S(1)}, bf16[8,128,256]{2,1,0:T(8,128)(2,1)S(1)}, u32[]{:S(2)}, u32[]{:S(2)}) collective-permute-start(bf16[8,128,256]{2,1,0:T(8,128)(2,1)S(1)} %constant_dynamic-update-slice_fusion.refs_0_.refs_4_), channel_id=1, source_target_pairs={{0,16},{8,24},{16,0},{24,8},{1,17},{9,25},{17,1},{25,9},{2,18},{10... | collective-permute-start | bytes 1572872 | tf_op jit(solution)/shard_map/ppermute | solution.py:376
  51.9 53.2 %collective-permute-start.6 = (bf16[8,128,256]{2,1,0:T(8,128)(2,1)S(1)}, bf16[8,128,256]{2,1,0:T(8,128)(2,1)S(1)}, u32[]{:S(2)}, u32[]{:S(2)}) collective-permute-start(bf16[8,128,256]{2,1,0:T(8,128)(2,1)S(1)} %constant_dynamic-update-slice_fusion.refs_0_.refs_4_), channel_id=1, source_target_pairs={{0,24},{8,0},{16,8},{24,16},{1,25},{9,1},{17,9},{25,17},{2,26},{10... | collective-permute-start | bytes 1572872 | tf_op jit(solution)/shard_map/ppermute | solution.py:376
  52.8 52.4 %collective-permute-start.4 = (bf16[8,128,256]{2,1,0:T(8,128)(2,1)S(1)}, bf16[8,128,256]{2,1,0:T(8,128)(2,1)S(1)}, u32[]{:S(2)}, u32[]{:S(2)}) collective-permute-start(bf16[8,128,256]{2,1,0:T(8,128)(2,1)S(1)} %constant_dynamic-update-slice_fusion.refs_0_.refs_4_), channel_id=1, source_target_pairs={{0,8},{8,16},{16,24},{24,0},{1,9},{9,17},{17,25},{25,1},{2,10},{10... | collective-permute-start | bytes 1572872 | tf_op jit(solution)/shard_map/ppermute | solution.py:376
  53.4 51.9 %collective-permute-start.7 = (bf16[8,128,256]{2,1,0:T(8,128)(2,1)S(1)}, bf16[8,128,256]{2,1,0:T(8,128)(2,1)S(1)}, u32[]{:S(2)}, u32[]{:S(2)}) collective-permute-start(bf16[8,128,256]{2,1,0:T(8,128)(2,1)S(1)} %constant_dynamic-update-slice_fusion.refs_0_.refs_4_), channel_id=1, source_target_pairs={{0,2},{2,4},{4,6},{6,0},{1,3},{3,5},{5,7},{7,1},{8,10},{10,12},{12... | collective-permute-start | bytes 1572872 | tf_op jit(solution)/shard_map/ppermute | solution.py:376
  54.6 51.4 %collective-permute-start.8 = (bf16[8,128,256]{2,1,0:T(8,128)(2,1)S(1)}, bf16[8,128,256]{2,1,0:T(8,128)(2,1)S(1)}, u32[]{:S(2)}, u32[]{:S(2)}) collective-permute-start(bf16[8,128,256]{2,1,0:T(8,128)(2,1)S(1)} %constant_dynamic-update-slice_fusion.refs_0_.refs_4_), channel_id=1, source_target_pairs={{0,4},{2,6},{4,0},{6,2},{1,5},{3,7},{5,1},{7,3},{8,12},{10,14},{12... | collective-permute-start | bytes 1572872 | tf_op jit(solution)/shard_map/ppermute | solution.py:376
  84.4 22.5 %collective-permute-start.9 = (bf16[8,128,256]{2,1,0:T(8,128)(2,1)S(1)}, bf16[8,128,256]{2,1,0:T(8,128)(2,1)S(1)}, u32[]{:S(2)}, u32[]{:S(2)}) collective-permute-start(bf16[8,128,256]{2,1,0:T(8,128)(2,1)S(1)} %constant_dynamic-update-slice_fusion.refs_0_.refs_4_), channel_id=1, source_target_pairs={{0,6},{2,0},{4,2},{6,4},{1,7},{3,1},{5,3},{7,5},{8,14},{10,8},{12,... | collective-permute-start | bytes 1572872 | tf_op jit(solution)/shard_map/ppermute | solution.py:376
  105.3 0.8 copy-start.7
  106.1 0.8 copy-start.9
  106.9 0.8 copy-start.11
  107.7 21.1 %collective-permute-start.10 = (bf16[12,128,256]{2,1,0:T(8,128)(2,1)S(1)}, bf16[12,128,256]{2,1,0:T(8,128)(2,1)}, u32[]{:S(2)}, u32[]{:S(2)}) collective-permute-start(bf16[12,128,256]{2,1,0:T(8,128)(2,1)S(1)} %pad_maximum_fusion.refs_1_.refs_8_), channel_id=1, source_target_pairs={{0,2},{2,4},{4,6},{6,0},{1,3},{3,5},{5,7},{7,1},{8,10},{10,12},{12... | collective-permute-start | bytes 2359304 | tf_op jit(solution)/shard_map/ppermute | solution.py:376
  108.5 20.2 %collective-permute-start.11 = (bf16[12,128,256]{2,1,0:T(8,128)(2,1)S(1)}, bf16[12,128,256]{2,1,0:T(8,128)(2,1)}, u32[]{:S(2)}, u32[]{:S(2)}) collective-permute-start(bf16[12,128,256]{2,1,0:T(8,128)(2,1)S(1)} %pad_maximum_fusion.1.refs_2_.refs_9_), channel_id=1, source_target_pairs={{0,6},{2,0},{4,2},{6,4},{1,7},{3,1},{5,3},{7,5},{8,14},{10,8},{12,... | collective-permute-start | bytes 2359304 | tf_op jit(solution)/shard_map/ppermute | solution.py:376
  110.6 9.9 %copy-start.14 = (s32[36]{0:T(128)}, s32[36]{0:T(128)S(1)}, u32[]{:S(2)}) copy-start(s32[36]{0:T(128)S(1)} %concatenate.12.pos_ref) | copy-start | bytes 436
  110.6 33.9 %collective-permute-start.15 = (bf16[12,128,256]{2,1,0:T(8,128)(2,1)S(1)}, bf16[12,128,256]{2,1,0:T(8,128)(2,1)}, u32[]{:S(2)}, u32[]{:S(2)}) collective-permute-start(bf16[12,128,256]{2,1,0:T(8,128)(2,1)S(1)} %pad_maximum_fusion.1.refs_2_.refs_9_), channel_id=1, source_target_pairs={{0,2},{2,4},{4,6},{6,0},{1,3},{3,5},{5,7},{7,1},{8,10},{10,12},{12... | collective-permute-start | bytes 2359304 | tf_op jit(solution)/shard_map/ppermute | solution.py:376
  110.7 36.7 %collective-permute-start.18 = (bf16[12,128,256]{2,1,0:T(8,128)(2,1)S(1)}, bf16[12,128,256]{2,1,0:T(8,128)(2,1)}, u32[]{:S(2)}, u32[]{:S(2)}) collective-permute-start(bf16[12,128,256]{2,1,0:T(8,128)(2,1)S(1)} %pad_maximum_fusion.refs_1_.refs_8_), channel_id=1, source_target_pairs={{0,6},{2,0},{4,2},{6,4},{1,7},{3,1},{5,3},{7,5},{8,14},{10,8},{12,... | collective-permute-start | bytes 2359304 | tf_op jit(solution)/shard_map/ppermute | solution.py:376
  113.3 3.4 %copy-start = (bf16[1024,4096]{1,0:T(8,128)(2,1)S(1)}, bf16[1024,4096]{1,0:T(8,128)(2,1)}, u32[]{:S(2)}) copy-start(bf16[1024,4096]{1,0:T(8,128)(2,1)} %all-gather.2.cloned.1.call-done.x_ref) | copy-start | bytes 25165828
  116.7 3.8 %copy-start.2 = (bf16[1024,256]{1,0:T(8,128)(2,1)S(1)}, bf16[1024,256]{1,0:T(8,128)(2,1)}, u32[]{:S(2)}) copy-start(bf16[1024,256]{1,0:T(8,128)(2,1)} %refs_1_.3) | copy-start | bytes 1572868
  116.7 3.8 %copy-start.16 = (bf16[2,1024,256]{2,1,0:T(8,128)(2,1)S(1)}, bf16[2,1024,256]{2,1,0:T(8,128)(2,1)}, u32[]{:S(2)}) copy-start(bf16[2,1024,256]{2,1,0:T(8,128)(2,1)} %local_ref.1) | copy-start | bytes 3145732
  120.5 5.0 %copy-start.1 = (bf16[1024,256]{1,0:T(8,128)(2,1)}, bf16[1024,256]{1,0:T(8,128)(2,1)S(1)}, u32[]{:S(2)}) copy-start(bf16[1024,256]{1,0:T(8,128)(2,1)S(1)} %project.1.query_ref.refs_0_) | copy-start | bytes 1572868
  125.5 0.8 copy-start.3
  126.4 0.8 copy-start.4
  127.1 0.8 copy-start.5
  128.0 0.8 copy-start.6
  128.8 31.0 %collective-permute-start.16 = (bf16[12,128,256]{2,1,0:T(8,128)(2,1)}, bf16[12,128,256]{2,1,0:T(8,128)(2,1)S(1)}, u32[]{:S(2)}, u32[]{:S(2)}) collective-permute-start(bf16[12,128,256]{2,1,0:T(8,128)(2,1)} %collective-permute-done.10.refs_10_), channel_id=1, source_target_pairs={{0,2},{2,4},{4,6},{6,0},{1,3},{3,5},{5,7},{7,1},{8,10},{10,12},{12... | collective-permute-start | bytes 2359304 | tf_op jit(solution)/shard_map/ppermute | solution.py:376
  128.8 31.0 %collective-permute-start.17 = (bf16[12,128,256]{2,1,0:T(8,128)(2,1)}, bf16[12,128,256]{2,1,0:T(8,128)(2,1)}, u32[]{:S(2)}, u32[]{:S(2)}) collective-permute-start(bf16[12,128,256]{2,1,0:T(8,128)(2,1)} %collective-permute-done.11.refs_15_), channel_id=1, source_target_pairs={{0,6},{2,0},{4,2},{6,4},{1,7},{3,1},{5,3},{7,5},{8,14},{10,8},{12,... | collective-permute-start | bytes 2359304 | tf_op jit(solution)/shard_map/ppermute | solution.py:376
  143.3 12.9 %collective-permute-start.12 = (bf16[256,256]{1,0:T(8,128)(2,1)}, bf16[256,256]{1,0:T(8,128)(2,1)S(1)}, u32[]{:S(2)}, u32[]{:S(2)}) collective-permute-start(bf16[256,256]{1,0:T(8,128)(2,1)} %get-tuple-element.47), channel_id=1, source_target_pairs={{0,2},{2,4},{4,6},{6,0},{1,3},{3,5},{5,7},{7,1},{8,10},{10,12},{12... | collective-permute-start | bytes 393224 | tf_op jit(solution)/shard_map/ppermute | solution.py:376
  144.6 15.2 %collective-permute-start.13 = (bf16[256,256]{1,0:T(8,128)(2,1)}, bf16[256,256]{1,0:T(8,128)(2,1)S(1)}, u32[]{:S(2)}, u32[]{:S(2)}) collective-permute-start(bf16[256,256]{1,0:T(8,128)(2,1)} %get-tuple-element.48), channel_id=1, source_target_pairs={{0,4},{2,6},{4,0},{6,2},{1,5},{3,7},{5,1},{7,3},{8,12},{10,14},{12... | collective-permute-start | bytes 393224 | tf_op jit(solution)/shard_map/ppermute | solution.py:376
  147.3 12.4 %collective-permute-start.14 = (bf16[256,256]{1,0:T(8,128)(2,1)}, bf16[256,256]{1,0:T(8,128)(2,1)S(1)}, u32[]{:S(2)}, u32[]{:S(2)}) collective-permute-start(bf16[256,256]{1,0:T(8,128)(2,1)} %get-tuple-element.49), channel_id=1, source_target_pairs={{0,6},{2,0},{4,2},{6,4},{1,7},{3,1},{5,3},{7,5},{8,14},{10,8},{12,... | collective-permute-start | bytes 393224 | tf_op jit(solution)/shard_map/ppermute | solution.py:376
  148.4 11.3 %copy-start.8 = (bf16[8,128,256]{2,1,0:T(8,128)(2,1)S(1)}, bf16[8,128,256]{2,1,0:T(8,128)(2,1)}, u32[]{:S(2)}) copy-start(bf16[8,128,256]{2,1,0:T(8,128)(2,1)} %copy-done.7) | copy-start | bytes 1572868
  148.4 11.3 %copy-start.10 = (bf16[8,128,256]{2,1,0:T(8,128)(2,1)S(1)}, bf16[8,128,256]{2,1,0:T(8,128)(2,1)}, u32[]{:S(2)}) copy-start(bf16[8,128,256]{2,1,0:T(8,128)(2,1)} %copy-done.9) | copy-start | bytes 1572868
  148.4 11.4 %copy-start.12 = (bf16[8,128,256]{2,1,0:T(8,128)(2,1)S(1)}, bf16[8,128,256]{2,1,0:T(8,128)(2,1)}, u32[]{:S(2)}) copy-start(bf16[8,128,256]{2,1,0:T(8,128)(2,1)} %copy-done.11) | copy-start | bytes 1572868
  148.4 11.4 %copy-start.15 = (s32[36]{0:T(128)S(1)}, s32[36]{0:T(128)}, u32[]{:S(2)}) copy-start(s32[36]{0:T(128)} %copy-done.14) | copy-start | bytes 436
  159.8 0.9 copy-start.13
  165.3 12.0 %collective-permute-start.19 = (bf16[128,4096]{1,0:T(8,128)(2,1)S(1)}, bf16[128,4096]{1,0:T(8,128)(2,1)S(1)}, u32[]{:S(2)}, u32[]{:S(2)}) collective-permute-start(bf16[128,4096]{1,0:T(8,128)(2,1)S(1)} %get-tuple-element.57), channel_id=1, source_target_pairs={{0,1},{1,0},{2,3},{3,2},{4,5},{5,4},{6,7},{7,6},{8,9},{9,8},{10,11... | collective-permute-start | bytes 3145736 | tf_op jit(solution)/shard_map/ppermute | solution.py:376
Sparse Core Ops, SparseCore 0:
  9.9 57.1 all-gather.1

commit v4 on v3

--- a/solution.py
+++ b/solution.py
@@ -25,7 +25,7 @@
 MEM = ("z", "x")
 MIB = 1024 * 1024
 PICK_PARTS = 4
-Z_ORDER = (0, 4, 1, 5, 2, 6, 7, 3)
+Z_ORDER = tuple(range(ZN))
 HALF = (XN - 1) * ZN // 2
 NEG_FILL = -1e30
 SCALE = 1.0 / math.sqrt(HD)
@@ -385,12 +385,11 @@
         jnp.where(owner_of[:, :, None] == owners, (memory_ids % MB_DEV)[:, :, None], 0),
         axis=(0, 1),
     )
-    pair = jnp.stack([w_query, move(w_query, "z", ZN, 4)])
-    weights = [pair, *[move(pair, "z", ZN, shift) for shift in (1, 2, -1)]]
+    weights = [move(w_query, "z", ZN, shift) for shift in Z_ORDER]
     asked = lax.all_to_all(wanted.reshape(OWNERS, 1), MEM, 0, 0, tiled=True)
     asked, weights = lax.optimization_barrier((asked, weights))
     received = lax.all_to_all(pick_blocks(asked[:, 0], memory_kv), MEM, 0, 0, tiled=True)
-    own = jnp.concatenate(weights)
+    own = jnp.stack(weights)
     rows = lax.all_gather(layer_input, ("y", "c"), axis=0, tiled=True)
     others = [move(own, "x", XN, shift) for shift in range(1, XN)]
     first = jnp.concatenate([others[0], others[1][: ZN // 2]])

time: 186 us -> 185 us (level)
  waiting for transfers between devices: 64.3 us -> 53.9 us
  starting transfers between devices: 46.2 us -> 55 us
    ppermute x20 -> x23, waiting for transfers between devices: 61.2 us -> 47.3 us  [move(): lax.ppermute(array, axis, [(i, (i + shift) % count) for i in range(count)])]
    ppermute x20 -> x23, starting transfers between devices: 36.6 us -> 45.2 us  [move(): lax.ppermute(array, axis, [(i, (i + shift) % count) for i in range(count)])]
    all_to_all x1, waiting for transfers between devices: 2.42 us -> 5.87 us  [local(): lax.all_to_all(pick_blocks(asked[:, 0], memory_kv), MEM, 0, 0, tiled=True)]
    unnamed x37 -> x43, local copies, waits for them, and re-layouts: 9.93 us -> 9.96 us
  transfers between devices with their start and end apart: 22 -> 25, of which waited for: 7 -> 5; matrix products, arithmetic and copies ran while one was open for 2% -> 1% of each run, Pallas kernels for 15% -> 16%
where the time goes in v4:
time: 185 us; the launch traced here: 183 us
  starting transfers between devices  55 us (30%)
  waiting for transfers between devices  53.9 us (29%)
  Pallas kernels  33.2 us (18%)
  between operations  14.4 us (8%)
  blocking collectives  12.9 us (7%)
  local copies, waits for them, and re-layouts  10.3 us (6%)
  other arithmetic  3.28 us (2%)
    ppermute x23, waiting for transfers between devices, move(): lax.ppermute(array, axis, [(i, (i + shift) % count) for i in range(count)])  47.3 us
    ppermute x23, starting transfers between devices, move(): lax.ppermute(array, axis, [(i, (i + shift) % count) for i in range(count)])  45.2 us
    pallas_call x2, Pallas kernels, attend_memory(): pl.pallas_call(functools.partial(attend_memory_kernel, shifts), in_specs=...  15.2 us
    all_to_all x1, blocking collectives, local(): asked = lax.all_to_all(wanted.reshape(OWNERS, 1), MEM, 0, 0, tiled=True)  12.9 us
    unnamed x43, local copies, waits for them, and re-layouts  9.96 us
    all_to_all x1, starting transfers between devices, local(): lax.all_to_all(pick_blocks(asked[:, 0], memory_kv), MEM, 0, 0, tiled=True)  9.72 us
    all_to_all x1, waiting for transfers between devices, local(): lax.all_to_all(pick_blocks(asked[:, 0], memory_kv), MEM, 0, 0, tiled=True)  5.87 us
    pallas_call x1, Pallas kernels, attend_local(): pl.pallas_call(attend_local_kernel, in_specs=[in_vmem] * 3, out_specs=[in...  5 us
  transfers between devices with their start and end apart: 25, of which 5 were waited for; matrix products, arithmetic and copies ran while one was open for 1% of the time, Pallas kernels for 16%

profile of v4, /device:TPU:129, one launch (start us, length us, event | category | flops | bytes accessed | tf_op | source)
XLA Modules:
  0.0 182.9 jit_solution(16946244686875034479)
XLA Ops:
  7.2 0.0 all-gather.2.cloned.1.call-start
  7.2 0.7 all-gather.2.cloned.1.call-update
  7.9 0.8 collective-permute-start
  8.7 1.2 collective-permute-start.1
  9.9 0.0 collective-permute-start.2
  9.9 4.9 %collective-permute-start.3 = (bf16[128,256]{1,0:T(8,128)(2,1)}, bf16[128,256]{1,0:T(8,128)(2,1)S(1)}, u32[]{:S(2)}, u32[]{:S(2)}) collective-permute-start(bf16[128,256]{1,0:T(8,128)(2,1)} %param.7), channel_id=1, source_target_pairs={{0,128},{32,160},{64,192},{96,224},{128,0},{160,32},{192,64},{224,... | collective-permute-start | bytes 196616 | tf_op jit(solution)/shard_map/ppermute | solution.py:376
  14.8 0.7 collective-permute-start.4
  15.5 0.7 add_select_fusion
  16.2 2.2 %collective-permute-start.5 = (bf16[128,256]{1,0:T(8,128)(2,1)}, bf16[128,256]{1,0:T(8,128)(2,1)S(1)}, u32[]{:S(2)}, u32[]{:S(2)}) collective-permute-start(bf16[128,256]{1,0:T(8,128)(2,1)} %param.7), channel_id=1, source_target_pairs={{0,192},{32,224},{64,0},{96,32},{128,64},{160,96},{192,128},{224,1... | collective-permute-start | bytes 196616 | tf_op jit(solution)/shard_map/ppermute | solution.py:376
  18.4 0.0 collective-permute-done.1
  18.5 1.3 collective-permute-start.6
  19.7 0.1 select_reduce_fusion
  19.8 0.1 copy.23
  19.9 12.9 %all_to_all.17 = s32[32,1,1]{2,1,0:T(1,128)S(1)} all-to-all(s32[32,1,1]{2,1,0:T(1,128)S(1)} %copy.23), channel_id=1, replica_groups=mesh['z'=8,'x'=4,'y'=4,'c'=2] {'z','x'}, dimensions={0} | all-to-all | bytes 256 | tf_op jit(solution)/shard_map/all_to_all | solution.py:389
  32.9 1.2 reduce
  34.0 0.0 collective-permute-done.5
  34.1 0.0 collective-permute-done.6
  34.1 4.5 %pick_blocks.1 = bf16[32,2,128,256]{3,2,1,0:T(8,128)(2,1)} custom-call(s32[32]{0:T(128)} %reduce, bf16[16,2,128,256]{3,2,1,0:T(8,128)(2,1)} %memory_ref.1), custom_call_target="tpu_custom_call" | custom-call | bytes 8388608 | tf_op jit(solution)/shard_map/pick_blocks/pallas_call | solution.py:60
  38.6 0.0 copy-start.17
  38.6 9.7 %all-to-all-start.1 = ((bf16[32,2,128,256]{3,2,1,0:T(8,128)(2,1)}), bf16[32,2,128,256]{3,2,1,0:T(8,128)(2,1)}, u32[]{:S(2)}, u32[]{:S(2)}) async-start(bf16[32,2,128,256]{3,2,1,0:T(8,128)(2,1)} %pick_blocks.1), calls=%async_computation.1 | async-start | bytes 8388608 | tf_op jit(solution)/shard_map/all_to_all | solution.py:391
  48.5 2.8 %collective-permute-start.8 = (bf16[8,128,256]{2,1,0:T(8,128)(2,1)S(1)}, bf16[8,128,256]{2,1,0:T(8,128)(2,1)S(1)}, u32[]{:S(2)}, u32[]{:S(2)}) collective-permute-start(bf16[8,128,256]{2,1,0:T(8,128)(2,1)S(1)} %bitcast_dynamic-update-slice_fusion.refs_0_.refs_4_), channel_id=1, source_target_pairs={{0,16},{8,24},{16,0},{24,8},{1,17},{9,25},{17,1},{25,9},{2,18},{10... | collective-permute-start | bytes 1572872 | tf_op jit(solution)/shard_map/ppermute | solution.py:376
  51.3 0.9 collective-permute-start.9
  52.1 0.6 collective-permute-start.7
  52.7 1.2 collective-permute-start.10
  53.9 2.6 %collective-permute-start.11 = (bf16[8,128,256]{2,1,0:T(8,128)(2,1)S(1)}, bf16[8,128,256]{2,1,0:T(8,128)(2,1)S(1)}, u32[]{:S(2)}, u32[]{:S(2)}) collective-permute-start(bf16[8,128,256]{2,1,0:T(8,128)(2,1)S(1)} %bitcast_dynamic-update-slice_fusion.refs_0_.refs_4_), channel_id=1, source_target_pairs={{0,4},{2,6},{4,0},{6,2},{1,5},{3,7},{5,1},{7,3},{8,12},{10,14},{12... | collective-permute-start | bytes 1572872 | tf_op jit(solution)/shard_map/ppermute | solution.py:376
  56.5 29.7 %collective-permute-done.8 = bf16[8,128,256]{2,1,0:T(8,128)(2,1)S(1)} collective-permute-done((bf16[8,128,256]{2,1,0:T(8,128)(2,1)S(1)}, bf16[8,128,256]{2,1,0:T(8,128)(2,1)S(1)}, u32[]{:S(2)}, u32[]{:S(2)}) %collective-permute-start.8) | collective-permute-done | bytes 524320 | tf_op jit(solution)/shard_map/ppermute | solution.py:376
  86.2 2.5 %collective-permute-start.12 = (bf16[8,128,256]{2,1,0:T(8,128)(2,1)S(1)}, bf16[8,128,256]{2,1,0:T(8,128)(2,1)S(1)}, u32[]{:S(2)}, u32[]{:S(2)}) collective-permute-start(bf16[8,128,256]{2,1,0:T(8,128)(2,1)S(1)} %bitcast_dynamic-update-slice_fusion.refs_0_.refs_4_), channel_id=1, source_target_pairs={{0,6},{2,0},{4,2},{6,4},{1,7},{3,1},{5,3},{7,5},{8,14},{10,8},{12,... | collective-permute-start | bytes 1572872 | tf_op jit(solution)/shard_map/ppermute | solution.py:376
  88.7 14.0 %collective-permute-done.9 = bf16[8,128,256]{2,1,0:T(8,128)(2,1)S(1)} collective-permute-done((bf16[8,128,256]{2,1,0:T(8,128)(2,1)S(1)}, bf16[8,128,256]{2,1,0:T(8,128)(2,1)S(1)}, u32[]{:S(2)}, u32[]{:S(2)}) %collective-permute-start.9) | collective-permute-done | bytes 524320 | tf_op jit(solution)/shard_map/ppermute | solution.py:376
  102.7 0.1 pad_maximum_fusion.1.refs_2_.refs_9_
  102.8 0.1 pad_maximum_fusion.refs_1_.refs_8_
  102.8 0.0 collective-permute-done.10.refs_5_
  102.9 0.8 copy-done.7
  103.6 0.0 collective-permute-done.11.refs_6_
  103.7 0.8 copy-done.9
  104.5 0.8 copy-done.11
  105.3 1.2 collective-permute-start.13
  106.5 1.5 collective-permute-start.14
  108.0 0.1 copy.22
  108.0 0.1 reshape.13
  108.1 0.1 concatenate.9.pos_ref
  108.2 0.0 collective-permute-start.18
  108.2 2.7 %collective-permute-start.21 = (bf16[12,128,256]{2,1,0:T(8,128)(2,1)S(1)}, bf16[12,128,256]{2,1,0:T(8,128)(2,1)}, u32[]{:S(2)}, u32[]{:S(2)}) collective-permute-start(bf16[12,128,256]{2,1,0:T(8,128)(2,1)S(1)} %pad_maximum_fusion.refs_1_.refs_8_), channel_id=1, source_target_pairs={{0,6},{2,0},{4,2},{6,4},{1,7},{3,1},{5,3},{7,5},{8,14},{10,8},{12,... | collective-permute-start | bytes 2359304 | tf_op jit(solution)/shard_map/ppermute | solution.py:376
  110.9 3.4 %copy-done = bf16[1024,4096]{1,0:T(8,128)(2,1)S(1)} copy-done((bf16[1024,4096]{1,0:T(8,128)(2,1)S(1)}, bf16[1024,4096]{1,0:T(8,128)(2,1)}, u32[]{:S(2)}) %copy-start) | copy-done | bytes 8388632
  114.3 3.8 %project.1.query_ref.refs_0_ = bf16[1024,256]{1,0:T(8,128)(2,1)S(1)} custom-call(s32[36]{0:T(128)S(1)} %concatenate.9.pos_ref, bf16[1024,4096]{1,0:T(8,128)(2,1)S(1)} %copy-done, bf16[8,128,256]{2,1,0:T(8,128)(2,1)S(1)} %bitcast_dynamic-update-slice_fusion.refs_0_.refs_4_, bf16[12,128,256]{2,1,0:T(8,128)(2,1)S(1)} %pad_maximum_fusion.refs_1_.refs_8_, ...), custom_call_target="tpu_custom_call" | custom-call | flops 2147483648 | bytes 11010048 | tf_op jit(solution)/shard_map/project/pallas_call | solution.py:101
  118.1 0.0 copy-start.1
  118.1 5.0 %attend_local.1 = (bf16[1024,256]{1,0:T(8,128)(2,1)S(1)}, bf16[1024,256]{1,0:T(8,128)(2,1)S(1)}, bf16[1024,256]{1,0:T(8,128)(2,1)S(1)}, f32[1024,128]{1,0:T(8,128)S(1)}) custom-call(bf16[1024,256]{1,0:T(8,128)(2,1)S(1)} %project.1.query_ref.refs_0_, bf16[2,1024,256]{2,1,0:T(8,128)(2,1)S(1)} %copy-done.16, bf16[1024,256]{1,0:T(8,128)(2,1)S(1)} %copy-done.2), custom_call_target="tpu_custom_call" | custom-call | flops 1509949440 | bytes 6291456 | tf_op jit(solution)/shard_map/attend_local/pallas_call | solution.py:162
  123.2 0.8 copy-done.3
  124.0 0.8 copy-done.4
  124.8 0.8 copy-done.5
  125.6 0.8 copy-done.6
  126.4 0.0 collective-permute-start.19
  126.4 2.7 %collective-permute-start.20 = (bf16[12,128,256]{2,1,0:T(8,128)(2,1)}, bf16[12,128,256]{2,1,0:T(8,128)(2,1)}, u32[]{:S(2)}, u32[]{:S(2)}) collective-permute-start(bf16[12,128,256]{2,1,0:T(8,128)(2,1)} %collective-permute-done.14.refs_15_), channel_id=1, source_target_pairs={{0,6},{2,0},{4,2},{6,4},{1,7},{3,1},{5,3},{7,5},{8,14},{10,8},{12,... | collective-permute-start | bytes 2359304 | tf_op jit(solution)/shard_map/ppermute | solution.py:376
  129.1 5.9 %all-to-all-done.1.refs_6_ = bf16[32,2,128,256]{3,2,1,0:T(8,128)(2,1)} async-done(((bf16[32,2,128,256]{3,2,1,0:T(8,128)(2,1)}), bf16[32,2,128,256]{3,2,1,0:T(8,128)(2,1)}, u32[]{:S(2)}, u32[]{:S(2)}) %all-to-all-start.1) | async-done | bytes 4194336 | tf_op jit(solution)/shard_map/all_to_all | solution.py:391
  134.9 9.5 %attend_memory.2 = (bf16[256,256]{1,0:T(8,128)(2,1)}, bf16[256,256]{1,0:T(8,128)(2,1)}, bf16[256,256]{1,0:T(8,128)(2,1)}, bf16[256,256]{1,0:T(8,128)(2,1)}, bf16...) custom-call(s32[36]{0:T(128)} %copy-done.14, bf16[1024,256]{1,0:T(8,128)(2,1)} %copy-done.1, bf16[1024,256]{1,0:T(8,128)(2,1)} %refs_1_.3, ...), custom_call_target="tpu_custom_call" | custom-call | flops 805306368 | bytes 6291456 | tf_op jit(solution)/shard_map/attend_memory/pallas_call | solution.py:280
  144.4 1.3 collective-permute-start.15
  145.7 2.5 %collective-permute-start.16 = (bf16[256,256]{1,0:T(8,128)(2,1)}, bf16[256,256]{1,0:T(8,128)(2,1)S(1)}, u32[]{:S(2)}, u32[]{:S(2)}) collective-permute-start(bf16[256,256]{1,0:T(8,128)(2,1)} %get-tuple-element.56), channel_id=1, source_target_pairs={{0,4},{2,6},{4,0},{6,2},{1,5},{3,7},{5,1},{7,3},{8,12},{10,14},{12... | collective-permute-start | bytes 393224 | tf_op jit(solution)/shard_map/ppermute | solution.py:376
  148.2 1.1 collective-permute-start.17
  149.4 5.7 %attend_memory.3 = (bf16[1024,256]{1,0:T(8,128)(2,1)}, bf16[256,256]{1,0:T(8,128)(2,1)}) custom-call(s32[36]{0:T(128)} %copy-done.14, bf16[1024,256]{1,0:T(8,128)(2,1)} %copy-done.1, bf16[1024,256]{1,0:T(8,128)(2,1)} %refs_1_.3, bf16[1024,256]{1,0:T(8,128)(2,1)} %copy-done.3, bf16[1024,256]{1,0:T(8,128)(2,1)} %copy-done.4, bf16[1024,256]{1,0:T(8,128)(2,1)} %copy-done.5, ...), custom_call_target="tpu_custom_call" | custom-call | flops 268435456 | bytes 6291456 | tf_op jit(solution)/shard_map/attend_memory/pallas_call | solution.py:280
  155.1 1.3 collective-permute-done.16.refs_2_
  156.5 0.9 copy-done.13
  157.4 4.6 %back_project.1 = (f32[128,4096]{1,0:T(8,128)S(1)}, bf16[128,4096]{1,0:T(8,128)(2,1)S(1)}) custom-call(s32[36]{0:T(128)S(1)} %copy-done.15, bf16[256,256]{1,0:T(8,128)(2,1)S(1)} %copy-done.13, bf16[256,256]{1,0:T(8,128)(2,1)S(1)} %collective-permute-done.15.refs_1_, bf16[256,256]{1,0:T(8,128)(2,1)S(1)} %collective-permute-done.16.refs_2_, ...), custom_call_target="tpu_custom_call" | custom-call | flops 2147483648 | bytes 12582912 | tf_op jit(solution)/shard_map/back_project/pallas_call | solution.py:348
  162.0 10.6 %collective-permute-start.22 = (bf16[128,4096]{1,0:T(8,128)(2,1)S(1)}, bf16[128,4096]{1,0:T(8,128)(2,1)S(1)}, u32[]{:S(2)}, u32[]{:S(2)}) collective-permute-start(bf16[128,4096]{1,0:T(8,128)(2,1)S(1)} %get-tuple-element.65), channel_id=1, source_target_pairs={{0,1},{1,0},{2,3},{3,2},{4,5},{5,4},{6,7},{7,6},{8,9},{9,8},{10,11... | collective-permute-start | bytes 3145736 | tf_op jit(solution)/shard_map/ppermute | solution.py:376
  172.6 2.3 %collective-permute-done.22 = bf16[128,4096]{1,0:T(8,128)(2,1)S(1)} collective-permute-done((bf16[128,4096]{1,0:T(8,128)(2,1)S(1)}, bf16[128,4096]{1,0:T(8,128)(2,1)S(1)}, u32[]{:S(2)}, u32[]{:S(2)}) %collective-permute-start.22) | collective-permute-done | bytes 1048608 | tf_op jit(solution)/shard_map/ppermute | solution.py:376
  174.9 1.2 add_convert_fusion
  (49 shorter events, 0.2 us)
Async XLA Ops:
  7.2 103.7 %all-gather.2.cloned.1.call-start = ((), (), s32[]{:S(2)}) async-start(), calls=%async_computation.2 | async-start | bytes 9437184 | tf_op jit(solution)/shard_map/all_gather | solution.py:393
  7.9 8.3 %collective-permute-start = (bf16[128,256]{1,0:T(8,128)(2,1)}, bf16[128,256]{1,0:T(8,128)(2,1)S(1)}, u32[]{:S(2)}, u32[]{:S(2)}) collective-permute-start(bf16[128,256]{1,0:T(8,128)(2,1)} %param.7), channel_id=1, source_target_pairs={{0,32},{32,64},{64,96},{96,128},{128,160},{160,192},{192,224},{224... | collective-permute-start | bytes 196616 | tf_op jit(solution)/shard_map/ppermute | solution.py:376
  8.7 9.7 %collective-permute-start.1 = (bf16[128,256]{1,0:T(8,128)(2,1)}, bf16[128,256]{1,0:T(8,128)(2,1)S(1)}, u32[]{:S(2)}, u32[]{:S(2)}) collective-permute-start(bf16[128,256]{1,0:T(8,128)(2,1)} %param.7), channel_id=1, source_target_pairs={{0,64},{32,96},{64,128},{96,160},{128,192},{160,224},{192,0},{224,... | collective-permute-start | bytes 196616 | tf_op jit(solution)/shard_map/ppermute | solution.py:376
  9.9 24.1 %collective-permute-start.2 = (bf16[128,256]{1,0:T(8,128)(2,1)}, bf16[128,256]{1,0:T(8,128)(2,1)S(1)}, u32[]{:S(2)}, u32[]{:S(2)}) collective-permute-start(bf16[128,256]{1,0:T(8,128)(2,1)} %param.7), channel_id=1, source_target_pairs={{0,96},{32,128},{64,160},{96,192},{128,224},{160,0},{192,32},{224,... | collective-permute-start | bytes 196616 | tf_op jit(solution)/shard_map/ppermute | solution.py:376
  9.9 24.1 %collective-permute-start.3 = (bf16[128,256]{1,0:T(8,128)(2,1)}, bf16[128,256]{1,0:T(8,128)(2,1)S(1)}, u32[]{:S(2)}, u32[]{:S(2)}) collective-permute-start(bf16[128,256]{1,0:T(8,128)(2,1)} %param.7), channel_id=1, source_target_pairs={{0,128},{32,160},{64,192},{96,224},{128,0},{160,32},{192,64},{224,... | collective-permute-start | bytes 196616 | tf_op jit(solution)/shard_map/ppermute | solution.py:376
  14.8 19.2 %collective-permute-start.4 = (bf16[128,256]{1,0:T(8,128)(2,1)}, bf16[128,256]{1,0:T(8,128)(2,1)S(1)}, u32[]{:S(2)}, u32[]{:S(2)}) collective-permute-start(bf16[128,256]{1,0:T(8,128)(2,1)} %param.7), channel_id=1, source_target_pairs={{0,160},{32,192},{64,224},{96,0},{128,32},{160,64},{192,96},{224,1... | collective-permute-start | bytes 196616 | tf_op jit(solution)/shard_map/ppermute | solution.py:376
  16.2 17.8 %collective-permute-start.5 = (bf16[128,256]{1,0:T(8,128)(2,1)}, bf16[128,256]{1,0:T(8,128)(2,1)S(1)}, u32[]{:S(2)}, u32[]{:S(2)}) collective-permute-start(bf16[128,256]{1,0:T(8,128)(2,1)} %param.7), channel_id=1, source_target_pairs={{0,192},{32,224},{64,0},{96,32},{128,64},{160,96},{192,128},{224,1... | collective-permute-start | bytes 196616 | tf_op jit(solution)/shard_map/ppermute | solution.py:376
  18.5 15.6 %collective-permute-start.6 = (bf16[128,256]{1,0:T(8,128)(2,1)}, bf16[128,256]{1,0:T(8,128)(2,1)S(1)}, u32[]{:S(2)}, u32[]{:S(2)}) collective-permute-start(bf16[128,256]{1,0:T(8,128)(2,1)} %param.7), channel_id=1, source_target_pairs={{0,224},{32,0},{64,32},{96,64},{128,96},{160,128},{192,160},{224,1... | collective-permute-start | bytes 196616 | tf_op jit(solution)/shard_map/ppermute | solution.py:376
  38.6 9.7 %copy-start.17 = (bf16[128,256]{1,0:T(8,128)(2,1)S(1)}, bf16[128,256]{1,0:T(8,128)(2,1)}, u32[]{:S(2)}) copy-start(bf16[128,256]{1,0:T(8,128)(2,1)} %param.7) | copy-start | bytes 196612
  38.6 96.3 %all-to-all-start.1 = ((bf16[32,2,128,256]{3,2,1,0:T(8,128)(2,1)}), bf16[32,2,128,256]{3,2,1,0:T(8,128)(2,1)}, u32[]{:S(2)}, u32[]{:S(2)}) async-start(bf16[32,2,128,256]{3,2,1,0:T(8,128)(2,1)} %pick_blocks.1), calls=%async_computation.1 | async-start | bytes 8388608 | tf_op jit(solution)/shard_map/all_to_all | solution.py:391
  48.5 37.7 %collective-permute-start.8 = (bf16[8,128,256]{2,1,0:T(8,128)(2,1)S(1)}, bf16[8,128,256]{2,1,0:T(8,128)(2,1)S(1)}, u32[]{:S(2)}, u32[]{:S(2)}) collective-permute-start(bf16[8,128,256]{2,1,0:T(8,128)(2,1)S(1)} %bitcast_dynamic-update-slice_fusion.refs_0_.refs_4_), channel_id=1, source_target_pairs={{0,16},{8,24},{16,0},{24,8},{1,17},{9,25},{17,1},{25,9},{2,18},{10... | collective-permute-start | bytes 1572872 | tf_op jit(solution)/shard_map/ppermute | solution.py:376
  51.3 51.4 %collective-permute-start.9 = (bf16[8,128,256]{2,1,0:T(8,128)(2,1)S(1)}, bf16[8,128,256]{2,1,0:T(8,128)(2,1)S(1)}, u32[]{:S(2)}, u32[]{:S(2)}) collective-permute-start(bf16[8,128,256]{2,1,0:T(8,128)(2,1)S(1)} %bitcast_dynamic-update-slice_fusion.refs_0_.refs_4_), channel_id=1, source_target_pairs={{0,24},{8,0},{16,8},{24,16},{1,25},{9,1},{17,9},{25,17},{2,26},{10... | collective-permute-start | bytes 1572872 | tf_op jit(solution)/shard_map/ppermute | solution.py:376
  52.1 50.6 %collective-permute-start.7 = (bf16[8,128,256]{2,1,0:T(8,128)(2,1)S(1)}, bf16[8,128,256]{2,1,0:T(8,128)(2,1)S(1)}, u32[]{:S(2)}, u32[]{:S(2)}) collective-permute-start(bf16[8,128,256]{2,1,0:T(8,128)(2,1)S(1)} %bitcast_dynamic-update-slice_fusion.refs_0_.refs_4_), channel_id=1, source_target_pairs={{0,8},{8,16},{16,24},{24,0},{1,9},{9,17},{17,25},{25,1},{2,10},{10... | collective-permute-start | bytes 1572872 | tf_op jit(solution)/shard_map/ppermute | solution.py:376
  52.7 50.1 %collective-permute-start.10 = (bf16[8,128,256]{2,1,0:T(8,128)(2,1)S(1)}, bf16[8,128,256]{2,1,0:T(8,128)(2,1)S(1)}, u32[]{:S(2)}, u32[]{:S(2)}) collective-permute-start(bf16[8,128,256]{2,1,0:T(8,128)(2,1)S(1)} %bitcast_dynamic-update-slice_fusion.refs_0_.refs_4_), channel_id=1, source_target_pairs={{0,2},{2,4},{4,6},{6,0},{1,3},{3,5},{5,7},{7,1},{8,10},{10,12},{12... | collective-permute-start | bytes 1572872 | tf_op jit(solution)/shard_map/ppermute | solution.py:376
  53.9 49.7 %collective-permute-start.11 = (bf16[8,128,256]{2,1,0:T(8,128)(2,1)S(1)}, bf16[8,128,256]{2,1,0:T(8,128)(2,1)S(1)}, u32[]{:S(2)}, u32[]{:S(2)}) collective-permute-start(bf16[8,128,256]{2,1,0:T(8,128)(2,1)S(1)} %bitcast_dynamic-update-slice_fusion.refs_0_.refs_4_), channel_id=1, source_target_pairs={{0,4},{2,6},{4,0},{6,2},{1,5},{3,7},{5,1},{7,3},{8,12},{10,14},{12... | collective-permute-start | bytes 1572872 | tf_op jit(solution)/shard_map/ppermute | solution.py:376
  86.2 18.3 %collective-permute-start.12 = (bf16[8,128,256]{2,1,0:T(8,128)(2,1)S(1)}, bf16[8,128,256]{2,1,0:T(8,128)(2,1)S(1)}, u32[]{:S(2)}, u32[]{:S(2)}) collective-permute-start(bf16[8,128,256]{2,1,0:T(8,128)(2,1)S(1)} %bitcast_dynamic-update-slice_fusion.refs_0_.refs_4_), channel_id=1, source_target_pairs={{0,6},{2,0},{4,2},{6,4},{1,7},{3,1},{5,3},{7,5},{8,14},{10,8},{12,... | collective-permute-start | bytes 1572872 | tf_op jit(solution)/shard_map/ppermute | solution.py:376
  102.9 0.8 copy-start.7
  103.6 0.8 copy-start.9
  104.5 0.8 copy-start.11
  105.3 21.1 %collective-permute-start.13 = (bf16[12,128,256]{2,1,0:T(8,128)(2,1)S(1)}, bf16[12,128,256]{2,1,0:T(8,128)(2,1)}, u32[]{:S(2)}, u32[]{:S(2)}) collective-permute-start(bf16[12,128,256]{2,1,0:T(8,128)(2,1)S(1)} %pad_maximum_fusion.refs_1_.refs_8_), channel_id=1, source_target_pairs={{0,2},{2,4},{4,6},{6,0},{1,3},{3,5},{5,7},{7,1},{8,10},{10,12},{12... | collective-permute-start | bytes 2359304 | tf_op jit(solution)/shard_map/ppermute | solution.py:376
  106.5 19.9 %collective-permute-start.14 = (bf16[12,128,256]{2,1,0:T(8,128)(2,1)S(1)}, bf16[12,128,256]{2,1,0:T(8,128)(2,1)}, u32[]{:S(2)}, u32[]{:S(2)}) collective-permute-start(bf16[12,128,256]{2,1,0:T(8,128)(2,1)S(1)} %pad_maximum_fusion.1.refs_2_.refs_9_), channel_id=1, source_target_pairs={{0,6},{2,0},{4,2},{6,4},{1,7},{3,1},{5,3},{7,5},{8,14},{10,8},{12,... | collective-permute-start | bytes 2359304 | tf_op jit(solution)/shard_map/ppermute | solution.py:376
  108.2 9.9 %copy-start.14 = (s32[36]{0:T(128)}, s32[36]{0:T(128)S(1)}, u32[]{:S(2)}) copy-start(s32[36]{0:T(128)S(1)} %concatenate.9.pos_ref) | copy-start | bytes 436
  108.2 37.5 %collective-permute-start.18 = (bf16[12,128,256]{2,1,0:T(8,128)(2,1)S(1)}, bf16[12,128,256]{2,1,0:T(8,128)(2,1)}, u32[]{:S(2)}, u32[]{:S(2)}) collective-permute-start(bf16[12,128,256]{2,1,0:T(8,128)(2,1)S(1)} %pad_maximum_fusion.1.refs_2_.refs_9_), channel_id=1, source_target_pairs={{0,2},{2,4},{4,6},{6,0},{1,3},{3,5},{5,7},{7,1},{8,10},{10,12},{12... | collective-permute-start | bytes 2359304 | tf_op jit(solution)/shard_map/ppermute | solution.py:376
  108.2 40.0 %collective-permute-start.21 = (bf16[12,128,256]{2,1,0:T(8,128)(2,1)S(1)}, bf16[12,128,256]{2,1,0:T(8,128)(2,1)}, u32[]{:S(2)}, u32[]{:S(2)}) collective-permute-start(bf16[12,128,256]{2,1,0:T(8,128)(2,1)S(1)} %pad_maximum_fusion.refs_1_.refs_8_), channel_id=1, source_target_pairs={{0,6},{2,0},{4,2},{6,4},{1,7},{3,1},{5,3},{7,5},{8,14},{10,8},{12,... | collective-permute-start | bytes 2359304 | tf_op jit(solution)/shard_map/ppermute | solution.py:376
  110.9 3.4 %copy-start = (bf16[1024,4096]{1,0:T(8,128)(2,1)S(1)}, bf16[1024,4096]{1,0:T(8,128)(2,1)}, u32[]{:S(2)}) copy-start(bf16[1024,4096]{1,0:T(8,128)(2,1)} %all-gather.2.cloned.1.call-done.x_ref) | copy-start | bytes 25165828
  114.3 3.8 %copy-start.2 = (bf16[1024,256]{1,0:T(8,128)(2,1)S(1)}, bf16[1024,256]{1,0:T(8,128)(2,1)}, u32[]{:S(2)}) copy-start(bf16[1024,256]{1,0:T(8,128)(2,1)} %refs_1_.3) | copy-start | bytes 1572868
  114.3 3.8 %copy-start.16 = (bf16[2,1024,256]{2,1,0:T(8,128)(2,1)S(1)}, bf16[2,1024,256]{2,1,0:T(8,128)(2,1)}, u32[]{:S(2)}) copy-start(bf16[2,1024,256]{2,1,0:T(8,128)(2,1)} %local_ref.1) | copy-start | bytes 3145732
  118.1 5.0 %copy-start.1 = (bf16[1024,256]{1,0:T(8,128)(2,1)}, bf16[1024,256]{1,0:T(8,128)(2,1)S(1)}, u32[]{:S(2)}) copy-start(bf16[1024,256]{1,0:T(8,128)(2,1)S(1)} %project.1.query_ref.refs_0_) | copy-start | bytes 1572868
  123.1 0.8 copy-start.3
  124.0 0.8 copy-start.4
  124.8 0.8 copy-start.5
  125.6 0.8 copy-start.6
  126.4 30.0 %collective-permute-start.19 = (bf16[12,128,256]{2,1,0:T(8,128)(2,1)}, bf16[12,128,256]{2,1,0:T(8,128)(2,1)S(1)}, u32[]{:S(2)}, u32[]{:S(2)}) collective-permute-start(bf16[12,128,256]{2,1,0:T(8,128)(2,1)} %collective-permute-done.13.refs_10_), channel_id=1, source_target_pairs={{0,2},{2,4},{4,6},{6,0},{1,3},{3,5},{5,7},{7,1},{8,10},{10,12},{12... | collective-permute-start | bytes 2359304 | tf_op jit(solution)/shard_map/ppermute | solution.py:376
  126.4 30.0 %collective-permute-start.20 = (bf16[12,128,256]{2,1,0:T(8,128)(2,1)}, bf16[12,128,256]{2,1,0:T(8,128)(2,1)}, u32[]{:S(2)}, u32[]{:S(2)}) collective-permute-start(bf16[12,128,256]{2,1,0:T(8,128)(2,1)} %collective-permute-done.14.refs_15_), channel_id=1, source_target_pairs={{0,6},{2,0},{4,2},{6,4},{1,7},{3,1},{5,3},{7,5},{8,14},{10,8},{12,... | collective-permute-start | bytes 2359304 | tf_op jit(solution)/shard_map/ppermute | solution.py:376
  144.4 10.7 %collective-permute-start.15 = (bf16[256,256]{1,0:T(8,128)(2,1)}, bf16[256,256]{1,0:T(8,128)(2,1)S(1)}, u32[]{:S(2)}, u32[]{:S(2)}) collective-permute-start(bf16[256,256]{1,0:T(8,128)(2,1)} %get-tuple-element.55), channel_id=1, source_target_pairs={{0,2},{2,4},{4,6},{6,0},{1,3},{3,5},{5,7},{7,1},{8,10},{10,12},{12... | collective-permute-start | bytes 393224 | tf_op jit(solution)/shard_map/ppermute | solution.py:376
  145.7 10.7 %collective-permute-start.16 = (bf16[256,256]{1,0:T(8,128)(2,1)}, bf16[256,256]{1,0:T(8,128)(2,1)S(1)}, u32[]{:S(2)}, u32[]{:S(2)}) collective-permute-start(bf16[256,256]{1,0:T(8,128)(2,1)} %get-tuple-element.56), channel_id=1, source_target_pairs={{0,4},{2,6},{4,0},{6,2},{1,5},{3,7},{5,1},{7,3},{8,12},{10,14},{12... | collective-permute-start | bytes 393224 | tf_op jit(solution)/shard_map/ppermute | solution.py:376
  148.2 8.2 %collective-permute-start.17 = (bf16[256,256]{1,0:T(8,128)(2,1)}, bf16[256,256]{1,0:T(8,128)(2,1)S(1)}, u32[]{:S(2)}, u32[]{:S(2)}) collective-permute-start(bf16[256,256]{1,0:T(8,128)(2,1)} %get-tuple-element.57), channel_id=1, source_target_pairs={{0,6},{2,0},{4,2},{6,4},{1,7},{3,1},{5,3},{7,5},{8,14},{10,8},{12,... | collective-permute-start | bytes 393224 | tf_op jit(solution)/shard_map/ppermute | solution.py:376
  149.4 7.0 %copy-start.8 = (bf16[8,128,256]{2,1,0:T(8,128)(2,1)S(1)}, bf16[8,128,256]{2,1,0:T(8,128)(2,1)}, u32[]{:S(2)}) copy-start(bf16[8,128,256]{2,1,0:T(8,128)(2,1)} %copy-done.7) | copy-start | bytes 1572868
  149.4 7.1 %copy-start.10 = (bf16[8,128,256]{2,1,0:T(8,128)(2,1)S(1)}, bf16[8,128,256]{2,1,0:T(8,128)(2,1)}, u32[]{:S(2)}) copy-start(bf16[8,128,256]{2,1,0:T(8,128)(2,1)} %copy-done.9) | copy-start | bytes 1572868
  149.4 7.1 %copy-start.12 = (bf16[8,128,256]{2,1,0:T(8,128)(2,1)S(1)}, bf16[8,128,256]{2,1,0:T(8,128)(2,1)}, u32[]{:S(2)}) copy-start(bf16[8,128,256]{2,1,0:T(8,128)(2,1)} %copy-done.11) | copy-start | bytes 1572868
  149.4 7.1 %copy-start.15 = (s32[36]{0:T(128)S(1)}, s32[36]{0:T(128)}, u32[]{:S(2)}) copy-start(s32[36]{0:T(128)} %copy-done.14) | copy-start | bytes 436
  156.5 0.9 copy-start.13
  162.0 12.9 %collective-permute-start.22 = (bf16[128,4096]{1,0:T(8,128)(2,1)S(1)}, bf16[128,4096]{1,0:T(8,128)(2,1)S(1)}, u32[]{:S(2)}, u32[]{:S(2)}) collective-permute-start(bf16[128,4096]{1,0:T(8,128)(2,1)S(1)} %get-tuple-element.65), channel_id=1, source_target_pairs={{0,1},{1,0},{2,3},{3,2},{4,5},{5,4},{6,7},{7,6},{8,9},{9,8},{10,11... | collective-permute-start | bytes 3145736 | tf_op jit(solution)/shard_map/ppermute | solution.py:376
Sparse Core Ops, SparseCore 0:
  9.9 58.1 all-gather.1
